TPU v7x, 128 devices: a whole 4x4x4 slice. The times are simulated.
128 devices in a mesh: space: 4 (over y_hi, core), filt: 32 (over y_lo, z, x).
Axes of the slice: x: 4, y: 4 (y_hi: 2, y_lo: 2; y = y_hi * 2 + y_lo), z: 4, core: 2. Of those that a mesh axis runs over, the one named last changes fastest.
Arguments:
- features: bfloat16 [256, 12, 2048], P('filt', 'space'), may hold values from -6 to 6
- weight: bfloat16 [256, 27, 256], P('filt'), may hold values from -0.078125 to 0.078125
- bias_vec: bfloat16 [256], P('filt'), may hold values from -3 to 3
- cotangent: bfloat16 [256, 12, 2048], P('filt', 'space'), may hold values from -6 to 6
Outputs:
- activation: bfloat16 [256, 12, 2048], P('filt', 'space')
- input_grad: bfloat16 [256, 12, 2048], P('filt', 'space')
- weight_grad: float32 [256, 27, 256], P('filt')
All inputs are finite; a program needn't handle non-finite values.
Results may differ from a plain program's by a relative error of at most 0.014.
Values may be sent and summed in bfloat16 or wider, within the bound.
No kernel may reach another device: no remote copies, remote signals or barrier semaphores. Data moves between devices by JAX's collectives and lax.ppermute only.
A program may use at most 192 MiB of HBM per device.

v0:
```python
import math

import jax
import jax.numpy as jnp
from jax import lax
from jax.sharding import PartitionSpec as P

H = 32
W = 64


DIMS = ("NCDHW", "OIDHW", "NCDHW")


def with_halo(x, sides, width):
    for axis, dim in sides:
        size, length = (lax.axis_size(axis), x.shape[dim])
        up = [(i, (i + 1) % size) for i in range(size - 1)]
        down = [(j, i) for i, j in up]
        last = lax.slice_in_dim(x, length - width, length, axis=dim)
        leading = lax.slice_in_dim(x, 0, width, axis=dim)
        before = lax.ppermute(last, axis, up)
        after = lax.ppermute(leading, axis, down)
        x = jnp.concatenate([before, x, after], axis=dim)
    return x


def to_kernel(weight):
    grid = weight.reshape(weight.shape[0], 3, 3, 3, weight.shape[2])
    return jnp.transpose(grid, (0, 4, 1, 2, 3))


def flip_kernel(weight):
    flipped = weight[:, ::-1, :]
    grid = flipped.reshape(weight.shape[0], 3, 3, 3, weight.shape[2])
    return jnp.transpose(grid, (4, 0, 1, 2, 3))


def conv_block(x_pad, kernel):
    return lax.conv_general_dilated(
        x_pad[None],
        kernel,
        (1, 1, 1),
        "VALID",
        dimension_numbers=DIMS,
        preferred_element_type=jnp.float32,
    )[0]


def filter_grad(x_pad, grad_grid):
    outputs, depth_n, rows_n, cols_n = grad_grid.shape
    flat_grad = grad_grid.reshape(outputs, depth_n * rows_n * cols_n)
    inputs = x_pad.shape[0]
    terms = []
    for position in range(27):
        depth_at = position // 9
        row_at = position // 3 % 3
        col_at = position % 3
        window = x_pad[
            :, depth_at : depth_at + depth_n, row_at : row_at + rows_n, col_at : col_at + cols_n
        ]
        window = window.reshape(inputs, depth_n * rows_n * cols_n)
        terms.append(
            lax.dot_general(
                flat_grad, window, (((1,), (1,)), ((), ())), preferred_element_type=jnp.float32
            )
        )
    return jnp.stack(terms, 1)


def pad_rows(flat, local_rows):
    grid = flat.reshape(flat.shape[0], flat.shape[1], local_rows, W)
    return jnp.pad(grid, ((0, 0), (0, 0), (1, 1), (1, 1)))


def halo_planes(flat):
    return with_halo(flat, (("space", 1),), 1)


def activate(pre_act, cotangent):
    sigmoid = jax.nn.sigmoid(pre_act)
    activation = (pre_act * sigmoid).astype(jnp.bfloat16)
    slope = sigmoid * (1.0 + pre_act * (1.0 - sigmoid))
    pre_grad = (cotangent.astype(jnp.float32) * slope).astype(jnp.bfloat16)
    return (activation, pre_grad)


def per_device(features, weight, bias_vec, cotangent):
    block = features.shape[0]
    planes = features.shape[1]
    slabs = lax.axis_size("space")
    x_flat = halo_planes(features)
    kernel = to_kernel(weight)
    start_sum = jnp.zeros((block, planes, H * W), jnp.float32)
    shard_piece = lax.all_gather(x_flat, "filt", axis=0, tiled=True)
    part = kernel
    pre_act = start_sum + conv_block(pad_rows(shard_piece, H), part).reshape(start_sum.shape)
    pre_act = pre_act + bias_vec.astype(jnp.float32)[:, None, None]
    activation, pre_grad = activate(pre_act, cotangent)
    grad_grid = pre_grad.reshape(block, planes, H, W)
    part = filter_grad(pad_rows(lax.all_gather(x_flat, "filt", axis=0, tiled=True), H), grad_grid)
    weight_part = part
    grad_flat = halo_planes(pre_grad)
    swapped = lax.all_to_all(weight, "filt", split_axis=2, concat_axis=0, tiled=True)
    flipped = flip_kernel(swapped)
    shard_piece = lax.all_gather(grad_flat, "filt", axis=0, tiled=True)
    length = shard_piece.shape[0]
    part = lax.slice_in_dim(flipped, 0, length, axis=1)
    input_sum = start_sum + conv_block(pad_rows(shard_piece, H), part).reshape(start_sum.shape)
    input_grad = input_sum.astype(jnp.bfloat16)
    weight_grad = lax.psum(weight_part.astype(jnp.bfloat16), "space").astype(jnp.float32) * (
        1.0 / math.sqrt(planes * slabs * H * W)
    )
    return (activation, input_grad, weight_grad)


def solution(mesh):
    return jax.shard_map(
        per_device,
        mesh=mesh,
        in_specs=(
            P("filt", "space", None),
            P("filt", None, None),
            P("filt"),
            P("filt", "space", None),
        ),
        out_specs=(P("filt", "space", None), P("filt", "space", None), P("filt", None, None)),
        check_vma=False,
    )
```

profile of v0, /device:TPU:0, one launch (start us, length us, event | category | flops | bytes accessed | tf_op | source)
XLA Modules:
  0.0 583.5 jit_solution(1625603222768519648)
XLA Ops:
  10.6 5.3 collective-permute-done.1
  18.7 163.2 %all-gather.3.cloned.1.call-done = bf16[256,5,2048]{2,0,1:T(8,128)(2,1)} async-done(((bf16[8,5,2048]{2,0,1:T(8,128)(2,1)}), bf16[256,5,2048]{2,0,1:T(8,128)(2,1)}) %all-gather.3.cloned.1.call-update) | async-done | bytes 5242896 | tf_op jit(solution)/shard_map/all_gather | solution.py:95
  181.9 7.9 %copy.74 = bf16[256,5,2048]{0,2,1:T(8,128)(2,1)} copy(bf16[256,5,2048]{2,0,1:T(8,128)(2,1)} %all-gather.3.cloned.1.call-done) | data formatting | bytes 10485760 | tf_op jit(solution)/shard_map/all_gather | solution.py:95
  189.8 6.1 %pad_bitcast_fusion.1 = bf16[256,5,34,1,66]{0,4,2,1,3:T(8,128)(2,1)S(1)} fusion(bf16[256,5,32,64]{0,3,2,1:T(8,128)(2,1)} %bitcast.228), kind=kLoop, calls=%fused_computation.125 | loop fusion | bytes 10987520 | tf_op jit(solution)/shard_map/broadcast_in_dim | solution.py:41
  195.9 22.9 %pad_slice_fusion = (bf16[256,3,32,64]{0,3,2,1:T(8,128)(2,1)}, bf16[256,3,32,64]{0,3,2,1:T(8,128)(2,1)}, bf16[256,3,32,64]{0,3,2,1:T(8,128)(2,1)}, bf16[256,3,32...) fusion(bf16[256,5,32,64]{0,3,2,1:T(8,128)(2,1)S(1)} %bitcast.231), kind=kLoop, calls=%fused_computation.101 | loop fusion | bytes 65011712 | tf_op jit(solution)/shard_map/slice | solution.py:59
  218.8 10.3 %pad_slice_fusion.1 = (bf16[256,3,32,64]{0,3,2,1:T(8,128)(2,1)}, bf16[256,3,32,64]{0,3,2,1:T(8,128)(2,1)}, bf16[256,3,32,64]{0,3,2,1:T(8,128)(2,1)}, bf16[256,3,...) fusion(bf16[256,5,32,64]{0,3,2,1:T(8,128)(2,1)S(1)} %bitcast.232), kind=kLoop, calls=%fused_computation.102 | loop fusion | bytes 39845888 | tf_op jit(solution)/shard_map/slice | solution.py:59
  229.1 4.1 copy.91
  233.2 3.5 pad.10.clone
  236.7 3.9 copy.77
  240.7 1.7 slice.131
  242.4 28.2 %fusion.4 = f32[3,32,8,9,8]{4,2,3,1,0:T(8,128)} fusion(bf16[8,3,3,3,256]{4,0,3,2,1:T(8,128)(2,1)S(1)} %bitcast.295, bf16[256,5,34,1,7,2]{0,4,5,2,1,3:T(8,128)(2,1)S(1)} %slice.131, bf16[256,5,34,1,8,9]{0,4,5,2,1,3:T(8,128)(2,1)} %copy.77), kind=kOutput, calls=%fused_computation.5 | convolution fusion | flops 787390464 | bytes 7817216 | tf_op jit(solution)/shard_map/conv_general_dilated | solution.py:40
  270.6 2.8 copy.78
  274.5 2.3 copy.79
  277.9 1.7 multiply_convert_fusion
  283.0 2.6 fusion.19
  315.0 15.5 %all_to_all.18 = bf16[32,2,864]{2,1,0:T(2,128)(2,1)S(1)} all-to-all(bf16[32,2,864]{2,1,0:T(2,128)(2,1)S(1)} %reshape.157), channel_id=1, replica_groups=mesh['space'=4,'filt'=32] {'filt'}, dimensions={0} | all-to-all | bytes 221184 | tf_op jit(solution)/shard_map/all_to_all | solution.py:104
  332.8 24.2 %all-reduce.4.cloned.1.call-done = bf16[8,27,256]{2,0,1:T(8,128)(2,1)} async-done(((bf16[8,27,256]{2,0,1:T(8,128)(2,1)}), bf16[8,27,256]{2,0,1:T(8,128)(2,1)}) %all-reduce.4.cloned.1.call-update) | async-done | bytes 110608 | tf_op jit(solution)/shard_map/psum | solution.py:111
  358.6 160.9 %all-gather.5.cloned.1.call-done = bf16[256,5,2048]{2,0,1:T(8,128)(2,1)} async-done(((bf16[8,5,2048]{2,0,1:T(8,128)(2,1)}), bf16[256,5,2048]{2,0,1:T(8,128)(2,1)}) %all-gather.5.cloned.1.call-update) | async-done | bytes 5242896 | tf_op jit(solution)/shard_map/all_gather | solution.py:106
  519.5 7.9 %copy.80 = bf16[256,5,2048]{0,2,1:T(8,128)(2,1)} copy(bf16[256,5,2048]{2,0,1:T(8,128)(2,1)} %all-gather.5.cloned.1.call-done) | data formatting | bytes 10485760 | tf_op jit(solution)/shard_map/all_gather | solution.py:106
  527.3 6.0 %pad_bitcast_fusion = bf16[256,5,34,1,66]{0,4,2,1,3:T(8,128)(2,1)S(1)} fusion(bf16[256,5,32,64]{0,3,2,1:T(8,128)(2,1)} %bitcast.262), kind=kLoop, calls=%fused_computation.15 | loop fusion | bytes 10987520 | tf_op jit(solution)/shard_map/broadcast_in_dim | solution.py:41
  533.3 4.1 copy.92
  537.4 3.5 pad.12.clone
  540.9 3.9 copy.83
  546.6 27.1 %fusion.8 = bf16[3,32,8,9,8]{4,2,3,1,0:T(8,128)(2,1)S(1)} fusion(bf16[256,3,3,3,8]{0,4,3,2,1:T(8,128)(2,1)S(1)} %bitcast.296, bf16[256,5,34,1,7,2]{0,4,5,2,1,3:T(8,128)(2,1)S(1)} %slice.135, bf16[256,5,34,1,8,9]{0,4,5,2,1,3:T(8,128)(2,1)} %copy.83), kind=kOutput, calls=%fused_computation.8 | convolution fusion | flops 787390464 | bytes 7706624 | tf_op jit(solution)/shard_map/conv_general_dilated | solution.py:40
  (123 shorter events, 49.5 us)
Async XLA Ops:
  7.2 174.8 %all-gather.3.cloned.1.call-start = ((), (), s32[]{:S(2)}) async-start(), calls=%async_computation.1 | async-start | bytes 5406720 | tf_op jit(solution)/shard_map/all_gather | solution.py:95
  8.0 2.6 collective-permute-start
  9.3 6.6 %collective-permute-start.1 = (bf16[8,1,2048]{2,0,1:T(8,128)(2,1)S(1)}, bf16[8,1,2048]{2,0,1:T(8,128)(2,1)S(1)}, u32[]{:S(2)}, u32[]{:S(2)}) collective-permute-start(bf16[8,1,2048]{2,0,1:T(8,128)(2,1)S(1)} %get-tuple-element.38), channel_id=1, source_target_pairs={{32,0},{64,32},{96,64},{33,1},{65,33},{97,65},{34,2},{66,34},{98,6... | collective-permute-start | bytes 98312 | tf_op jit(solution)/shard_map/ppermute | solution.py:23
  17.5 339.5 %all-reduce.4.cloned.1.call-start = ((), (), s32[]{:S(2)}) async-start(), calls=%async_computation.3 | async-start | bytes 221184 | tf_op jit(solution)/shard_map/psum | solution.py:111
  189.8 6.1 %slice-start = ((s8[5242880]{0:T(1024)(128)(4,1)}), s8[4194304]{0:T(1024)(128)(4,1)S(1)}, s32[]{:S(2)}) async-start(s8[5242880]{0:T(1024)(128)(4,1)} %bitcast.229), calls=%async_computation.4 | async-start | bytes 8388608
  189.8 6.1 %slice-start.1 = ((s8[5242880]{0:T(1024)(128)(4,1)}), s8[1048576]{0:T(1024)(128)(4,1)S(1)}, s32[]{:S(2)}) async-start(s8[5242880]{0:T(1024)(128)(4,1)} %bitcast.229), calls=%async_computation.5 | async-start | bytes 2097152
  236.7 5.6 copy-start.27
  270.6 2.8 copy-start.28
  274.5 11.1 %copy-start.17 = (bf16[256,3,32,64]{0,3,2,1:T(8,128)(2,1)S(1)}, bf16[256,3,32,64]{0,3,2,1:T(8,128)(2,1)}, u32[]{:S(2)}) copy-start(bf16[256,3,32,64]{0,3,2,1:T(8,128)(2,1)} %get-tuple-element.8) | copy-start | bytes 9437188
  280.2 32.5 %collective-permute-start.2 = (bf16[8,1,2048]{2,0,1:T(8,128)(2,1)}, bf16[8,1,2048]{2,0,1:T(8,128)(2,1)S(1)}, u32[]{:S(2)}, u32[]{:S(2)}) collective-permute-start(bf16[8,1,2048]{2,0,1:T(8,128)(2,1)} %get-tuple-element.35), channel_id=1, source_target_pairs={{0,32},{32,64},{64,96},{1,33},{33,65},{65,97},{2,34},{34,66},{66,9... | collective-permute-start | bytes 98312 | tf_op jit(solution)/shard_map/ppermute | solution.py:22
  281.5 31.3 %collective-permute-start.3 = (bf16[8,1,2048]{2,0,1:T(8,128)(2,1)}, bf16[8,1,2048]{2,0,1:T(8,128)(2,1)S(1)}, u32[]{:S(2)}, u32[]{:S(2)}) collective-permute-start(bf16[8,1,2048]{2,0,1:T(8,128)(2,1)} %get-tuple-element.36), channel_id=1, source_target_pairs={{32,0},{64,32},{96,64},{33,1},{65,33},{97,65},{34,2},{66,34},{98,6... | collective-permute-start | bytes 98312 | tf_op jit(solution)/shard_map/ppermute | solution.py:23
  283.0 3.1 copy-start.16
  286.1 2.4 copy-start.25
  287.5 2.1 copy-start.14
  289.6 2.1 copy-start.12
  291.8 2.1 copy-start.10
  293.9 2.1 copy-start.8
  294.7 2.1 copy-start.7
  296.0 2.1 copy-start.24
  296.8 2.1 copy-start.6
  298.9 2.1 copy-start.4
  306.5 2.1 copy-start.20
  309.4 2.1 copy-start
  312.7 206.8 %all-gather.5.cloned.1.call-start = ((), (), s32[]{:S(2)}) async-start(), calls=%async_computation.2 | async-start | bytes 5406720 | tf_op jit(solution)/shard_map/all_gather | solution.py:106
  (14 other events, 27.8 us)
Sparse Core Ops, SparseCore 0:
  17.6 164.2 all-gather.2
  312.9 44.0 all-reduce.3
  358.8 160.6 all-gather.4
where the time goes:
time: 591 us; the launch traced here: 584 us
  waiting for transfers between devices  354 us (60%)
  local copies, waits for them, and re-layouts  116 us (20%)
  matrix products  71.2 us (12%)
  blocking collectives  15.5 us (3%)
  between operations  14.5 us (2%)
  other arithmetic  7.07 us (1%)
    all_gather x1, waiting for transfers between devices, per_device(): shard_piece = lax.all_gather(x_flat, 'filt', axis=0, tiled=True)  163 us
    all_gather x1, waiting for transfers between devices, per_device(): shard_piece = lax.all_gather(grad_flat, 'filt', axis=0, tiled=True)  161 us
    conv_general_dilated x2, matrix products, conv_block(): lax.conv_general_dilated(x_pad[None], kernel, (1, 1, 1), 'VALID', dimensi...  55.3 us
    slice x2, local copies, waits for them, and re-layouts, filter_grad(): x_pad[:, depth_at:depth_at + depth_n, row_at:row_at + rows_n, col_at:col_...  33.2 us
    unnamed x67, local copies, waits for them, and re-layouts  24.8 us
    psum x1, waiting for transfers between devices, per_device(): lax.psum(weight_part.astype(jnp.bfloat16), 'space').astype(jnp.float32)  24.2 us
    broadcast_in_dim x4, local copies, waits for them, and re-layouts, conv_block(): x_pad[None]  19.1 us
    conv_general_dilated x8, local copies, waits for them, and re-layouts, conv_block(): lax.conv_general_dilated(x_pad[None], kernel, (1, 1, 1), 'VALID', dimensi...  18.8 us
  transfers between devices with their start and end apart: 7, of which 4 were waited for; matrix products, arithmetic and copies ran while one was open for 4% of the time, Pallas kernels for 0%

commit v1 on v0

v1 whole, which is shorter than its diff:
```python
import functools
import math

import jax
import jax.numpy as jnp
from jax import lax
from jax.experimental import pallas as pl
from jax.experimental.pallas import tpu as pltpu
from jax.sharding import PartitionSpec as P

H = 32
W = 64
PLANE = H * W
TAPS = [(kd, kh, kw) for kd in (-1, 0, 1) for kh in (-1, 0, 1) for kw in (-1, 0, 1)]


def moved(x, shift):
    return pltpu.roll(x, shift % x.shape[-1], x.ndim - 1) if shift else x


def columns(rows):
    lane = lax.broadcasted_iota(jnp.int32, (rows, PLANE), 1)
    return lane % W, lane // W


def forward_kernel(planes, block, x_ref, w_ref, own_ref, low_ref, high_ref, maps):
    w = w_ref[...]
    for d in range(planes):
        maps[d] = jnp.dot(
            w, x_ref[:, d * PLANE : (d + 1) * PLANE], preferred_element_type=jnp.float32
        )
    col, row = columns(block)
    for out in range(-1, planes + 1):
        total = None
        for kh in (-1, 0, 1):
            line = None
            for kw in (-1, 0, 1):
                term = None
                for kd in (-1, 0, 1):
                    if 0 <= out + kd < planes:
                        at = TAPS.index((kd, kh, kw)) * block
                        part = maps[out + kd, at : at + block, :]
                        term = part if term is None else term + part
                if kw:
                    inside = (col + kw >= 0) & (col + kw < W)
                    term = jnp.where(inside, moved(term, -kw), 0.0)
                line = term if line is None else line + term
            if kh:
                inside = (row + kh >= 0) & (row + kh < H)
                line = jnp.where(inside, moved(line, -kh * W), 0.0)
            total = line if total is None else total + line
        if out < 0:
            low_ref[...] = total
        elif out >= planes:
            high_ref[...] = total
        else:
            own_ref[:, out * PLANE : (out + 1) * PLANE] = total


def activate_kernel(planes, own_ref, before_ref, after_ref, bias_ref, cot_ref, act_ref, grad_ref):
    for d in range(planes):
        at = slice(d * PLANE, (d + 1) * PLANE)
        pre = own_ref[:, at]
        if d == 0:
            pre = pre + before_ref[...]
        if d == planes - 1:
            pre = pre + after_ref[...]
        pre = pre + bias_ref[...]
        s = jax.nn.sigmoid(pre)
        act_ref[:, at] = (pre * s).astype(act_ref.dtype)
        slope = s * (1.0 + pre * (1.0 - s))
        grad_ref[:, at] = (cot_ref[:, at].astype(jnp.float32) * slope).astype(grad_ref.dtype)


def backward_kernel(
    planes, block, grad_ref, before_ref, after_ref, x_ref, w_ref, part_ref, filt_ref, shifted, bank
):
    col, row = columns(block)
    for src in range(-1, planes + 1):
        if src < 0:
            g = before_ref[...]
        elif src >= planes:
            g = after_ref[...]
        else:
            g = grad_ref[:, src * PLANE : (src + 1) * PLANE]
        g = g.astype(jnp.float32)
        for kh in (-1, 0, 1):
            line = g
            if kh:
                inside = (row - kh >= 0) & (row - kh < H)
                line = jnp.where(inside, moved(g, kh * W), 0.0)
            for kw in (-1, 0, 1):
                term = line
                if kw:
                    inside = (col - kw >= 0) & (col - kw < W)
                    term = jnp.where(inside, moved(line, kw), 0.0)
                for kd in (-1, 0, 1):
                    if 0 <= src + kd < planes:
                        at = TAPS.index((kd, kh, kw)) * block
                        bank[src + kd, at : at + block, :] = term
    w = w_ref[...]
    total = None
    for d in range(planes):
        at = slice(d * PLANE, (d + 1) * PLANE)
        shifted[...] = bank[d].astype(jnp.bfloat16)
        part = lax.dot_general(
            shifted[...], x_ref[:, at], (((1,), (1,)), ((), ())), preferred_element_type=jnp.float32
        )
        total = part if total is None else total + part
        part_ref[:, at] = lax.dot_general(
            w, shifted[...], (((0,), (0,)), ((), ())), preferred_element_type=jnp.float32
        ).astype(part_ref.dtype)
    filt_ref[...] = total.astype(filt_ref.dtype)


def call(kernel, outs, scratch, flops, moved_bytes, name):
    return pl.pallas_call(
        kernel,
        out_shape=outs,
        scratch_shapes=scratch,
        compiler_params=pltpu.CompilerParams(vmem_limit_bytes=48 * 2**20),
        cost_estimate=pl.CostEstimate(flops=flops, bytes_accessed=moved_bytes, transcendentals=0),
        name=name,
    )


def neighbours(last, first):
    size = lax.axis_size("space")
    up = [(i, i + 1) for i in range(size - 1)]
    down = [(i + 1, i) for i in range(size - 1)]
    return lax.ppermute(last, "space", up), lax.ppermute(first, "space", down)


def per_device(features, weight, bias_vec, cotangent):
    block, planes, _ = features.shape
    channels = weight.shape[2]
    parts = lax.axis_size("filt")
    slabs = lax.axis_size("space")
    voxels = planes * PLANE
    rows = len(TAPS) * block
    x_own = features.reshape(block, voxels)
    w = jnp.transpose(weight, (1, 0, 2)).reshape(rows, channels)
    copies = jnp.broadcast_to(x_own[None], (parts, block, voxels))
    x = lax.all_to_all(copies, "filt", 0, 0, tiled=True).reshape(channels, voxels)

    plane_f32 = jax.ShapeDtypeStruct((block, PLANE), jnp.float32)
    flops = 2 * rows * channels * voxels
    own, low, high = call(
        functools.partial(forward_kernel, planes, block),
        (jax.ShapeDtypeStruct((block, voxels), jnp.float32), plane_f32, plane_f32),
        [pltpu.VMEM((planes, rows, PLANE), jnp.float32)],
        flops,
        2 * channels * voxels,
        "conv_forward",
    )(x, w)
    before, after = neighbours(high, low)
    half = jax.ShapeDtypeStruct((block, voxels), jnp.bfloat16)
    bias = jnp.broadcast_to(bias_vec.astype(jnp.float32)[:, None], (block, PLANE))
    activation, grad = call(
        functools.partial(activate_kernel, planes), (half, half), [], 20 * block * voxels, 12 * block * voxels, "activate"
    )(own, before, after, bias, cotangent.reshape(block, voxels))

    before, after = neighbours(grad[:, voxels - PLANE :], grad[:, :PLANE])
    part, filt = call(
        functools.partial(backward_kernel, planes, block),
        (
            jax.ShapeDtypeStruct((channels, voxels), jnp.bfloat16),
            jax.ShapeDtypeStruct((rows, channels), jnp.bfloat16),
        ),
        [
            pltpu.VMEM((rows, PLANE), jnp.bfloat16),
            pltpu.VMEM((planes, rows, PLANE), jnp.float32),
        ],
        2 * flops,
        4 * channels * voxels,
        "conv_backward",
    )(grad, before, after, x, w)
    scale = 1.0 / math.sqrt(planes * slabs * PLANE)
    weight_grad = lax.psum(filt, "space").astype(jnp.float32) * scale
    weight_grad = jnp.transpose(weight_grad.reshape(len(TAPS), block, channels), (1, 0, 2))
    got = lax.all_to_all(part.reshape(parts, block, voxels), "filt", 0, 0, tiled=True)
    input_grad = jnp.sum(got.astype(jnp.float32), axis=0).astype(jnp.bfloat16)
    shape = features.shape
    return activation.reshape(shape), input_grad.reshape(shape), weight_grad


def solution(mesh):
    return jax.shard_map(
        per_device,
        mesh=mesh,
        in_specs=(
            P("filt", "space", None),
            P("filt", None, None),
            P("filt"),
            P("filt", "space", None),
        ),
        out_specs=(P("filt", "space", None), P("filt", "space", None), P("filt", None, None)),
        check_vma=False,
    )
```

time: 591 us -> 157 us (0.27)
  the two profiles are of different devices: /device:TPU:0 before, /device:TPU:1 now
where the time goes in v1:
time: 157 us
  waiting for transfers between devices  63.5 us (40%)
  blocking collectives  47.8 us (30%)
  starting transfers between devices  19.9 us (13%)
  between operations  14.1 us (9%)
  Pallas kernels  7.64 us (5%)
  other arithmetic  2.68 us (2%)
    psum x1, waiting for transfers between devices, per_device(): weight_grad = lax.psum(filt, 'space').astype(jnp.float32) * scale  56.7 us
    all_to_all x1, blocking collectives, per_device(): lax.all_to_all(copies, 'filt', 0, 0, tiled=True).reshape(channels, voxels)  47.8 us
    ppermute x4, starting transfers between devices, neighbours(): return (lax.ppermute(last, 'space', up), lax.ppermute(first, 'space', down))  15.8 us
    ppermute x4, waiting for transfers between devices, neighbours(): return (lax.ppermute(last, 'space', up), lax.ppermute(first, 'space', down))  6.15 us
    pallas_call x1, Pallas kernels, per_device(): call(functools.partial(backward_kernel, planes, block), (jax.ShapeDtypeSt...  5.76 us
    all_to_all x1, starting transfers between devices, per_device(): lax.all_to_all(part.reshape(parts, block, voxels), 'filt', 0, 0, tiled=True)  4.06 us
  transfers between devices with their start and end apart: 6, of which 3 were waited for; matrix products, arithmetic and copies ran while one was open for 1% of the time, Pallas kernels for 0%

profile of v1, /device:TPU:1, one launch (start us, length us, event | category | flops | bytes accessed | tf_op | source)
XLA Modules:
  0.0 156.9 jit_solution(8312609868031881781)
XLA Ops:
  7.2 1.2 broadcast_in_dim.14
  8.4 0.0 copy-start.1
  8.4 47.8 %all_to_all.10 = bf16[32,8,6144]{2,1,0:T(8,128)(2,1)S(1)} all-to-all(bf16[32,8,6144]{2,1,0:T(8,128)(2,1)S(1)} %broadcast_in_dim.14), channel_id=1, replica_groups=mesh['space'=4,'filt'=32] {'filt'}, dimensions={0} | all-to-all | bytes 6291456 | tf_op jit(solution)/shard_map/all_to_all | solution.py:144
  56.2 0.0 copy-done.1
  56.2 1.2 conv_forward.1
  57.4 6.8 %collective-permute-start = (f32[8,2048]{1,0:T(8,128)S(1)}, f32[8,2048]{1,0:T(8,128)S(1)}, u32[]{:S(2)}, u32[]{:S(2)}) collective-permute-start(f32[8,2048]{1,0:T(8,128)S(1)} %get-tuple-element.11), channel_id=1, source_target_pairs={{0,32},{32,64},{64,96},{1,33},{33,65},{65,97},{2,34},{34,66},{66,9... | collective-permute-start | bytes 196616 | tf_op jit(solution)/shard_map/ppermute | solution.py:131
  64.2 1.9 %collective-permute-start.1 = (f32[8,2048]{1,0:T(8,128)S(1)}, f32[8,2048]{1,0:T(8,128)S(1)}, u32[]{:S(2)}, u32[]{:S(2)}) collective-permute-start(f32[8,2048]{1,0:T(8,128)S(1)} %get-tuple-element.12), channel_id=1, source_target_pairs={{32,0},{64,32},{96,64},{33,1},{65,33},{97,65},{34,2},{66,34},{98,6... | collective-permute-start | bytes 196616 | tf_op jit(solution)/shard_map/ppermute | solution.py:131
  66.1 0.0 collective-permute-done.before_ref
  66.1 5.2 %collective-permute-done.1.after_ref = f32[8,2048]{1,0:T(8,128)S(1)} collective-permute-done((f32[8,2048]{1,0:T(8,128)S(1)}, f32[8,2048]{1,0:T(8,128)S(1)}, u32[]{:S(2)}, u32[]{:S(2)}) %collective-permute-start.1) | collective-permute-done | bytes 65568 | tf_op jit(solution)/shard_map/ppermute | solution.py:131
  71.3 0.0 copy-done.3
  71.3 0.1 broadcast_in_dim.15.bias_ref
  71.4 0.7 activate.1
  72.1 1.9 %collective-permute-start.3 = (bf16[8,2048]{1,0:T(8,128)(2,1)S(1)}, bf16[8,2048]{1,0:T(8,128)(2,1)S(1)}, u32[]{:S(2)}, u32[]{:S(2)}) collective-permute-start(bf16[8,2048]{1,0:T(8,128)(2,1)S(1)} %get-tuple-element.17), channel_id=1, source_target_pairs={{32,0},{64,32},{96,64},{33,1},{65,33},{97,65},{34,2},{66,34},{98,6... | collective-permute-start | bytes 98312 | tf_op jit(solution)/shard_map/ppermute | solution.py:131
  74.0 5.1 %collective-permute-start.2 = (bf16[8,2048]{1,0:T(8,128)(2,1)S(1)}, bf16[8,2048]{1,0:T(8,128)(2,1)S(1)}, u32[]{:S(2)}, u32[]{:S(2)}) collective-permute-start(bf16[8,2048]{1,0:T(8,128)(2,1)S(1)} %get-tuple-element.18), channel_id=1, source_target_pairs={{0,32},{32,64},{64,96},{1,33},{33,65},{65,97},{2,34},{34,66},{66,9... | collective-permute-start | bytes 98312 | tf_op jit(solution)/shard_map/ppermute | solution.py:131
  79.1 0.0 collective-permute-done.3.after_ref
  79.2 1.0 collective-permute-done.2.before_ref
  80.1 5.8 %conv_backward.1 = (bf16[256,6144]{1,0:T(8,128)(2,1)}, bf16[216,256]{1,0:T(8,128)(2,1)}) custom-call(bf16[8,6144]{1,0:T(8,128)(2,1)S(1)} %get-tuple-element.14.grad_ref, bf16[8,2048]{1,0:T(8,128)(2,1)S(1)} %collective-permute-done.2.before_ref, bf16[8,2048]{1,0:T(8,128)(2,1)S(1)} %collective-permute-done.3.after_ref, bf16[256,6144]{1,0:T(8,128)(2,1)} %bitcast.14, ...), custom_call_target="tpu_custom_call" | custom-call | flops 1358954496 | bytes 6291456 | tf_op jit(solution)/shard_map/conv_backward/pallas_call | solution.py:164
  85.9 4.1 %all-to-all-start.1 = ((bf16[32,8,6144]{2,1,0:T(8,128)(2,1)}), bf16[32,8,6144]{2,1,0:T(8,128)(2,1)S(1)}, u32[]{:S(2)}, u32[]{:S(2)}) async-start(bf16[32,8,6144]{2,1,0:T(8,128)(2,1)} %bitcast.7), calls=%async_computation.1 | async-start | bytes 6291456 | tf_op jit(solution)/shard_map/all_to_all | solution.py:181
  90.0 0.0 all-reduce.2.cloned.1.call-start
  90.0 0.7 all-reduce.2.cloned.1.call-update
  90.7 56.7 %all-reduce.2.cloned.1.call-done = bf16[216,256]{1,0:T(8,128)(2,1)} async-done(((bf16[216,256]{1,0:T(8,128)(2,1)}), bf16[216,256]{1,0:T(8,128)(2,1)}) %all-reduce.2.cloned.1.call-update) | async-done | bytes 110608 | tf_op jit(solution)/shard_map/psum | solution.py:179
  147.4 1.6 %multiply_bitcast_fusion = f32[8,27,256]{2,0,1:T(8,128)} fusion(bf16[216,256]{1,0:T(8,128)(2,1)} %all-reduce.2.cloned.1.call-done), kind=kLoop, calls=%fused_computation | loop fusion | flops 110592 | bytes 331776 | tf_op jit(solution)/shard_map/transpose | solution.py:180
  149.0 0.0 all-to-all-done.1
  149.0 1.1 reduce_sum.12
  (6 shorter events, 0.0 us)
Async XLA Ops:
  8.4 47.8 %copy-start.1 = (bf16[8,27,256]{2,0,1:T(8,128)(2,1)S(1)}, bf16[8,27,256]{2,0,1:T(8,128)(2,1)}, u32[]{:S(2)}) copy-start(bf16[8,27,256]{2,0,1:T(8,128)(2,1)} %param.5) | copy-start | bytes 331780
  56.2 23.9 %copy-start = (bf16[32,8,6144]{2,1,0:T(8,128)(2,1)}, bf16[32,8,6144]{2,1,0:T(8,128)(2,1)S(1)}, u32[]{:S(2)}) copy-start(bf16[32,8,6144]{2,1,0:T(8,128)(2,1)S(1)} %all_to_all.10) | copy-start | bytes 9437188
  56.2 15.1 %copy-start.3 = (bf16[8]{0:T(256)(128)(2,1)S(1)}, bf16[8]{0:T(256)(128)(2,1)}, u32[]{:S(2)}) copy-start(bf16[8]{0:T(256)(128)(2,1)} %param.6) | copy-start | bytes 52
  56.2 15.2 %copy-start.2 = (bf16[8,3,2048]{2,0,1:T(8,128)(2,1)S(1)}, bf16[8,3,2048]{2,0,1:T(8,128)(2,1)}, u32[]{:S(2)}) copy-start(bf16[8,3,2048]{2,0,1:T(8,128)(2,1)} %param.7) | copy-start | bytes 294916
  57.4 8.7 %collective-permute-start = (f32[8,2048]{1,0:T(8,128)S(1)}, f32[8,2048]{1,0:T(8,128)S(1)}, u32[]{:S(2)}, u32[]{:S(2)}) collective-permute-start(f32[8,2048]{1,0:T(8,128)S(1)} %get-tuple-element.11), channel_id=1, source_target_pairs={{0,32},{32,64},{64,96},{1,33},{33,65},{65,97},{2,34},{34,66},{66,9... | collective-permute-start | bytes 196616 | tf_op jit(solution)/shard_map/ppermute | solution.py:131
  64.2 7.1 %collective-permute-start.1 = (f32[8,2048]{1,0:T(8,128)S(1)}, f32[8,2048]{1,0:T(8,128)S(1)}, u32[]{:S(2)}, u32[]{:S(2)}) collective-permute-start(f32[8,2048]{1,0:T(8,128)S(1)} %get-tuple-element.12), channel_id=1, source_target_pairs={{32,0},{64,32},{96,64},{33,1},{65,33},{97,65},{34,2},{66,34},{98,6... | collective-permute-start | bytes 196616 | tf_op jit(solution)/shard_map/ppermute | solution.py:131
  72.1 7.1 %collective-permute-start.3 = (bf16[8,2048]{1,0:T(8,128)(2,1)S(1)}, bf16[8,2048]{1,0:T(8,128)(2,1)S(1)}, u32[]{:S(2)}, u32[]{:S(2)}) collective-permute-start(bf16[8,2048]{1,0:T(8,128)(2,1)S(1)} %get-tuple-element.17), channel_id=1, source_target_pairs={{32,0},{64,32},{96,64},{33,1},{65,33},{97,65},{34,2},{66,34},{98,6... | collective-permute-start | bytes 98312 | tf_op jit(solution)/shard_map/ppermute | solution.py:131
  74.0 6.2 %collective-permute-start.2 = (bf16[8,2048]{1,0:T(8,128)(2,1)S(1)}, bf16[8,2048]{1,0:T(8,128)(2,1)S(1)}, u32[]{:S(2)}, u32[]{:S(2)}) collective-permute-start(bf16[8,2048]{1,0:T(8,128)(2,1)S(1)} %get-tuple-element.18), channel_id=1, source_target_pairs={{0,32},{32,64},{64,96},{1,33},{33,65},{65,97},{2,34},{34,66},{66,9... | collective-permute-start | bytes 98312 | tf_op jit(solution)/shard_map/ppermute | solution.py:131
  85.9 63.1 %all-to-all-start.1 = ((bf16[32,8,6144]{2,1,0:T(8,128)(2,1)}), bf16[32,8,6144]{2,1,0:T(8,128)(2,1)S(1)}, u32[]{:S(2)}, u32[]{:S(2)}) async-start(bf16[32,8,6144]{2,1,0:T(8,128)(2,1)} %bitcast.7), calls=%async_computation.1 | async-start | bytes 6291456 | tf_op jit(solution)/shard_map/all_to_all | solution.py:181
  90.0 57.4 %all-reduce.2.cloned.1.call-start = ((), (), s32[]{:S(2)}) async-start(), calls=%async_computation.2 | async-start | bytes 221184 | tf_op jit(solution)/shard_map/psum | solution.py:179
Sparse Core Ops, SparseCore 0:
  93.9 53.4 all-reduce.1

commit v2 on v0

v2 whole, which is shorter than its diff:
```python
import functools
import math

import jax
import jax.numpy as jnp
from jax import lax
from jax.experimental import pallas as pl
from jax.experimental.pallas import tpu as pltpu
from jax.sharding import PartitionSpec as P

H = 32
W = 64
PLANE = H * W
TAPS = [(kd, kh, kw) for kd in (-1, 0, 1) for kh in (-1, 0, 1) for kw in (-1, 0, 1)]
RING = 4
ROWS = H // RING
INNER = ROWS * W
OUTER = INNER + 2 * W
BLOCK = 8
WIDE = 256
TAP_ROWS = 224
F32 = jnp.float32
BF16 = jnp.bfloat16


def moved(x, shift):
    return pltpu.roll(x, shift % x.shape[-1], x.ndim - 1) if shift else x


def fold(x):
    return jnp.concatenate([x[:, :WIDE], x[:, WIDE:]], axis=0)


def unfold(x):
    return jnp.concatenate([x[:BLOCK], x[BLOCK:]], axis=1)


def inside_row(rows, kw):
    col = lax.broadcasted_iota(jnp.int32, (rows, OUTER), 1) % W
    return (col + kw >= 0) & (col + kw < W)


def pack_kernel(planes, at_ref, x_ref, cot_ref, w_ref, bias_ref, chunks_ref, *packs):
    w = jnp.concatenate([w_ref[...].astype(F32), jnp.zeros((BLOCK, WIDE), F32)], 0).astype(BF16)
    bias = bias_ref[...].astype(F32)
    bias = jnp.concatenate([bias, bias], 0).astype(BF16)
    for m, pack in enumerate(packs):
        pack[0:TAP_ROWS, :] = w
        chunk = jnp.bitwise_xor(at_ref[0], m)
        for d in range(planes):
            lanes = pl.ds(pl.multiple_of(chunk * INNER + d * PLANE, INNER), INNER)
            start = TAP_ROWS + 16 * d
            pack[start : start + 16, :] = fold(cot_ref[:, lanes].astype(F32)).astype(BF16)
        start = TAP_ROWS + 16 * planes
        pack[start : start + 16, :] = bias
    lane = lax.broadcasted_iota(jnp.int32, (BLOCK, 2 * W), 1)
    for v in range(RING):
        for d in range(planes):
            base = d * PLANE + v * INNER
            halo = jnp.zeros((BLOCK, 2 * W), F32)
            if v < RING - 1:
                below = x_ref[:, base + INNER : base + INNER + 2 * W].astype(F32)
                halo = jnp.where(lane < W, below, halo)
            if v > 0:
                above = x_ref[:, base - 2 * W : base].astype(F32)
                halo = jnp.where(lane < W, halo, above)
            own = x_ref[:, base : base + INNER]
            for g in range(chunks_ref.shape[0] // RING):
                chunks_ref[g * RING + v, :, d * OUTER : d * OUTER + INNER] = own
                chunks_ref[g * RING + v, :, d * OUTER + INNER : (d + 1) * OUTER] = halo.astype(BF16)


def forward_kernel(planes, x_ref, *refs):
    packs, (own_ref, low_ref, high_ref, up_ref, down_ref, maps) = refs[:RING], refs[RING:]
    for m in range(RING):
        maps[m] = jnp.dot(packs[m][0:TAP_ROWS, :], x_ref[...], preferred_element_type=F32)
    masks = {kw: inside_row(BLOCK, kw) for kw in (-1, 1)}
    for out in range(-1, planes + 1):
        pieces = []
        for m in range(RING):
            total = None
            for kh in (-1, 0, 1):
                line = None
                for kw in (-1, 0, 1):
                    term = None
                    for kd in (-1, 0, 1):
                        if 0 <= out + kd < planes:
                            at = TAPS.index((kd, kh, kw)) * BLOCK
                            d = out + kd
                            part = maps[m, at : at + BLOCK, d * OUTER : (d + 1) * OUTER]
                            term = part if term is None else term + part
                    if kw:
                        term = jnp.where(masks[kw], moved(term, -kw), 0.0)
                    line = term if line is None else line + term
                line = moved(line, -kh * W)
                total = line if total is None else total + line
            pieces.append(total[:, :INNER])
        total = jnp.concatenate(pieces, 0)
        if out < 0:
            low_ref[...] = total
            down_ref[:, 0:INNER] = total.astype(BF16)
        elif out >= planes:
            high_ref[...] = total
            up_ref[:, 0:INNER] = total.astype(BF16)
        else:
            own_ref[:, out * INNER : (out + 1) * INNER] = total
        for edge, ref in ((planes - 1, up_ref), (0, down_ref)):
            if out == edge:
                ref[:, INNER : 2 * INNER] = total.astype(BF16)
                ref[:, 2 * INNER : 3 * INNER] = upstream(packs, out).astype(BF16)


def upstream(packs, d):
    start = TAP_ROWS + 16 * d
    return jnp.concatenate([unfold(p[start : start + 16, :].astype(F32)) for p in packs], 0)


def backward_kernel(planes, x_ref, own_ref, low_ref, high_ref, before_ref, after_ref, *refs):
    packs, part_ref, backs = refs[:RING], refs[RING], refs[RING + 1 : 2 * RING + 1]
    bank, shifted = refs[2 * RING + 1 :]
    start = TAP_ROWS + 16 * planes
    bias = jnp.concatenate([p[start : start + BLOCK, 0:1].astype(F32) for p in packs], 0)
    masks = {kw: inside_row(BLOCK, kw) for kw in (-1, 1)}
    for m in range(RING):
        end = (m + 1) * TAP_ROWS
        bank[end - BLOCK : end, :] = jnp.zeros((BLOCK, planes * OUTER), F32)
    for src in range(-1, planes + 1):
        if src < 0:
            pre = before_ref[:, INNER : 2 * INNER].astype(F32) + low_ref[...]
            cot = before_ref[:, 2 * INNER : 3 * INNER].astype(F32)
        elif src >= planes:
            pre = after_ref[:, INNER : 2 * INNER].astype(F32) + high_ref[...]
            cot = after_ref[:, 2 * INNER : 3 * INNER].astype(F32)
        else:
            pre = own_ref[:, src * INNER : (src + 1) * INNER]
            cot = upstream(packs, src)
            if src == 0:
                pre = pre + before_ref[:, 0:INNER].astype(F32)
            if src == planes - 1:
                pre = pre + after_ref[:, 0:INNER].astype(F32)
        pre = pre + bias
        s = jax.nn.sigmoid(pre)
        if 0 <= src < planes:
            act = pre * s
            at = TAP_ROWS + 16 * src
            for m in range(RING):
                rows = act[m * BLOCK : (m + 1) * BLOCK]
                backs[m][at : at + 16, :] = fold(rows).astype(BF16)
        grad = (cot * (s * (1.0 + pre * (1.0 - s)))).astype(BF16).astype(F32)
        grad = jnp.concatenate([grad, jnp.zeros((grad.shape[0], 2 * W), F32)], 1)
        for m in range(RING):
            own = grad[m * BLOCK : (m + 1) * BLOCK]
            for kh in (-1, 0, 1):
                line = moved(own, kh * W)
                for kw in (-1, 0, 1):
                    term = line
                    if kw:
                        term = jnp.where(masks[-kw], moved(line, kw), 0.0)
                    for kd in (-1, 0, 1):
                        d = src + kd
                        if 0 <= d < planes:
                            at = m * TAP_ROWS + TAPS.index((kd, kh, kw)) * BLOCK
                            bank[at : at + BLOCK, d * OUTER : (d + 1) * OUTER] = term
    shifted[...] = bank[...].astype(BF16)
    filt = lax.dot_general(
        shifted[...], x_ref[...], (((1,), (1,)), ((), ())), preferred_element_type=F32
    )
    for m in range(RING):
        backs[m][0:TAP_ROWS, :] = filt[m * TAP_ROWS : (m + 1) * TAP_ROWS].astype(BF16)
    w = jnp.concatenate([p[0:TAP_ROWS, :] for p in packs], 0)
    part_ref[...] = lax.dot_general(
        w, shifted[...], (((0,), (0,)), ((), ())), preferred_element_type=F32
    ).astype(BF16)


def unpack_kernel(planes, at_ref, *refs):
    backs, (filt_ref, act_ref) = refs[:RING], refs[RING:]
    total = None
    for m, back in enumerate(backs):
        part = back[0:TAP_ROWS, :].astype(F32)
        total = part if total is None else total + part
        chunk = jnp.bitwise_xor(at_ref[0], m)
        for d in range(planes):
            lanes = pl.ds(pl.multiple_of(chunk * INNER + d * PLANE, INNER), INNER)
            start = TAP_ROWS + 16 * d
            act_ref[:, lanes] = unfold(back[start : start + 16, :].astype(F32)).astype(BF16)
    filt_ref[...] = total.astype(BF16)


def collect_kernel(planes, got_ref, out_ref):
    lane = lax.broadcasted_iota(jnp.int32, (BLOCK, 2 * W), 1)
    for d in range(planes):
        sums = []
        for v in range(RING):
            total = None
            for g in range(got_ref.shape[0] // RING):
                part = got_ref[g * RING + v, :, d * OUTER : (d + 1) * OUTER].astype(F32)
                total = part if total is None else total + part
            sums.append(total)
        for v in range(RING):
            first, last = sums[v][:, : 2 * W], sums[v][:, INNER - 2 * W : INNER]
            if v > 0:
                first = first + jnp.where(lane < W, sums[v - 1][:, INNER:], 0.0)
            if v < RING - 1:
                last = last + jnp.where(lane < W, 0.0, sums[v + 1][:, INNER:])
            whole = jnp.concatenate([first, sums[v][:, 2 * W : INNER - 2 * W], last], 1)
            base = d * PLANE + v * INNER
            out_ref[:, base : base + INNER] = whole.astype(BF16)


def call(kernel, ins, outs, scratch, flops, moved_bytes, name):
    smem = pl.BlockSpec(memory_space=pltpu.SMEM)
    vmem = pl.BlockSpec(memory_space=pltpu.VMEM)
    shapes = tuple(jax.ShapeDtypeStruct(shape, kind) for shape, kind in outs)
    return pl.pallas_call(
        kernel,
        out_shape=shapes,
        in_specs=[smem if x.dtype == jnp.int32 else vmem for x in ins],
        out_specs=tuple(vmem for _ in outs),
        scratch_shapes=scratch,
        compiler_params=pltpu.CompilerParams(vmem_limit_bytes=48 * 2**20),
        cost_estimate=pl.CostEstimate(flops=flops, bytes_accessed=moved_bytes, transcendentals=0),
        name=name,
    )(*ins)


def per_device(features, weight, bias_vec, cotangent):
    block, planes, _ = features.shape
    channels = weight.shape[2]
    parts = lax.axis_size("filt")
    slabs = lax.axis_size("space")
    voxels = planes * PLANE
    outer = planes * OUTER
    inner = planes * INNER
    group = RING * BLOCK
    at = (lax.axis_index("filt") % RING).astype(jnp.int32).reshape(1)
    w = jnp.transpose(weight, (1, 0, 2)).reshape(len(TAPS) * block, channels)
    bias = jnp.broadcast_to(bias_vec[:, None], (block, WIDE))
    pack = ((TAP_ROWS + 16 * planes + 16, WIDE), BF16)
    chunks, *packs = call(
        functools.partial(pack_kernel, planes),
        (at, features.reshape(block, voxels), cotangent.reshape(block, voxels), w, bias),
        [((parts, block, outer), BF16)] + [pack] * RING,
        [],
        0,
        2 * parts * block * outer,
        "pack",
    )

    def to_ring(values):
        swap = lambda m: [(i, i ^ m) for i in range(parts)]
        return [values[0]] + [lax.ppermute(values[m], "filt", swap(m)) for m in range(1, RING)]

    packs = to_ring(packs)
    x = lax.all_to_all(chunks, "filt", 0, 0, tiled=True).reshape(channels, outer)

    edge = ((group, 3 * INNER), BF16)
    plane = ((group, INNER), F32)
    flops = 2 * RING * TAP_ROWS * channels * outer
    own, low, high, up, down = call(
        functools.partial(forward_kernel, planes),
        (x, *packs),
        [((group, inner), F32), plane, plane, edge, edge],
        [pltpu.VMEM((RING, TAP_ROWS, outer), F32)],
        flops,
        2 * channels * outer,
        "conv_forward",
    )
    before = lax.ppermute(up, "space", [(i, i + 1) for i in range(slabs - 1)])
    after = lax.ppermute(down, "space", [(i + 1, i) for i in range(slabs - 1)])
    back = ((TAP_ROWS + 16 * planes, WIDE), BF16)
    part, *backs = call(
        functools.partial(backward_kernel, planes),
        (x, own, low, high, before, after, *packs),
        [((channels, outer), BF16)] + [back] * RING,
        [
            pltpu.VMEM((RING * TAP_ROWS, outer), F32),
            pltpu.VMEM((RING * TAP_ROWS, outer), BF16),
        ],
        2 * flops,
        4 * channels * outer,
        "conv_backward",
    )
    backs = to_ring(backs)
    got = lax.all_to_all(part.reshape(parts, block, outer), "filt", 0, 0, tiled=True)
    filt, activation = call(
        functools.partial(unpack_kernel, planes),
        (at, *backs),
        [((TAP_ROWS, WIDE), BF16), ((block, voxels), BF16)],
        [],
        0,
        RING * TAP_ROWS * WIDE * 2,
        "unpack",
    )
    for m in (1, 2):
        other = lax.ppermute(filt, "space", [(i, i ^ m) for i in range(slabs)])
        filt = filt.astype(F32) + other.astype(F32)
        filt = filt.astype(BF16) if m == 1 else filt * (1.0 / math.sqrt(planes * slabs * PLANE))
    weight_grad = filt[: len(TAPS) * block].reshape(len(TAPS), block, channels)
    (input_grad,) = call(
        functools.partial(collect_kernel, planes),
        (got,),
        [((block, voxels), BF16)],
        [],
        0,
        2 * channels * outer,
        "collect",
    )
    shape = features.shape
    return (
        activation.reshape(shape),
        input_grad.reshape(shape),
        jnp.transpose(weight_grad, (1, 0, 2)),
    )


def solution(mesh):
    return jax.shard_map(
        per_device,
        mesh=mesh,
        in_specs=(
            P("filt", "space", None),
            P("filt", None, None),
            P("filt"),
            P("filt", "space", None),
        ),
        out_specs=(P("filt", "space", None), P("filt", "space", None), P("filt", None, None)),
        check_vma=False,
    )
```

time: 591 us -> 85.4 us (0.14)
  the two profiles are of different devices: /device:TPU:0 before, /device:TPU:1 now
where the time goes in v2:
time: 85.4 us; the launch traced here: 85 us
  waiting for transfers between devices  41.3 us (48%)
  starting transfers between devices  31.2 us (37%)
  Pallas kernels  7.62 us (9%)
  local copies, waits for them, and re-layouts  3.4 us (4%)
    ppermute x6, waiting for transfers between devices, to_ring(): lax.ppermute(values[m], 'filt', swap(m))  28.4 us
    all_to_all x1, starting transfers between devices, per_device(): lax.all_to_all(chunks, 'filt', 0, 0, tiled=True).reshape(channels, outer)  9.72 us
    ppermute x6, starting transfers between devices, to_ring(): lax.ppermute(values[m], 'filt', swap(m))  7.88 us
    pallas_call x5, Pallas kernels, call(): pl.pallas_call(kernel, out_shape=shapes, in_specs=[smem if x.dtype == jnp...  7.62 us
    ppermute x2, waiting for transfers between devices, per_device(): other = lax.ppermute(filt, 'space', [(i, i ^ m) for i in range(slabs)])  7.41 us
    ppermute x1, starting transfers between devices, per_device(): before = lax.ppermute(up, 'space', [(i, i + 1) for i in range(slabs - 1)])  6.28 us
    ppermute x1, waiting for transfers between devices, per_device(): after = lax.ppermute(down, 'space', [(i + 1, i) for i in range(slabs - 1)])  5.5 us
    all_to_all x1, starting transfers between devices, per_device(): lax.all_to_all(part.reshape(parts, block, outer), 'filt', 0, 0, tiled=True)  5.31 us
  transfers between devices with their start and end apart: 12, of which 7 were waited for; matrix products, arithmetic and copies ran while one was open for 1% of the time, Pallas kernels for 1%

profile of v2, /device:TPU:1, one launch (start us, length us, event | category | flops | bytes accessed | tf_op | source)
XLA Modules:
  0.0 85.0 jit_solution(11927359252857768320)
XLA Ops:
  1.4 0.9 %copy-done = bf16[8,27,256]{2,0,1:T(8,128)(2,1)S(1)} copy-done((bf16[8,27,256]{2,0,1:T(8,128)(2,1)S(1)}, bf16[8,27,256]{2,0,1:T(8,128)(2,1)}, u32[]{:S(2)}) %copy-start) | copy-done | bytes 110616
  2.3 0.9 %copy-done.1 = bf16[8,3,2048]{2,0,1:T(8,128)(2,1)S(1)} copy-done((bf16[8,3,2048]{2,0,1:T(8,128)(2,1)S(1)}, bf16[8,3,2048]{2,0,1:T(8,128)(2,1)}, u32[]{:S(2)}) %copy-start.1) | copy-done | bytes 98328
  3.2 0.9 %copy-done.2 = bf16[8,3,2048]{2,0,1:T(8,128)(2,1)S(1)} copy-done((bf16[8,3,2048]{2,0,1:T(8,128)(2,1)S(1)}, bf16[8,3,2048]{2,0,1:T(8,128)(2,1)}, u32[]{:S(2)}) %copy-start.2) | copy-done | bytes 98328
  4.1 1.1 %pack.1 = (bf16[32,8,1920]{2,1,0:T(8,128)(2,1)}, bf16[288,256]{1,0:T(8,128)(2,1)S(1)}, bf16[288,256]{1,0:T(8,128)(2,1)S(1)}, bf16[288,256]{1,0:T(8,128)(2,1)S(1)}, bf16[288,256]{1,0:T(8,128)(2,1)S(1)}) custom-call(s32[1]{0:T(128)} %bitcast.at_ref, bf16[8,6144]{1,0:T(8,128)(2,1)S(1)} %bitcast.17, bf16[8,6144]{1,0:T(8,128)(2,1)S(1)} %bitcast.18, ...), custom_call_target="tpu_custom_call" | custom-call | bytes 983040 | tf_op jit(solution)/shard_map/pack/pallas_call | solution.py:215
  5.1 9.7 %all-to-all-start = ((bf16[32,8,1920]{2,1,0:T(8,128)(2,1)}), bf16[32,8,1920]{2,1,0:T(8,128)(2,1)S(1)}, u32[]{:S(2)}, u32[]{:S(2)}) async-start(bf16[32,8,1920]{2,1,0:T(8,128)(2,1)} %get-tuple-element.20), calls=%async_computation | async-start | bytes 1966080 | tf_op jit(solution)/shard_map/all_to_all | solution.py:255
  14.9 1.3 %collective-permute-start = (bf16[288,256]{1,0:T(8,128)(2,1)S(1)}, bf16[288,256]{1,0:T(8,128)(2,1)S(1)}, u32[]{:S(2)}, u32[]{:S(2)}) collective-permute-start(bf16[288,256]{1,0:T(8,128)(2,1)S(1)} %get-tuple-element.22), channel_id=1, source_target_pairs={{0,1},{1,0},{2,3},{3,2},{4,5},{5,4},{6,7},{7,6},{8,9},{9,8},{10,11... | collective-permute-start | bytes 442376 | tf_op jit(solution)/shard_map/ppermute | solution.py:252
  16.2 2.4 %collective-permute-start.1 = (bf16[288,256]{1,0:T(8,128)(2,1)S(1)}, bf16[288,256]{1,0:T(8,128)(2,1)S(1)}, u32[]{:S(2)}, u32[]{:S(2)}) collective-permute-start(bf16[288,256]{1,0:T(8,128)(2,1)S(1)} %get-tuple-element.23), channel_id=1, source_target_pairs={{0,2},{1,3},{2,0},{3,1},{4,6},{5,7},{6,4},{7,5},{8,10},{9,11},{10,... | collective-permute-start | bytes 442376 | tf_op jit(solution)/shard_map/ppermute | solution.py:252
  18.8 10.9 %collective-permute-done.refs_1_ = bf16[288,256]{1,0:T(8,128)(2,1)S(1)} collective-permute-done((bf16[288,256]{1,0:T(8,128)(2,1)S(1)}, bf16[288,256]{1,0:T(8,128)(2,1)S(1)}, u32[]{:S(2)}, u32[]{:S(2)}) %collective-permute-start) | collective-permute-done | bytes 147488 | tf_op jit(solution)/shard_map/ppermute | solution.py:252
  29.7 4.7 %collective-permute-done.1.refs_2_ = bf16[288,256]{1,0:T(8,128)(2,1)S(1)} collective-permute-done((bf16[288,256]{1,0:T(8,128)(2,1)S(1)}, bf16[288,256]{1,0:T(8,128)(2,1)S(1)}, u32[]{:S(2)}, u32[]{:S(2)}) %collective-permute-start.1) | collective-permute-done | bytes 147488 | tf_op jit(solution)/shard_map/ppermute | solution.py:252
  34.3 1.4 %conv_forward.1 = (f32[32,1536]{1,0:T(8,128)S(1)}, f32[32,512]{1,0:T(8,128)S(1)}, f32[32,512]{1,0:T(8,128)S(1)}, bf16[32,1536]{1,0:T(8,128)(2,1)S(1)}, bf16[32,1536]{1,0:T(8,128)(2,1)S(1)}) custom-call(bf16[256,1920]{1,0:T(8,128)(2,1)S(1)} %bitcast.14, bf16[288,256]{1,0:T(8,128)(2,1)S(1)} %get-tuple-element.21.refs_0_, ...), custom_call_target="tpu_custom_call" | custom-call | flops 880803840 | bytes 983040 | tf_op jit(solution)/shard_map/conv_forward/pallas_call | solution.py:215
  35.8 6.3 %collective-permute-start.3 = (bf16[32,1536]{1,0:T(8,128)(2,1)S(1)}, bf16[32,1536]{1,0:T(8,128)(2,1)S(1)}, u32[]{:S(2)}, u32[]{:S(2)}) collective-permute-start(bf16[32,1536]{1,0:T(8,128)(2,1)S(1)} %get-tuple-element.28), channel_id=1, source_target_pairs={{0,32},{32,64},{64,96},{1,33},{33,65},{65,97},{2,34},{34,66},{66,9... | collective-permute-start | bytes 294920 | tf_op jit(solution)/shard_map/ppermute | solution.py:269
  42.0 1.9 %collective-permute-start.4 = (bf16[32,1536]{1,0:T(8,128)(2,1)S(1)}, bf16[32,1536]{1,0:T(8,128)(2,1)S(1)}, u32[]{:S(2)}, u32[]{:S(2)}) collective-permute-start(bf16[32,1536]{1,0:T(8,128)(2,1)S(1)} %get-tuple-element.29), channel_id=1, source_target_pairs={{32,0},{64,32},{96,64},{33,1},{65,33},{97,65},{34,2},{66,34},{98,6... | collective-permute-start | bytes 294920 | tf_op jit(solution)/shard_map/ppermute | solution.py:270
  44.0 5.5 %collective-permute-done.4.after_ref = bf16[32,1536]{1,0:T(8,128)(2,1)S(1)} collective-permute-done((bf16[32,1536]{1,0:T(8,128)(2,1)S(1)}, bf16[32,1536]{1,0:T(8,128)(2,1)S(1)}, u32[]{:S(2)}, u32[]{:S(2)}) %collective-permute-start.4) | collective-permute-done | bytes 98336 | tf_op jit(solution)/shard_map/ppermute | solution.py:270
  49.5 3.7 %conv_backward.1 = (bf16[256,1920]{1,0:T(8,128)(2,1)}, bf16[272,256]{1,0:T(8,128)(2,1)S(1)}, bf16[272,256]{1,0:T(8,128)(2,1)S(1)}, bf16[272,256]{1,0:T(8,128)(2,1)S(1)}, bf16[272,256]{1,0:T(8,128)(2,1)S(1)}) custom-call(bf16[256,1920]{1,0:T(8,128)(2,1)S(1)} %bitcast.15, f32[32,1536]{1,0:T(8,128)S(1)} %get-tuple-element.25.own_ref, ...), custom_call_target="tpu_custom_call" | custom-call | flops 1761607680 | bytes 1966080 | tf_op jit(solution)/shard_map/conv_backward/pallas_call | solution.py:215
  53.2 5.3 %all-to-all-start.1 = ((bf16[32,8,1920]{2,1,0:T(8,128)(2,1)}), bf16[32,8,1920]{2,1,0:T(8,128)(2,1)S(1)}, u32[]{:S(2)}, u32[]{:S(2)}) async-start(bf16[32,8,1920]{2,1,0:T(8,128)(2,1)} %bitcast.7), calls=%async_computation.1 | async-start | bytes 1966080 | tf_op jit(solution)/shard_map/all_to_all | solution.py:285
  58.5 1.3 %collective-permute-start.5 = (bf16[272,256]{1,0:T(8,128)(2,1)S(1)}, bf16[272,256]{1,0:T(8,128)(2,1)S(1)}, u32[]{:S(2)}, u32[]{:S(2)}) collective-permute-start(bf16[272,256]{1,0:T(8,128)(2,1)S(1)} %get-tuple-element.31), channel_id=1, source_target_pairs={{0,1},{1,0},{2,3},{3,2},{4,5},{5,4},{6,7},{7,6},{8,9},{9,8},{10,11... | collective-permute-start | bytes 417800 | tf_op jit(solution)/shard_map/ppermute | solution.py:252
  59.8 2.4 %collective-permute-start.6 = (bf16[272,256]{1,0:T(8,128)(2,1)S(1)}, bf16[272,256]{1,0:T(8,128)(2,1)S(1)}, u32[]{:S(2)}, u32[]{:S(2)}) collective-permute-start(bf16[272,256]{1,0:T(8,128)(2,1)S(1)} %get-tuple-element.32), channel_id=1, source_target_pairs={{0,2},{1,3},{2,0},{3,1},{4,6},{5,7},{6,4},{7,5},{8,10},{9,11},{10,... | collective-permute-start | bytes 417800 | tf_op jit(solution)/shard_map/ppermute | solution.py:252
  62.4 9.9 %collective-permute-done.5.refs_1_ = bf16[272,256]{1,0:T(8,128)(2,1)S(1)} collective-permute-done((bf16[272,256]{1,0:T(8,128)(2,1)S(1)}, bf16[272,256]{1,0:T(8,128)(2,1)S(1)}, u32[]{:S(2)}, u32[]{:S(2)}) %collective-permute-start.5) | collective-permute-done | bytes 139296 | tf_op jit(solution)/shard_map/ppermute | solution.py:252
  72.3 3.0 %collective-permute-done.6.refs_2_ = bf16[272,256]{1,0:T(8,128)(2,1)S(1)} collective-permute-done((bf16[272,256]{1,0:T(8,128)(2,1)S(1)}, bf16[272,256]{1,0:T(8,128)(2,1)S(1)}, u32[]{:S(2)}, u32[]{:S(2)}) %collective-permute-start.6) | collective-permute-done | bytes 139296 | tf_op jit(solution)/shard_map/ppermute | solution.py:252
  75.3 0.7 unpack.1
  75.9 1.3 %collective-permute-done.8 = bf16[224,256]{1,0:T(8,128)(2,1)S(1)} collective-permute-done((bf16[224,256]{1,0:T(8,128)(2,1)S(1)}, bf16[224,256]{1,0:T(8,128)(2,1)S(1)}, u32[]{:S(2)}, u32[]{:S(2)}) %collective-permute-start.8) | collective-permute-done | bytes 114720 | tf_op jit(solution)/shard_map/ppermute | solution.py:296
  77.4 6.1 %collective-permute-done.9 = bf16[224,256]{1,0:T(8,128)(2,1)S(1)} collective-permute-done((bf16[224,256]{1,0:T(8,128)(2,1)S(1)}, bf16[224,256]{1,0:T(8,128)(2,1)S(1)}, u32[]{:S(2)}, u32[]{:S(2)}) %collective-permute-start.9) | collective-permute-done | bytes 114720 | tf_op jit(solution)/shard_map/ppermute | solution.py:296
  83.5 0.7 multiply_bitcast_fusion
  84.2 0.8 collect.1
  (16 shorter events, 1.3 us)
Async XLA Ops:
  0.6 0.7 copy-start.3
  1.4 0.9 %copy-start = (bf16[8,27,256]{2,0,1:T(8,128)(2,1)S(1)}, bf16[8,27,256]{2,0,1:T(8,128)(2,1)}, u32[]{:S(2)}) copy-start(bf16[8,27,256]{2,0,1:T(8,128)(2,1)} %param.5) | copy-start | bytes 331780
  2.3 0.9 %copy-start.1 = (bf16[8,3,2048]{2,0,1:T(8,128)(2,1)S(1)}, bf16[8,3,2048]{2,0,1:T(8,128)(2,1)}, u32[]{:S(2)}) copy-start(bf16[8,3,2048]{2,0,1:T(8,128)(2,1)} %param.4) | copy-start | bytes 294916
  3.2 0.9 %copy-start.2 = (bf16[8,3,2048]{2,0,1:T(8,128)(2,1)S(1)}, bf16[8,3,2048]{2,0,1:T(8,128)(2,1)}, u32[]{:S(2)}) copy-start(bf16[8,3,2048]{2,0,1:T(8,128)(2,1)} %param.7) | copy-start | bytes 294916
  5.1 29.2 %all-to-all-start = ((bf16[32,8,1920]{2,1,0:T(8,128)(2,1)}), bf16[32,8,1920]{2,1,0:T(8,128)(2,1)S(1)}, u32[]{:S(2)}, u32[]{:S(2)}) async-start(bf16[32,8,1920]{2,1,0:T(8,128)(2,1)} %get-tuple-element.20), calls=%async_computation | async-start | bytes 1966080 | tf_op jit(solution)/shard_map/all_to_all | solution.py:255
  14.9 14.8 %collective-permute-start = (bf16[288,256]{1,0:T(8,128)(2,1)S(1)}, bf16[288,256]{1,0:T(8,128)(2,1)S(1)}, u32[]{:S(2)}, u32[]{:S(2)}) collective-permute-start(bf16[288,256]{1,0:T(8,128)(2,1)S(1)} %get-tuple-element.22), channel_id=1, source_target_pairs={{0,1},{1,0},{2,3},{3,2},{4,5},{5,4},{6,7},{7,6},{8,9},{9,8},{10,11... | collective-permute-start | bytes 442376 | tf_op jit(solution)/shard_map/ppermute | solution.py:252
  16.2 18.1 %collective-permute-start.1 = (bf16[288,256]{1,0:T(8,128)(2,1)S(1)}, bf16[288,256]{1,0:T(8,128)(2,1)S(1)}, u32[]{:S(2)}, u32[]{:S(2)}) collective-permute-start(bf16[288,256]{1,0:T(8,128)(2,1)S(1)} %get-tuple-element.23), channel_id=1, source_target_pairs={{0,2},{1,3},{2,0},{3,1},{4,6},{5,7},{6,4},{7,5},{8,10},{9,11},{10,... | collective-permute-start | bytes 442376 | tf_op jit(solution)/shard_map/ppermute | solution.py:252
  18.6 15.8 %collective-permute-start.2 = (bf16[288,256]{1,0:T(8,128)(2,1)S(1)}, bf16[288,256]{1,0:T(8,128)(2,1)S(1)}, u32[]{:S(2)}, u32[]{:S(2)}) collective-permute-start(bf16[288,256]{1,0:T(8,128)(2,1)S(1)} %get-tuple-element.24), channel_id=1, source_target_pairs={{0,3},{1,2},{2,1},{3,0},{4,7},{5,6},{6,5},{7,4},{8,11},{9,10},{10,... | collective-permute-start | bytes 442376 | tf_op jit(solution)/shard_map/ppermute | solution.py:252
  35.8 8.2 %collective-permute-start.3 = (bf16[32,1536]{1,0:T(8,128)(2,1)S(1)}, bf16[32,1536]{1,0:T(8,128)(2,1)S(1)}, u32[]{:S(2)}, u32[]{:S(2)}) collective-permute-start(bf16[32,1536]{1,0:T(8,128)(2,1)S(1)} %get-tuple-element.28), channel_id=1, source_target_pairs={{0,32},{32,64},{64,96},{1,33},{33,65},{65,97},{2,34},{34,66},{66,9... | collective-permute-start | bytes 294920 | tf_op jit(solution)/shard_map/ppermute | solution.py:269
  42.0 7.4 %collective-permute-start.4 = (bf16[32,1536]{1,0:T(8,128)(2,1)S(1)}, bf16[32,1536]{1,0:T(8,128)(2,1)S(1)}, u32[]{:S(2)}, u32[]{:S(2)}) collective-permute-start(bf16[32,1536]{1,0:T(8,128)(2,1)S(1)} %get-tuple-element.29), channel_id=1, source_target_pairs={{32,0},{64,32},{96,64},{33,1},{65,33},{97,65},{34,2},{66,34},{98,6... | collective-permute-start | bytes 294920 | tf_op jit(solution)/shard_map/ppermute | solution.py:270
  53.2 31.0 %all-to-all-start.1 = ((bf16[32,8,1920]{2,1,0:T(8,128)(2,1)}), bf16[32,8,1920]{2,1,0:T(8,128)(2,1)S(1)}, u32[]{:S(2)}, u32[]{:S(2)}) async-start(bf16[32,8,1920]{2,1,0:T(8,128)(2,1)} %bitcast.7), calls=%async_computation.1 | async-start | bytes 1966080 | tf_op jit(solution)/shard_map/all_to_all | solution.py:285
  58.5 13.8 %collective-permute-start.5 = (bf16[272,256]{1,0:T(8,128)(2,1)S(1)}, bf16[272,256]{1,0:T(8,128)(2,1)S(1)}, u32[]{:S(2)}, u32[]{:S(2)}) collective-permute-start(bf16[272,256]{1,0:T(8,128)(2,1)S(1)} %get-tuple-element.31), channel_id=1, source_target_pairs={{0,1},{1,0},{2,3},{3,2},{4,5},{5,4},{6,7},{7,6},{8,9},{9,8},{10,11... | collective-permute-start | bytes 417800 | tf_op jit(solution)/shard_map/ppermute | solution.py:252
  59.8 15.5 %collective-permute-start.6 = (bf16[272,256]{1,0:T(8,128)(2,1)S(1)}, bf16[272,256]{1,0:T(8,128)(2,1)S(1)}, u32[]{:S(2)}, u32[]{:S(2)}) collective-permute-start(bf16[272,256]{1,0:T(8,128)(2,1)S(1)} %get-tuple-element.32), channel_id=1, source_target_pairs={{0,2},{1,3},{2,0},{3,1},{4,6},{5,7},{6,4},{7,5},{8,10},{9,11},{10,... | collective-permute-start | bytes 417800 | tf_op jit(solution)/shard_map/ppermute | solution.py:252
  62.2 13.1 %collective-permute-start.7 = (bf16[272,256]{1,0:T(8,128)(2,1)S(1)}, bf16[272,256]{1,0:T(8,128)(2,1)S(1)}, u32[]{:S(2)}, u32[]{:S(2)}) collective-permute-start(bf16[272,256]{1,0:T(8,128)(2,1)S(1)} %get-tuple-element.33), channel_id=1, source_target_pairs={{0,3},{1,2},{2,1},{3,0},{4,7},{5,6},{6,5},{7,4},{8,11},{9,10},{10,... | collective-permute-start | bytes 417800 | tf_op jit(solution)/shard_map/ppermute | solution.py:252
  75.9 1.3 %collective-permute-start.8 = (bf16[224,256]{1,0:T(8,128)(2,1)S(1)}, bf16[224,256]{1,0:T(8,128)(2,1)S(1)}, u32[]{:S(2)}, u32[]{:S(2)}) collective-permute-start(bf16[224,256]{1,0:T(8,128)(2,1)S(1)} %get-tuple-element.36), channel_id=1, source_target_pairs={{0,32},{32,0},{64,96},{96,64},{1,33},{33,1},{65,97},{97,65},{2,34}... | collective-permute-start | bytes 344072 | tf_op jit(solution)/shard_map/ppermute | solution.py:296
  77.3 6.2 %collective-permute-start.9 = (bf16[224,256]{1,0:T(8,128)(2,1)S(1)}, bf16[224,256]{1,0:T(8,128)(2,1)S(1)}, u32[]{:S(2)}, u32[]{:S(2)}) collective-permute-start(bf16[224,256]{1,0:T(8,128)(2,1)S(1)} %add_convert_fusion), channel_id=1, source_target_pairs={{0,64},{32,96},{64,0},{96,32},{1,65},{33,97},{65,1},{97,33},{2,66}... | collective-permute-start | bytes 344072 | tf_op jit(solution)/shard_map/ppermute | solution.py:296

commit v3 on v2

--- a/solution.py
+++ b/solution.py
@@ -19,6 +19,8 @@
 BLOCK = 8
 WIDE = 256
 TAP_ROWS = 224
+PREPARE = 16 * 10**9
+UNPACK = 16 * 10**9
 F32 = jnp.float32
 BF16 = jnp.bfloat16
 
@@ -40,12 +42,22 @@
     return (col + kw >= 0) & (col + kw < W)
 
 
-def pack_kernel(planes, at_ref, x_ref, cot_ref, w_ref, bias_ref, chunks_ref, *packs):
+def pack_kernel(planes, at_ref, x_any, cot_any, w_any, bias_ref, chunks_ref, *refs):
+    packs, (x_ref, cot_ref, w_ref, sems) = refs[:RING], refs[RING:]
+    copies = [
+        pltpu.make_async_copy(src, dst, sems.at[i])
+        for i, (src, dst) in enumerate(((w_any, w_ref), (cot_any, cot_ref), (x_any, x_ref)))
+    ]
+    for copy in copies:
+        copy.start()
+    bias = jnp.broadcast_to(bias_ref[...].astype(F32), (16, BLOCK))
+    bias = jnp.concatenate([bias, jnp.zeros((16, WIDE - BLOCK), F32)], 1).astype(BF16)
+    copies[0].wait()
     w = jnp.concatenate([w_ref[...].astype(F32), jnp.zeros((BLOCK, WIDE), F32)], 0).astype(BF16)
-    bias = bias_ref[...].astype(F32)
-    bias = jnp.concatenate([bias, bias], 0).astype(BF16)
+    for pack in packs:
+        pack[0:TAP_ROWS, :] = w
+    copies[1].wait()
     for m, pack in enumerate(packs):
-        pack[0:TAP_ROWS, :] = w
         chunk = jnp.bitwise_xor(at_ref[0], m)
         for d in range(planes):
             lanes = pl.ds(pl.multiple_of(chunk * INNER + d * PLANE, INNER), INNER)
@@ -53,6 +65,7 @@
             pack[start : start + 16, :] = fold(cot_ref[:, lanes].astype(F32)).astype(BF16)
         start = TAP_ROWS + 16 * planes
         pack[start : start + 16, :] = bias
+    copies[2].wait()
     lane = lax.broadcasted_iota(jnp.int32, (BLOCK, 2 * W), 1)
     for v in range(RING):
         for d in range(planes):
@@ -70,10 +83,29 @@
                 chunks_ref[g * RING + v, :, d * OUTER + INNER : (d + 1) * OUTER] = halo.astype(BF16)
 
 
-def forward_kernel(planes, x_ref, *refs):
-    packs, (own_ref, low_ref, high_ref, up_ref, down_ref, maps) = refs[:RING], refs[RING:]
-    for m in range(RING):
-        maps[m] = jnp.dot(packs[m][0:TAP_ROWS, :], x_ref[...], preferred_element_type=F32)
+def prepare_kernel(planes, *refs):
+    packs, (w_ref, turned_ref, cot_ref, bias_ref) = refs[:RING], refs[RING:]
+    diagonal = lax.broadcasted_iota(jnp.int32, (BLOCK, 2 * W), 0) == lax.broadcasted_iota(
+        jnp.int32, (BLOCK, 2 * W), 1
+    )
+    for m, pack in enumerate(packs):
+        own = slice(m * BLOCK, (m + 1) * BLOCK)
+        w_ref[m * TAP_ROWS : (m + 1) * TAP_ROWS, :] = pack[0:TAP_ROWS, :]
+        for d in range(planes):
+            start = TAP_ROWS + 16 * d
+            lanes = slice(d * INNER, (d + 1) * INNER)
+            cot_ref[own, lanes] = unfold(pack[start : start + 16, :].astype(F32))
+        start = TAP_ROWS + 16 * planes
+        row = pack[start : start + 16, 0 : 2 * W].astype(F32)[:BLOCK]
+        bias = jnp.sum(jnp.where(diagonal, row, 0.0), axis=1, keepdims=True)
+        bias_ref[own, :] = jnp.broadcast_to(bias, (BLOCK, 2 * W))
+    turned_ref[...] = w_ref[...].T
+
+
+def forward_kernel(
+    planes, x_ref, w_ref, cot_ref, own_ref, low_ref, high_ref, up_ref, down_ref, maps
+):
+    maps[...] = jnp.dot(w_ref[...], x_ref[...], preferred_element_type=F32)
     masks = {kw: inside_row(BLOCK, kw) for kw in (-1, 1)}
     for out in range(-1, planes + 1):
         pieces = []
@@ -85,9 +117,9 @@
                     term = None
                     for kd in (-1, 0, 1):
                         if 0 <= out + kd < planes:
-                            at = TAPS.index((kd, kh, kw)) * BLOCK
+                            at = m * TAP_ROWS + TAPS.index((kd, kh, kw)) * BLOCK
                             d = out + kd
-                            part = maps[m, at : at + BLOCK, d * OUTER : (d + 1) * OUTER]
+                            part = maps[at : at + BLOCK, d * OUTER : (d + 1) * OUTER]
                             term = part if term is None else term + part
                     if kw:
                         term = jnp.where(masks[kw], moved(term, -kw), 0.0)
@@ -107,19 +139,16 @@
         for edge, ref in ((planes - 1, up_ref), (0, down_ref)):
             if out == edge:
                 ref[:, INNER : 2 * INNER] = total.astype(BF16)
-                ref[:, 2 * INNER : 3 * INNER] = upstream(packs, out).astype(BF16)
-
-
-def upstream(packs, d):
-    start = TAP_ROWS + 16 * d
-    return jnp.concatenate([unfold(p[start : start + 16, :].astype(F32)) for p in packs], 0)
-
-
-def backward_kernel(planes, x_ref, own_ref, low_ref, high_ref, before_ref, after_ref, *refs):
-    packs, part_ref, backs = refs[:RING], refs[RING], refs[RING + 1 : 2 * RING + 1]
-    bank, shifted = refs[2 * RING + 1 :]
-    start = TAP_ROWS + 16 * planes
-    bias = jnp.concatenate([p[start : start + BLOCK, 0:1].astype(F32) for p in packs], 0)
+                ref[:, 2 * INNER : 3 * INNER] = cot_ref[
+                    :, out * INNER : (out + 1) * INNER
+                ].astype(BF16)
+
+
+def backward_kernel(
+    planes, x_ref, own_ref, low_ref, high_ref, before_ref, after_ref, cot_ref, bias_ref, *refs
+):
+    shifted, backs, bank = refs[0], refs[1 : RING + 1], refs[RING + 1]
+    bias = bias_ref[:, 0:1]
     masks = {kw: inside_row(BLOCK, kw) for kw in (-1, 1)}
     for m in range(RING):
         end = (m + 1) * TAP_ROWS
@@ -133,7 +162,7 @@
             cot = after_ref[:, 2 * INNER : 3 * INNER].astype(F32)
         else:
             pre = own_ref[:, src * INNER : (src + 1) * INNER]
-            cot = upstream(packs, src)
+            cot = cot_ref[:, src * INNER : (src + 1) * INNER]
             if src == 0:
                 pre = pre + before_ref[:, 0:INNER].astype(F32)
             if src == planes - 1:
@@ -167,10 +196,11 @@
     )
     for m in range(RING):
         backs[m][0:TAP_ROWS, :] = filt[m * TAP_ROWS : (m + 1) * TAP_ROWS].astype(BF16)
-    w = jnp.concatenate([p[0:TAP_ROWS, :] for p in packs], 0)
-    part_ref[...] = lax.dot_general(
-        w, shifted[...], (((0,), (0,)), ((), ())), preferred_element_type=F32
-    ).astype(BF16)
+
+
+def input_kernel(turned_ref, shifted, part_ref):
+    part = jnp.dot(turned_ref[...], shifted[...], preferred_element_type=F32)
+    part_ref[...] = part.astype(BF16)
 
 
 def unpack_kernel(planes, at_ref, *refs):
@@ -208,17 +238,18 @@
             out_ref[:, base : base + INNER] = whole.astype(BF16)
 
 
-def call(kernel, ins, outs, scratch, flops, moved_bytes, name):
+def call(kernel, ins, outs, scratch, flops, moved_bytes, name, hbm=(), limit=48):
     smem = pl.BlockSpec(memory_space=pltpu.SMEM)
     vmem = pl.BlockSpec(memory_space=pltpu.VMEM)
+    anywhere = pl.BlockSpec(memory_space=pl.ANY)
     shapes = tuple(jax.ShapeDtypeStruct(shape, kind) for shape, kind in outs)
     return pl.pallas_call(
         kernel,
         out_shape=shapes,
-        in_specs=[smem if x.dtype == jnp.int32 else vmem for x in ins],
+        in_specs=[smem if x.dtype == jnp.int32 else anywhere if i in hbm else vmem for i, x in enumerate(ins)],
         out_specs=tuple(vmem for _ in outs),
         scratch_shapes=scratch,
-        compiler_params=pltpu.CompilerParams(vmem_limit_bytes=48 * 2**20),
+        compiler_params=pltpu.CompilerParams(vmem_limit_bytes=limit * 2**20),
         cost_estimate=pl.CostEstimate(flops=flops, bytes_accessed=moved_bytes, transcendentals=0),
         name=name,
     )(*ins)
@@ -233,18 +264,24 @@
     outer = planes * OUTER
     inner = planes * INNER
     group = RING * BLOCK
-    at = (lax.axis_index("filt") % RING).astype(jnp.int32).reshape(1)
+    at = jnp.bitwise_and(lax.axis_index("filt"), RING - 1).astype(jnp.int32).reshape(1)
     w = jnp.transpose(weight, (1, 0, 2)).reshape(len(TAPS) * block, channels)
-    bias = jnp.broadcast_to(bias_vec[:, None], (block, WIDE))
     pack = ((TAP_ROWS + 16 * planes + 16, WIDE), BF16)
     chunks, *packs = call(
         functools.partial(pack_kernel, planes),
-        (at, features.reshape(block, voxels), cotangent.reshape(block, voxels), w, bias),
+        (at, features.reshape(block, voxels), cotangent.reshape(block, voxels), w, bias_vec[None]),
         [((parts, block, outer), BF16)] + [pack] * RING,
-        [],
+        [
+            pltpu.VMEM((block, voxels), BF16),
+            pltpu.VMEM((block, voxels), BF16),
+            pltpu.VMEM((len(TAPS) * block, channels), BF16),
+            pltpu.SemaphoreType.DMA((3,)),
+        ],
         0,
         2 * parts * block * outer,
         "pack",
+        (1, 2, 3),
+        61,
     )
 
     def to_ring(values):
@@ -257,11 +294,25 @@
     edge = ((group, 3 * INNER), BF16)
     plane = ((group, INNER), F32)
     flops = 2 * RING * TAP_ROWS * channels * outer
+    w, turned, cot, bias = call(
+        functools.partial(prepare_kernel, planes),
+        packs,
+        [
+            ((RING * TAP_ROWS, channels), BF16),
+            ((channels, RING * TAP_ROWS), BF16),
+            ((group, inner), F32),
+            ((group, 2 * W), F32),
+        ],
+        [],
+        PREPARE,
+        RING * TAP_ROWS * WIDE * 4,
+        "prepare",
+    )
     own, low, high, up, down = call(
         functools.partial(forward_kernel, planes),
-        (x, *packs),
+        (x, w, cot),
         [((group, inner), F32), plane, plane, edge, edge],
-        [pltpu.VMEM((RING, TAP_ROWS, outer), F32)],
+        [pltpu.VMEM((RING * TAP_ROWS, outer), F32)],
         flops,
         2 * channels * outer,
         "conv_forward",
@@ -269,26 +320,32 @@
     before = lax.ppermute(up, "space", [(i, i + 1) for i in range(slabs - 1)])
     after = lax.ppermute(down, "space", [(i + 1, i) for i in range(slabs - 1)])
     back = ((TAP_ROWS + 16 * planes, WIDE), BF16)
-    part, *backs = call(
+    shifted, *backs = call(
         functools.partial(backward_kernel, planes),
-        (x, own, low, high, before, after, *packs),
-        [((channels, outer), BF16)] + [back] * RING,
-        [
-            pltpu.VMEM((RING * TAP_ROWS, outer), F32),
-            pltpu.VMEM((RING * TAP_ROWS, outer), BF16),
-        ],
-        2 * flops,
+        (x, own, low, high, before, after, cot, bias),
+        [((RING * TAP_ROWS, outer), BF16)] + [back] * RING,
+        [pltpu.VMEM((RING * TAP_ROWS, outer), F32)],
+        flops,
         4 * channels * outer,
-        "conv_backward",
+        "filter_gradient",
     )
     backs = to_ring(backs)
+    (part,) = call(
+        input_kernel,
+        (turned, shifted),
+        [((channels, outer), BF16)],
+        [],
+        flops,
+        4 * channels * outer,
+        "input_gradient",
+    )
     got = lax.all_to_all(part.reshape(parts, block, outer), "filt", 0, 0, tiled=True)
     filt, activation = call(
         functools.partial(unpack_kernel, planes),
         (at, *backs),
         [((TAP_ROWS, WIDE), BF16), ((block, voxels), BF16)],
         [],
-        0,
+        UNPACK,
         RING * TAP_ROWS * WIDE * 2,
         "unpack",
     )

time: 85.4 us -> 74.6 us (0.87)
  waiting for transfers between devices: 41.3 us -> 30.2 us
  local copies, waits for them, and re-layouts: 3.4 us -> 0.91 us
  Pallas kernels: 7.62 us -> 9.77 us
    ppermute x6, waiting for transfers between devices: 28.4 us -> 0.33 us  [to_ring(): lax.ppermute(values[m], 'filt', swap(m))]
    all_to_all x1, waiting for transfers between devices: 0.01 us -> 12.5 us  [per_device(): lax.all_to_all(chunks, 'filt', 0, 0, tiled=True).reshape(channels, outer)]
    ppermute x2, waiting for transfers between devices: 7.41 us -> 10.5 us  [per_device(): other = lax.ppermute(filt, 'space', [(i, i ^ m) for i in range(slabs)])]
    unnamed x8 -> x2, local copies, waits for them, and re-layouts: 3.33 us -> 0.91 us
    pallas_call x5 -> x7, Pallas kernels: 7.62 us -> 9.77 us  [call(): pl.pallas_call(kernel, out_shape=shapes, in_specs=[smem if x.dtype == jnp...]
    ppermute x1, starting transfers between devices: 6.28 us -> 7.86 us  [per_device(): before = lax.ppermute(up, 'space', [(i, i + 1) for i in range(slabs - 1)])]
    all_to_all x1, waiting for transfers between devices: 0.01 us -> 1.42 us  [per_device(): lax.all_to_all(part.reshape(parts, block, outer), 'filt', 0, 0, tiled=True)]
    all_to_all x1, starting transfers between devices: 5.31 us -> 3.92 us  [per_device(): lax.all_to_all(part.reshape(parts, block, outer), 'filt', 0, 0, tiled=True)]
  transfers between devices with their start and end apart: 12 -> 12, of which waited for: 7 -> 6; matrix products, arithmetic and copies ran while one was open for 1% -> 1% of each run, Pallas kernels for 1% -> 4%
where the time goes in v3:
time: 74.6 us; the launch traced here: 74.2 us
  starting transfers between devices  31.8 us (43%)
  waiting for transfers between devices  30.2 us (40%)
  Pallas kernels  9.77 us (13%)
  local copies, waits for them, and re-layouts  0.91 us (1%)
  other arithmetic  0.75 us (1%)
  between operations  0.75 us (1%)
    all_to_all x1, waiting for transfers between devices, per_device(): lax.all_to_all(chunks, 'filt', 0, 0, tiled=True).reshape(channels, outer)  12.5 us
    ppermute x2, waiting for transfers between devices, per_device(): other = lax.ppermute(filt, 'space', [(i, i ^ m) for i in range(slabs)])  10.5 us
    pallas_call x7, Pallas kernels, call(): pl.pallas_call(kernel, out_shape=shapes, in_specs=[smem if x.dtype == jnp...  9.77 us
    all_to_all x1, starting transfers between devices, per_device(): lax.all_to_all(chunks, 'filt', 0, 0, tiled=True).reshape(channels, outer)  8.79 us
    ppermute x6, starting transfers between devices, to_ring(): lax.ppermute(values[m], 'filt', swap(m))  8.54 us
    ppermute x1, starting transfers between devices, per_device(): before = lax.ppermute(up, 'space', [(i, i + 1) for i in range(slabs - 1)])  7.86 us
    ppermute x1, waiting for transfers between devices, per_device(): after = lax.ppermute(down, 'space', [(i + 1, i) for i in range(slabs - 1)])  5.5 us
    all_to_all x1, starting transfers between devices, per_device(): lax.all_to_all(part.reshape(parts, block, outer), 'filt', 0, 0, tiled=True)  3.92 us
  transfers between devices with their start and end apart: 12, of which 6 were waited for; matrix products, arithmetic and copies ran while one was open for 1% of the time, Pallas kernels for 4%

profile of v3, /device:TPU:1, one launch (start us, length us, event | category | flops | bytes accessed | tf_op | source)
XLA Modules:
  0.0 74.2 jit_solution(17947596446459129228)
XLA Ops:
  0.6 2.8 %pack.1 = (bf16[32,8,1920]{2,1,0:T(8,128)(2,1)}, bf16[288,256]{1,0:T(8,128)(2,1)}, bf16[288,256]{1,0:T(8,128)(2,1)}, bf16[288,256]{1,0:T(8,128)(2,1)}, bf16[288,256]{1,0:T(8,128)(2,1)}) custom-call(s32[1]{0:T(128)} %bitcast.at_ref, bf16[8,6144]{1,0:T(8,128)(2,1)} %bitcast.19, bf16[8,6144]{1,0:T(8,128)(2,1)} %bitcast.20, bf16[216,256]{1,0:T(8,128)(2,1)} %bitcast.17, ...), custom_call_target="tpu_custom_call" | custom-call | bytes 983040 | tf_op jit(solution)/shard_map/pack/pallas_call | solution.py:246
  3.5 2.1 %collective-permute-start = (bf16[288,256]{1,0:T(8,128)(2,1)}, bf16[288,256]{1,0:T(8,128)(2,1)S(1)}, u32[]{:S(2)}, u32[]{:S(2)}) collective-permute-start(bf16[288,256]{1,0:T(8,128)(2,1)} %get-tuple-element.26), channel_id=1, source_target_pairs={{0,1},{1,0},{2,3},{3,2},{4,5},{5,4},{6,7},{7,6},{8,9},{9,8},{10,11... | collective-permute-start | bytes 442376 | tf_op jit(solution)/shard_map/ppermute | solution.py:289
  5.6 2.5 %collective-permute-start.1 = (bf16[288,256]{1,0:T(8,128)(2,1)}, bf16[288,256]{1,0:T(8,128)(2,1)S(1)}, u32[]{:S(2)}, u32[]{:S(2)}) collective-permute-start(bf16[288,256]{1,0:T(8,128)(2,1)} %get-tuple-element.27), channel_id=1, source_target_pairs={{0,2},{1,3},{2,0},{3,1},{4,6},{5,7},{6,4},{7,5},{8,10},{9,11},{10,... | collective-permute-start | bytes 442376 | tf_op jit(solution)/shard_map/ppermute | solution.py:289
  8.1 8.8 %all-to-all-start = ((bf16[32,8,1920]{2,1,0:T(8,128)(2,1)}), bf16[32,8,1920]{2,1,0:T(8,128)(2,1)S(1)}, u32[]{:S(2)}, u32[]{:S(2)}) async-start(bf16[32,8,1920]{2,1,0:T(8,128)(2,1)} %get-tuple-element.24), calls=%async_computation | async-start | bytes 1966080 | tf_op jit(solution)/shard_map/all_to_all | solution.py:292
  16.9 0.3 collective-permute-done.2.refs_3_
  17.2 0.9 %copy-done = bf16[288,256]{1,0:T(8,128)(2,1)S(1)} copy-done((bf16[288,256]{1,0:T(8,128)(2,1)S(1)}, bf16[288,256]{1,0:T(8,128)(2,1)}, u32[]{:S(2)}) %copy-start) | copy-done | bytes 147480
  18.1 0.2 prepare.1
  18.3 12.5 %all-to-all-done = bf16[32,8,1920]{2,1,0:T(8,128)(2,1)S(1)} async-done(((bf16[32,8,1920]{2,1,0:T(8,128)(2,1)}), bf16[32,8,1920]{2,1,0:T(8,128)(2,1)S(1)}, u32[]{:S(2)}, u32[]{:S(2)}) %all-to-all-start) | async-done | bytes 983072 | tf_op jit(solution)/shard_map/all_to_all | solution.py:292
  30.9 1.4 %conv_forward.1 = (f32[32,1536]{1,0:T(8,128)S(1)}, f32[32,512]{1,0:T(8,128)S(1)}, f32[32,512]{1,0:T(8,128)S(1)}, bf16[32,1536]{1,0:T(8,128)(2,1)S(1)}, bf16[32,1536]{1,0:T(8,128)(2,1)S(1)}) custom-call(bf16[256,1920]{1,0:T(8,128)(2,1)S(1)} %bitcast.15, bf16[896,256]{1,0:T(8,128)(2,1)S(1)} %get-tuple-element.29.w_ref, f32[32,1536]{1,0:T(8,128)S(1)} %get-tuple-element.30.cot_ref), custom_call_target="tpu_custom_call" | custom-call | flops 880803840 | bytes 983040 | tf_op jit(solution)/shard_map/conv_forward/pallas_call | solution.py:246
  32.2 7.9 %collective-permute-start.3 = (bf16[32,1536]{1,0:T(8,128)(2,1)S(1)}, bf16[32,1536]{1,0:T(8,128)(2,1)S(1)}, u32[]{:S(2)}, u32[]{:S(2)}) collective-permute-start(bf16[32,1536]{1,0:T(8,128)(2,1)S(1)} %get-tuple-element.34), channel_id=1, source_target_pairs={{0,32},{32,64},{64,96},{1,33},{33,65},{65,97},{2,34},{34,66},{66,9... | collective-permute-start | bytes 294920 | tf_op jit(solution)/shard_map/ppermute | solution.py:320
  40.1 1.9 %collective-permute-start.4 = (bf16[32,1536]{1,0:T(8,128)(2,1)S(1)}, bf16[32,1536]{1,0:T(8,128)(2,1)S(1)}, u32[]{:S(2)}, u32[]{:S(2)}) collective-permute-start(bf16[32,1536]{1,0:T(8,128)(2,1)S(1)} %get-tuple-element.35), channel_id=1, source_target_pairs={{32,0},{64,32},{96,64},{33,1},{65,33},{97,65},{34,2},{66,34},{98,6... | collective-permute-start | bytes 294920 | tf_op jit(solution)/shard_map/ppermute | solution.py:321
  42.0 5.5 %collective-permute-done.4.after_ref = bf16[32,1536]{1,0:T(8,128)(2,1)S(1)} collective-permute-done((bf16[32,1536]{1,0:T(8,128)(2,1)S(1)}, bf16[32,1536]{1,0:T(8,128)(2,1)S(1)}, u32[]{:S(2)}, u32[]{:S(2)}) %collective-permute-start.4) | collective-permute-done | bytes 98336 | tf_op jit(solution)/shard_map/ppermute | solution.py:321
  47.5 1.7 %filter_gradient.1 = (bf16[896,1920]{1,0:T(8,128)(2,1)S(1)}, bf16[272,256]{1,0:T(8,128)(2,1)S(1)}, bf16[272,256]{1,0:T(8,128)(2,1)S(1)}, bf16[272,256]{1,0:T(8,128)(2,1)S(1)}, bf16[272,256]{1,0:T(8,128)(2,1)S(1)}) custom-call(bf16[256,1920]{1,0:T(8,128)(2,1)S(1)} %bitcast.16, f32[32,1536]{1,0:T(8,128)S(1)} %get-tuple-element.31.own_ref, ...), custom_call_target="tpu_custom_call" | custom-call | flops 880803840 | bytes 1966080 | tf_op jit(solution)/shard_map/filter_gradient/pallas_call | solution.py:246
  49.5 1.8 %collective-permute-start.6 = (bf16[272,256]{1,0:T(8,128)(2,1)S(1)}, bf16[272,256]{1,0:T(8,128)(2,1)S(1)}, u32[]{:S(2)}, u32[]{:S(2)}) collective-permute-start(bf16[272,256]{1,0:T(8,128)(2,1)S(1)} %get-tuple-element.39), channel_id=1, source_target_pairs={{0,2},{1,3},{2,0},{3,1},{4,6},{5,7},{6,4},{7,5},{8,10},{9,11},{10,... | collective-permute-start | bytes 417800 | tf_op jit(solution)/shard_map/ppermute | solution.py:289
  51.3 2.0 %collective-permute-start.7 = (bf16[272,256]{1,0:T(8,128)(2,1)S(1)}, bf16[272,256]{1,0:T(8,128)(2,1)S(1)}, u32[]{:S(2)}, u32[]{:S(2)}) collective-permute-start(bf16[272,256]{1,0:T(8,128)(2,1)S(1)} %get-tuple-element.40), channel_id=1, source_target_pairs={{0,3},{1,2},{2,1},{3,0},{4,7},{5,6},{6,5},{7,4},{8,11},{9,10},{10,... | collective-permute-start | bytes 417800 | tf_op jit(solution)/shard_map/ppermute | solution.py:289
  53.2 2.2 %input_gradient.1 = bf16[256,1920]{1,0:T(8,128)(2,1)} custom-call(bf16[256,896]{1,0:T(8,128)(2,1)S(1)} %get-tuple-element.42.turned_ref, bf16[896,1920]{1,0:T(8,128)(2,1)S(1)} %get-tuple-element.43.shifted), custom_call_target="tpu_custom_call" | custom-call | flops 880803840 | bytes 1966080 | tf_op jit(solution)/shard_map/input_gradient/pallas_call | solution.py:246
  55.4 3.9 %all-to-all-start.1 = ((bf16[32,8,1920]{2,1,0:T(8,128)(2,1)}), bf16[32,8,1920]{2,1,0:T(8,128)(2,1)S(1)}, u32[]{:S(2)}, u32[]{:S(2)}) async-start(bf16[32,8,1920]{2,1,0:T(8,128)(2,1)} %bitcast.8), calls=%async_computation.1 | async-start | bytes 1966080 | tf_op jit(solution)/shard_map/all_to_all | solution.py:342
  59.4 0.7 unpack.1
  60.1 1.3 %collective-permute-done.8 = bf16[224,256]{1,0:T(8,128)(2,1)S(1)} collective-permute-done((bf16[224,256]{1,0:T(8,128)(2,1)S(1)}, bf16[224,256]{1,0:T(8,128)(2,1)S(1)}, u32[]{:S(2)}, u32[]{:S(2)}) %collective-permute-start.8) | collective-permute-done | bytes 114720 | tf_op jit(solution)/shard_map/ppermute | solution.py:353
  61.4 0.8 %collective-permute-start.9 = (bf16[224,256]{1,0:T(8,128)(2,1)S(1)}, bf16[224,256]{1,0:T(8,128)(2,1)S(1)}, u32[]{:S(2)}, u32[]{:S(2)}) collective-permute-start(bf16[224,256]{1,0:T(8,128)(2,1)S(1)} %add_convert_fusion), channel_id=1, source_target_pairs={{0,64},{32,96},{64,0},{96,32},{1,65},{33,97},{65,1},{97,33},{2,66}... | collective-permute-start | bytes 344072 | tf_op jit(solution)/shard_map/ppermute | solution.py:353
  62.2 9.1 %collective-permute-done.9 = bf16[224,256]{1,0:T(8,128)(2,1)S(1)} collective-permute-done((bf16[224,256]{1,0:T(8,128)(2,1)S(1)}, bf16[224,256]{1,0:T(8,128)(2,1)S(1)}, u32[]{:S(2)}, u32[]{:S(2)}) %collective-permute-start.9) | collective-permute-done | bytes 114720 | tf_op jit(solution)/shard_map/ppermute | solution.py:353
  71.3 0.7 multiply_bitcast_fusion
  72.0 1.4 %all-to-all-done.1.got_ref = bf16[32,8,1920]{2,1,0:T(8,128)(2,1)S(1)} async-done(((bf16[32,8,1920]{2,1,0:T(8,128)(2,1)}), bf16[32,8,1920]{2,1,0:T(8,128)(2,1)S(1)}, u32[]{:S(2)}, u32[]{:S(2)}) %all-to-all-start.1) | async-done | bytes 983072 | tf_op jit(solution)/shard_map/all_to_all | solution.py:342
  73.4 0.8 %collect.1 = bf16[8,6144]{1,0:T(8,128)(2,1)} custom-call(bf16[32,8,1920]{2,1,0:T(8,128)(2,1)S(1)} %all-to-all-done.1.got_ref), custom_call_target="tpu_custom_call" | custom-call | bytes 983040 | tf_op jit(solution)/shard_map/collect/pallas_call | solution.py:246
  (11 shorter events, 0.3 us)
Async XLA Ops:
  3.5 13.4 %collective-permute-start = (bf16[288,256]{1,0:T(8,128)(2,1)}, bf16[288,256]{1,0:T(8,128)(2,1)S(1)}, u32[]{:S(2)}, u32[]{:S(2)}) collective-permute-start(bf16[288,256]{1,0:T(8,128)(2,1)} %get-tuple-element.26), channel_id=1, source_target_pairs={{0,1},{1,0},{2,3},{3,2},{4,5},{5,4},{6,7},{7,6},{8,9},{9,8},{10,11... | collective-permute-start | bytes 442376 | tf_op jit(solution)/shard_map/ppermute | solution.py:289
  5.6 11.3 %collective-permute-start.1 = (bf16[288,256]{1,0:T(8,128)(2,1)}, bf16[288,256]{1,0:T(8,128)(2,1)S(1)}, u32[]{:S(2)}, u32[]{:S(2)}) collective-permute-start(bf16[288,256]{1,0:T(8,128)(2,1)} %get-tuple-element.27), channel_id=1, source_target_pairs={{0,2},{1,3},{2,0},{3,1},{4,6},{5,7},{6,4},{7,5},{8,10},{9,11},{10,... | collective-permute-start | bytes 442376 | tf_op jit(solution)/shard_map/ppermute | solution.py:289
  8.0 9.2 %collective-permute-start.2 = (bf16[288,256]{1,0:T(8,128)(2,1)}, bf16[288,256]{1,0:T(8,128)(2,1)S(1)}, u32[]{:S(2)}, u32[]{:S(2)}) collective-permute-start(bf16[288,256]{1,0:T(8,128)(2,1)} %get-tuple-element.28), channel_id=1, source_target_pairs={{0,3},{1,2},{2,1},{3,0},{4,7},{5,6},{6,5},{7,4},{8,11},{9,10},{10,... | collective-permute-start | bytes 442376 | tf_op jit(solution)/shard_map/ppermute | solution.py:289
  8.1 22.8 %all-to-all-start = ((bf16[32,8,1920]{2,1,0:T(8,128)(2,1)}), bf16[32,8,1920]{2,1,0:T(8,128)(2,1)S(1)}, u32[]{:S(2)}, u32[]{:S(2)}) async-start(bf16[32,8,1920]{2,1,0:T(8,128)(2,1)} %get-tuple-element.24), calls=%async_computation | async-start | bytes 1966080 | tf_op jit(solution)/shard_map/all_to_all | solution.py:292
  17.2 0.9 %copy-start = (bf16[288,256]{1,0:T(8,128)(2,1)S(1)}, bf16[288,256]{1,0:T(8,128)(2,1)}, u32[]{:S(2)}) copy-start(bf16[288,256]{1,0:T(8,128)(2,1)} %get-tuple-element.25.refs_0_) | copy-start | bytes 442372
  32.2 9.8 %collective-permute-start.3 = (bf16[32,1536]{1,0:T(8,128)(2,1)S(1)}, bf16[32,1536]{1,0:T(8,128)(2,1)S(1)}, u32[]{:S(2)}, u32[]{:S(2)}) collective-permute-start(bf16[32,1536]{1,0:T(8,128)(2,1)S(1)} %get-tuple-element.34), channel_id=1, source_target_pairs={{0,32},{32,64},{64,96},{1,33},{33,65},{65,97},{2,34},{34,66},{66,9... | collective-permute-start | bytes 294920 | tf_op jit(solution)/shard_map/ppermute | solution.py:320
  40.1 7.4 %collective-permute-start.4 = (bf16[32,1536]{1,0:T(8,128)(2,1)S(1)}, bf16[32,1536]{1,0:T(8,128)(2,1)S(1)}, u32[]{:S(2)}, u32[]{:S(2)}) collective-permute-start(bf16[32,1536]{1,0:T(8,128)(2,1)S(1)} %get-tuple-element.35), channel_id=1, source_target_pairs={{32,0},{64,32},{96,64},{33,1},{65,33},{97,65},{34,2},{66,34},{98,6... | collective-permute-start | bytes 294920 | tf_op jit(solution)/shard_map/ppermute | solution.py:321
  49.3 10.1 %collective-permute-start.5 = (bf16[272,256]{1,0:T(8,128)(2,1)S(1)}, bf16[272,256]{1,0:T(8,128)(2,1)S(1)}, u32[]{:S(2)}, u32[]{:S(2)}) collective-permute-start(bf16[272,256]{1,0:T(8,128)(2,1)S(1)} %get-tuple-element.38), channel_id=1, source_target_pairs={{0,1},{1,0},{2,3},{3,2},{4,5},{5,4},{6,7},{7,6},{8,9},{9,8},{10,11... | collective-permute-start | bytes 417800 | tf_op jit(solution)/shard_map/ppermute | solution.py:289
  49.5 9.9 %collective-permute-start.6 = (bf16[272,256]{1,0:T(8,128)(2,1)S(1)}, bf16[272,256]{1,0:T(8,128)(2,1)S(1)}, u32[]{:S(2)}, u32[]{:S(2)}) collective-permute-start(bf16[272,256]{1,0:T(8,128)(2,1)S(1)} %get-tuple-element.39), channel_id=1, source_target_pairs={{0,2},{1,3},{2,0},{3,1},{4,6},{5,7},{6,4},{7,5},{8,10},{9,11},{10,... | collective-permute-start | bytes 417800 | tf_op jit(solution)/shard_map/ppermute | solution.py:289
  51.3 8.1 %collective-permute-start.7 = (bf16[272,256]{1,0:T(8,128)(2,1)S(1)}, bf16[272,256]{1,0:T(8,128)(2,1)S(1)}, u32[]{:S(2)}, u32[]{:S(2)}) collective-permute-start(bf16[272,256]{1,0:T(8,128)(2,1)S(1)} %get-tuple-element.40), channel_id=1, source_target_pairs={{0,3},{1,2},{2,1},{3,0},{4,7},{5,6},{6,5},{7,4},{8,11},{9,10},{10,... | collective-permute-start | bytes 417800 | tf_op jit(solution)/shard_map/ppermute | solution.py:289
  55.4 18.0 %all-to-all-start.1 = ((bf16[32,8,1920]{2,1,0:T(8,128)(2,1)}), bf16[32,8,1920]{2,1,0:T(8,128)(2,1)S(1)}, u32[]{:S(2)}, u32[]{:S(2)}) async-start(bf16[32,8,1920]{2,1,0:T(8,128)(2,1)} %bitcast.8), calls=%async_computation.1 | async-start | bytes 1966080 | tf_op jit(solution)/shard_map/all_to_all | solution.py:342
  60.1 1.3 %collective-permute-start.8 = (bf16[224,256]{1,0:T(8,128)(2,1)S(1)}, bf16[224,256]{1,0:T(8,128)(2,1)S(1)}, u32[]{:S(2)}, u32[]{:S(2)}) collective-permute-start(bf16[224,256]{1,0:T(8,128)(2,1)S(1)} %get-tuple-element.44), channel_id=1, source_target_pairs={{0,32},{32,0},{64,96},{96,64},{1,33},{33,1},{65,97},{97,65},{2,34}... | collective-permute-start | bytes 344072 | tf_op jit(solution)/shard_map/ppermute | solution.py:353
  61.4 9.9 %collective-permute-start.9 = (bf16[224,256]{1,0:T(8,128)(2,1)S(1)}, bf16[224,256]{1,0:T(8,128)(2,1)S(1)}, u32[]{:S(2)}, u32[]{:S(2)}) collective-permute-start(bf16[224,256]{1,0:T(8,128)(2,1)S(1)} %add_convert_fusion), channel_id=1, source_target_pairs={{0,64},{32,96},{64,0},{96,32},{1,65},{33,97},{65,1},{97,33},{2,66}... | collective-permute-start | bytes 344072 | tf_op jit(solution)/shard_map/ppermute | solution.py:353

commit v4 on v3

--- a/solution.py
+++ b/solution.py
@@ -42,30 +42,19 @@
     return (col + kw >= 0) & (col + kw < W)
 
 
-def pack_kernel(planes, at_ref, x_any, cot_any, w_any, bias_ref, chunks_ref, *refs):
-    packs, (x_ref, cot_ref, w_ref, sems) = refs[:RING], refs[RING:]
+def pack_kernel(planes, x_any, cot_any, w_any, bias_any, chunks, *refs):
+    packs, (x_ref, cot_ref, w_ref, bias_ref, in_sems) = refs[:RING], refs[RING:]
     copies = [
-        pltpu.make_async_copy(src, dst, sems.at[i])
-        for i, (src, dst) in enumerate(((w_any, w_ref), (cot_any, cot_ref), (x_any, x_ref)))
+        pltpu.make_async_copy(src, dst, in_sems.at[i])
+        for i, (src, dst) in enumerate(((w_any, w_ref), (x_any, x_ref), (cot_any, cot_ref), (bias_any, bias_ref)))
     ]
     for copy in copies:
         copy.start()
-    bias = jnp.broadcast_to(bias_ref[...].astype(F32), (16, BLOCK))
-    bias = jnp.concatenate([bias, jnp.zeros((16, WIDE - BLOCK), F32)], 1).astype(BF16)
     copies[0].wait()
     w = jnp.concatenate([w_ref[...].astype(F32), jnp.zeros((BLOCK, WIDE), F32)], 0).astype(BF16)
-    for pack in packs:
-        pack[0:TAP_ROWS, :] = w
+    for m in range(RING):
+        packs[m][0:TAP_ROWS, :] = w
     copies[1].wait()
-    for m, pack in enumerate(packs):
-        chunk = jnp.bitwise_xor(at_ref[0], m)
-        for d in range(planes):
-            lanes = pl.ds(pl.multiple_of(chunk * INNER + d * PLANE, INNER), INNER)
-            start = TAP_ROWS + 16 * d
-            pack[start : start + 16, :] = fold(cot_ref[:, lanes].astype(F32)).astype(BF16)
-        start = TAP_ROWS + 16 * planes
-        pack[start : start + 16, :] = bias
-    copies[2].wait()
     lane = lax.broadcasted_iota(jnp.int32, (BLOCK, 2 * W), 1)
     for v in range(RING):
         for d in range(planes):
@@ -77,10 +66,22 @@
             if v > 0:
                 above = x_ref[:, base - 2 * W : base].astype(F32)
                 halo = jnp.where(lane < W, halo, above)
-            own = x_ref[:, base : base + INNER]
-            for g in range(chunks_ref.shape[0] // RING):
-                chunks_ref[g * RING + v, :, d * OUTER : d * OUTER + INNER] = own
-                chunks_ref[g * RING + v, :, d * OUTER + INNER : (d + 1) * OUTER] = halo.astype(BF16)
+            own, halo = x_ref[:, base : base + INNER], halo.astype(BF16)
+            for g in range(chunks.shape[0] // RING):
+                chunks[g * RING + v, :, d * OUTER : d * OUTER + INNER] = own
+                chunks[g * RING + v, :, d * OUTER + INNER : (d + 1) * OUTER] = halo
+    copies[2].wait()
+    copies[3].wait()
+    bias = jnp.broadcast_to(bias_ref[...].astype(F32), (16, BLOCK))
+    bias = jnp.concatenate([bias, jnp.zeros((16, WIDE - BLOCK), F32)], 1).astype(BF16)
+    for m in range(RING):
+        chunk = jnp.bitwise_xor(jnp.bitwise_and(lax.axis_index("filt"), RING - 1), m)
+        for d in range(planes):
+            lanes = pl.ds(pl.multiple_of(chunk * INNER + d * PLANE, INNER), INNER)
+            start = TAP_ROWS + 16 * d
+            packs[m][start : start + 16, :] = fold(cot_ref[:, lanes].astype(F32)).astype(BF16)
+        start = TAP_ROWS + 16 * planes
+        packs[m][start : start + 16, :] = bias
 
 
 def prepare_kernel(planes, *refs):
@@ -103,9 +104,11 @@
 
 
 def forward_kernel(
-    planes, x_ref, w_ref, cot_ref, own_ref, low_ref, high_ref, up_ref, down_ref, maps
+    planes, x_ref, w_ref, cot_ref, own_ref, low_ref, high_ref, up_ref, down_ref, *maps
 ):
-    maps[...] = jnp.dot(w_ref[...], x_ref[...], preferred_element_type=F32)
+    for m in range(RING):
+        w = w_ref[m * TAP_ROWS : (m + 1) * TAP_ROWS, :]
+        maps[m][...] = jnp.dot(w, x_ref[...], preferred_element_type=F32)
     masks = {kw: inside_row(BLOCK, kw) for kw in (-1, 1)}
     for out in range(-1, planes + 1):
         pieces = []
@@ -117,9 +120,9 @@
                     term = None
                     for kd in (-1, 0, 1):
                         if 0 <= out + kd < planes:
-                            at = m * TAP_ROWS + TAPS.index((kd, kh, kw)) * BLOCK
+                            at = TAPS.index((kd, kh, kw)) * BLOCK
                             d = out + kd
-                            part = maps[at : at + BLOCK, d * OUTER : (d + 1) * OUTER]
+                            part = maps[m][at : at + BLOCK, d * OUTER : (d + 1) * OUTER]
                             term = part if term is None else term + part
                     if kw:
                         term = jnp.where(masks[kw], moved(term, -kw), 0.0)
@@ -147,12 +150,12 @@
 def backward_kernel(
     planes, x_ref, own_ref, low_ref, high_ref, before_ref, after_ref, cot_ref, bias_ref, *refs
 ):
-    shifted, backs, bank = refs[0], refs[1 : RING + 1], refs[RING + 1]
+    turned_ref, part_any, backs = refs[0], refs[1], refs[2 : RING + 2]
+    bank, (shifted, part, sems) = refs[RING + 2 : 2 * RING + 2], refs[2 * RING + 2 :]
     bias = bias_ref[:, 0:1]
     masks = {kw: inside_row(BLOCK, kw) for kw in (-1, 1)}
     for m in range(RING):
-        end = (m + 1) * TAP_ROWS
-        bank[end - BLOCK : end, :] = jnp.zeros((BLOCK, planes * OUTER), F32)
+        bank[m][TAP_ROWS - BLOCK : TAP_ROWS, :] = jnp.zeros((BLOCK, planes * OUTER), F32)
     for src in range(-1, planes + 1):
         if src < 0:
             pre = before_ref[:, INNER : 2 * INNER].astype(F32) + low_ref[...]
@@ -188,28 +191,33 @@
                     for kd in (-1, 0, 1):
                         d = src + kd
                         if 0 <= d < planes:
-                            at = m * TAP_ROWS + TAPS.index((kd, kh, kw)) * BLOCK
-                            bank[at : at + BLOCK, d * OUTER : (d + 1) * OUTER] = term
-    shifted[...] = bank[...].astype(BF16)
-    filt = lax.dot_general(
-        shifted[...], x_ref[...], (((1,), (1,)), ((), ())), preferred_element_type=F32
-    )
-    for m in range(RING):
-        backs[m][0:TAP_ROWS, :] = filt[m * TAP_ROWS : (m + 1) * TAP_ROWS].astype(BF16)
-
-
-def input_kernel(turned_ref, shifted, part_ref):
-    part = jnp.dot(turned_ref[...], shifted[...], preferred_element_type=F32)
-    part_ref[...] = part.astype(BF16)
-
-
-def unpack_kernel(planes, at_ref, *refs):
+                            at = TAPS.index((kd, kh, kw)) * BLOCK
+                            bank[m][at : at + BLOCK, d * OUTER : (d + 1) * OUTER] = term
+    for m in range(RING):
+        rows = slice(m * TAP_ROWS, (m + 1) * TAP_ROWS)
+        shifted[rows, :] = bank[m][...].astype(BF16)
+        filt = lax.dot_general(
+            shifted[rows, :], x_ref[...], (((1,), (1,)), ((), ())), preferred_element_type=F32
+        )
+        backs[m][0:TAP_ROWS, :] = filt.astype(BF16)
+    copies = []
+    for d in range(planes):
+        lanes = slice(d * OUTER, (d + 1) * OUTER)
+        total = jnp.dot(turned_ref[...], shifted[:, lanes], preferred_element_type=F32)
+        part[:, lanes] = total.astype(BF16)
+        copies.append(pltpu.make_async_copy(part.at[:, lanes], part_any.at[:, lanes], sems.at[d]))
+        copies[-1].start()
+    for copy in copies:
+        copy.wait()
+
+
+def unpack_kernel(planes, *refs):
     backs, (filt_ref, act_ref) = refs[:RING], refs[RING:]
     total = None
     for m, back in enumerate(backs):
         part = back[0:TAP_ROWS, :].astype(F32)
         total = part if total is None else total + part
-        chunk = jnp.bitwise_xor(at_ref[0], m)
+        chunk = jnp.bitwise_xor(jnp.bitwise_and(lax.axis_index("filt"), RING - 1), m)
         for d in range(planes):
             lanes = pl.ds(pl.multiple_of(chunk * INNER + d * PLANE, INNER), INNER)
             start = TAP_ROWS + 16 * d
@@ -217,7 +225,10 @@
     filt_ref[...] = total.astype(BF16)
 
 
-def collect_kernel(planes, got_ref, out_ref):
+def collect_kernel(planes, scale, got_ref, filt_ref, other_ref, out_ref, weight_ref):
+    rows = weight_ref.shape[0]
+    filt = filt_ref[...].astype(F32) + other_ref[...].astype(F32)
+    weight_ref[...] = (filt * scale)[:rows]
     lane = lax.broadcasted_iota(jnp.int32, (BLOCK, 2 * W), 1)
     for d in range(planes):
         sums = []
@@ -238,7 +249,7 @@
             out_ref[:, base : base + INNER] = whole.astype(BF16)
 
 
-def call(kernel, ins, outs, scratch, flops, moved_bytes, name, hbm=(), limit=48):
+def call(kernel, ins, outs, scratch, flops, moved_bytes, name, hbm=(), outs_hbm=(), limit=48):
     smem = pl.BlockSpec(memory_space=pltpu.SMEM)
     vmem = pl.BlockSpec(memory_space=pltpu.VMEM)
     anywhere = pl.BlockSpec(memory_space=pl.ANY)
@@ -247,7 +258,7 @@
         kernel,
         out_shape=shapes,
         in_specs=[smem if x.dtype == jnp.int32 else anywhere if i in hbm else vmem for i, x in enumerate(ins)],
-        out_specs=tuple(vmem for _ in outs),
+        out_specs=tuple(anywhere if i in outs_hbm else vmem for i in range(len(outs))),
         scratch_shapes=scratch,
         compiler_params=pltpu.CompilerParams(vmem_limit_bytes=limit * 2**20),
         cost_estimate=pl.CostEstimate(flops=flops, bytes_accessed=moved_bytes, transcendentals=0),
@@ -264,23 +275,24 @@
     outer = planes * OUTER
     inner = planes * INNER
     group = RING * BLOCK
-    at = jnp.bitwise_and(lax.axis_index("filt"), RING - 1).astype(jnp.int32).reshape(1)
     w = jnp.transpose(weight, (1, 0, 2)).reshape(len(TAPS) * block, channels)
     pack = ((TAP_ROWS + 16 * planes + 16, WIDE), BF16)
     chunks, *packs = call(
         functools.partial(pack_kernel, planes),
-        (at, features.reshape(block, voxels), cotangent.reshape(block, voxels), w, bias_vec[None]),
+        (features.reshape(block, voxels), cotangent.reshape(block, voxels), w, bias_vec[None]),
         [((parts, block, outer), BF16)] + [pack] * RING,
         [
             pltpu.VMEM((block, voxels), BF16),
             pltpu.VMEM((block, voxels), BF16),
             pltpu.VMEM((len(TAPS) * block, channels), BF16),
-            pltpu.SemaphoreType.DMA((3,)),
+            pltpu.VMEM((1, block), BF16),
+            pltpu.SemaphoreType.DMA((4,)),
         ],
         0,
         2 * parts * block * outer,
         "pack",
-        (1, 2, 3),
+        (0, 1, 2, 3),
+        (),
         61,
     )
 
@@ -312,7 +324,7 @@
         functools.partial(forward_kernel, planes),
         (x, w, cot),
         [((group, inner), F32), plane, plane, edge, edge],
-        [pltpu.VMEM((RING * TAP_ROWS, outer), F32)],
+        [pltpu.VMEM((TAP_ROWS, outer), F32)] * RING,
         flops,
         2 * channels * outer,
         "conv_forward",
@@ -320,49 +332,47 @@
     before = lax.ppermute(up, "space", [(i, i + 1) for i in range(slabs - 1)])
     after = lax.ppermute(down, "space", [(i + 1, i) for i in range(slabs - 1)])
     back = ((TAP_ROWS + 16 * planes, WIDE), BF16)
-    shifted, *backs = call(
+    part, *backs = call(
         functools.partial(backward_kernel, planes),
-        (x, own, low, high, before, after, cot, bias),
-        [((RING * TAP_ROWS, outer), BF16)] + [back] * RING,
-        [pltpu.VMEM((RING * TAP_ROWS, outer), F32)],
-        flops,
+        (x, own, low, high, before, after, cot, bias, turned),
+        [((channels, outer), BF16)] + [back] * RING,
+        [pltpu.VMEM((TAP_ROWS, outer), F32)] * RING
+        + [
+            pltpu.VMEM((RING * TAP_ROWS, outer), BF16),
+            pltpu.VMEM((channels, outer), BF16),
+            pltpu.SemaphoreType.DMA((planes,)),
+        ],
+        2 * flops,
         4 * channels * outer,
-        "filter_gradient",
+        "conv_backward",
+        (),
+        (0,),
     )
     backs = to_ring(backs)
-    (part,) = call(
-        input_kernel,
-        (turned, shifted),
-        [((channels, outer), BF16)],
-        [],
-        flops,
-        4 * channels * outer,
-        "input_gradient",
-    )
     got = lax.all_to_all(part.reshape(parts, block, outer), "filt", 0, 0, tiled=True)
     filt, activation = call(
         functools.partial(unpack_kernel, planes),
-        (at, *backs),
+        (*backs,),
         [((TAP_ROWS, WIDE), BF16), ((block, voxels), BF16)],
         [],
         UNPACK,
         RING * TAP_ROWS * WIDE * 2,
         "unpack",
     )
-    for m in (1, 2):
-        other = lax.ppermute(filt, "space", [(i, i ^ m) for i in range(slabs)])
-        filt = filt.astype(F32) + other.astype(F32)
-        filt = filt.astype(BF16) if m == 1 else filt * (1.0 / math.sqrt(planes * slabs * PLANE))
-    weight_grad = filt[: len(TAPS) * block].reshape(len(TAPS), block, channels)
-    (input_grad,) = call(
-        functools.partial(collect_kernel, planes),
-        (got,),
-        [((block, voxels), BF16)],
+    by = lambda m: [(i, i ^ m) for i in range(slabs)]
+    other = lax.ppermute(filt, "space", by(1))
+    filt = (filt.astype(F32) + other.astype(F32)).astype(BF16)
+    other = lax.ppermute(filt, "space", by(2))
+    input_grad, weight_grad = call(
+        functools.partial(collect_kernel, planes, 1.0 / math.sqrt(planes * slabs * PLANE)),
+        (got, filt, other),
+        [((block, voxels), BF16), ((len(TAPS) * block, channels), F32)],
         [],
         0,
         2 * channels * outer,
         "collect",
     )
+    weight_grad = weight_grad.reshape(len(TAPS), block, channels)
     shape = features.shape
     return (
         activation.reshape(shape),

time: 74.6 us -> 73.8 us (0.989)
  starting transfers between devices: 31.8 us -> 35.8 us
  waiting for transfers between devices: 30.2 us -> 28 us
  Pallas kernels: 9.77 us -> 8.79 us
  local copies, waits for them, and re-layouts: 0.91 us -> 0.01 us
    ppermute x2, starting transfers between devices: 0.75 us -> 4.65 us  [the longest x1 4.65 us: per_device(): other = lax.ppermute(filt, 'space', by(2))]
    ppermute x2, waiting for transfers between devices: 10.5 us -> 6.89 us  [the longest x1 5.57 us: per_device(): other = lax.ppermute(filt, 'space', by(2))]
    all_to_all x1, waiting for transfers between devices: 12.5 us -> 13.6 us  [per_device(): lax.all_to_all(chunks, 'filt', 0, 0, tiled=True).reshape(channels, outer)]
    pallas_call x7 -> x6, Pallas kernels: 9.77 us -> 8.79 us  [call(): pl.pallas_call(kernel, out_shape=shapes, in_specs=[smem if x.dtype == jnp...]
    unnamed x2, local copies, waits for them, and re-layouts: 0.91 us -> 0.01 us
  transfers between devices with their start and end apart: 12 -> 12, of which waited for: 6 -> 6; matrix products, arithmetic and copies ran while one was open for 1% -> 0% of each run, Pallas kernels for 4% -> 1%
where the time goes in v4:
time: 73.8 us; the launch traced here: 73.4 us
  starting transfers between devices  35.8 us (49%)
  waiting for transfers between devices  28 us (38%)
  Pallas kernels  8.79 us (12%)
  between operations  0.75 us (1%)
    all_to_all x1, waiting for transfers between devices, per_device(): lax.all_to_all(chunks, 'filt', 0, 0, tiled=True).reshape(channels, outer)  13.6 us
    all_to_all x1, starting transfers between devices, per_device(): lax.all_to_all(chunks, 'filt', 0, 0, tiled=True).reshape(channels, outer)  8.92 us
    pallas_call x6, Pallas kernels, call(): pl.pallas_call(kernel, out_shape=shapes, in_specs=[smem if x.dtype == jnp...  8.79 us
    ppermute x6, starting transfers between devices, to_ring(): lax.ppermute(values[m], 'filt', swap(m))  8.54 us
    ppermute x1, starting transfers between devices, per_device(): before = lax.ppermute(up, 'space', [(i, i + 1) for i in range(slabs - 1)])  7.86 us
    ppermute x1, waiting for transfers between devices, per_device(): other = lax.ppermute(filt, 'space', by(2))  5.57 us
    ppermute x1, waiting for transfers between devices, per_device(): after = lax.ppermute(down, 'space', [(i + 1, i) for i in range(slabs - 1)])  5.5 us
    ppermute x1, starting transfers between devices, per_device(): other = lax.ppermute(filt, 'space', by(2))  4.65 us
  transfers between devices with their start and end apart: 12, of which 6 were waited for; matrix products, arithmetic and copies ran while one was open for 0% of the time, Pallas kernels for 1%

profile of v4, /device:TPU:1, one launch (start us, length us, event | category | flops | bytes accessed | tf_op | source)
XLA Modules:
  0.0 73.4 jit_solution(15618686317202611689)
XLA Ops:
  0.6 2.2 %pack.1 = (bf16[32,8,1920]{2,1,0:T(8,128)(2,1)}, bf16[288,256]{1,0:T(8,128)(2,1)}, bf16[288,256]{1,0:T(8,128)(2,1)}, bf16[288,256]{1,0:T(8,128)(2,1)}, bf16[288,256]{1,0:T(8,128)(2,1)}) custom-call(bf16[8,6144]{1,0:T(8,128)(2,1)} %bitcast.16, bf16[8,6144]{1,0:T(8,128)(2,1)} %bitcast.17, bf16[216,256]{1,0:T(8,128)(2,1)} %bitcast.15, bf16[1,8]{1,0:T(2,128)(2,1)} %bitcast.18), custom_call_target="tpu_custom_call" | custom-call | bytes 983040 | tf_op jit(solution)/shard_map/pack/pallas_call | solution.py:257
  2.8 2.1 %collective-permute-start = (bf16[288,256]{1,0:T(8,128)(2,1)}, bf16[288,256]{1,0:T(8,128)(2,1)S(1)}, u32[]{:S(2)}, u32[]{:S(2)}) collective-permute-start(bf16[288,256]{1,0:T(8,128)(2,1)} %get-tuple-element.28), channel_id=1, source_target_pairs={{0,1},{1,0},{2,3},{3,2},{4,5},{5,4},{6,7},{7,6},{8,9},{9,8},{10,11... | collective-permute-start | bytes 442376 | tf_op jit(solution)/shard_map/ppermute | solution.py:301
  5.0 2.5 %collective-permute-start.1 = (bf16[288,256]{1,0:T(8,128)(2,1)}, bf16[288,256]{1,0:T(8,128)(2,1)S(1)}, u32[]{:S(2)}, u32[]{:S(2)}) collective-permute-start(bf16[288,256]{1,0:T(8,128)(2,1)} %get-tuple-element.29), channel_id=1, source_target_pairs={{0,2},{1,3},{2,0},{3,1},{4,6},{5,7},{6,4},{7,5},{8,10},{9,11},{10,... | collective-permute-start | bytes 442376 | tf_op jit(solution)/shard_map/ppermute | solution.py:301
  7.4 0.0 collective-permute-start.2
  7.4 8.9 %all-to-all-start = ((bf16[32,8,1920]{2,1,0:T(8,128)(2,1)}), bf16[32,8,1920]{2,1,0:T(8,128)(2,1)S(1)}, u32[]{:S(2)}, u32[]{:S(2)}) async-start(bf16[32,8,1920]{2,1,0:T(8,128)(2,1)} %get-tuple-element.26), calls=%async_computation | async-start | bytes 1966080 | tf_op jit(solution)/shard_map/all_to_all | solution.py:304
  16.4 0.0 collective-permute-done.refs_1_
  16.4 0.2 collective-permute-done.2.refs_3_
  16.6 0.2 prepare.1
  16.8 13.6 %all-to-all-done = bf16[32,8,1920]{2,1,0:T(8,128)(2,1)S(1)} async-done(((bf16[32,8,1920]{2,1,0:T(8,128)(2,1)}), bf16[32,8,1920]{2,1,0:T(8,128)(2,1)S(1)}, u32[]{:S(2)}, u32[]{:S(2)}) %all-to-all-start) | async-done | bytes 983072 | tf_op jit(solution)/shard_map/all_to_all | solution.py:304
  30.4 1.3 %conv_forward.1 = (f32[32,1536]{1,0:T(8,128)S(1)}, f32[32,512]{1,0:T(8,128)S(1)}, f32[32,512]{1,0:T(8,128)S(1)}, bf16[32,1536]{1,0:T(8,128)(2,1)S(1)}, bf16[32,1536]{1,0:T(8,128)(2,1)S(1)}) custom-call(bf16[256,1920]{1,0:T(8,128)(2,1)S(1)} %bitcast.13, bf16[896,256]{1,0:T(8,128)(2,1)S(1)} %get-tuple-element.31.w_ref, f32[32,1536]{1,0:T(8,128)S(1)} %get-tuple-element.32.cot_ref), custom_call_target="tpu_custom_call" | custom-call | flops 880803840 | bytes 983040 | tf_op jit(solution)/shard_map/conv_forward/pallas_call | solution.py:257
  31.7 7.9 %collective-permute-start.3 = (bf16[32,1536]{1,0:T(8,128)(2,1)S(1)}, bf16[32,1536]{1,0:T(8,128)(2,1)S(1)}, u32[]{:S(2)}, u32[]{:S(2)}) collective-permute-start(bf16[32,1536]{1,0:T(8,128)(2,1)S(1)} %get-tuple-element.36), channel_id=1, source_target_pairs={{0,32},{32,64},{64,96},{1,33},{33,65},{65,97},{2,34},{34,66},{66,9... | collective-permute-start | bytes 294920 | tf_op jit(solution)/shard_map/ppermute | solution.py:332
  39.6 1.9 %collective-permute-start.4 = (bf16[32,1536]{1,0:T(8,128)(2,1)S(1)}, bf16[32,1536]{1,0:T(8,128)(2,1)S(1)}, u32[]{:S(2)}, u32[]{:S(2)}) collective-permute-start(bf16[32,1536]{1,0:T(8,128)(2,1)S(1)} %get-tuple-element.37), channel_id=1, source_target_pairs={{32,0},{64,32},{96,64},{33,1},{65,33},{97,65},{34,2},{66,34},{98,6... | collective-permute-start | bytes 294920 | tf_op jit(solution)/shard_map/ppermute | solution.py:333
  41.5 5.5 %collective-permute-done.4.after_ref = bf16[32,1536]{1,0:T(8,128)(2,1)S(1)} collective-permute-done((bf16[32,1536]{1,0:T(8,128)(2,1)S(1)}, bf16[32,1536]{1,0:T(8,128)(2,1)S(1)}, u32[]{:S(2)}, u32[]{:S(2)}) %collective-permute-start.4) | collective-permute-done | bytes 98336 | tf_op jit(solution)/shard_map/ppermute | solution.py:333
  47.0 3.6 %conv_backward.1 = (bf16[256,1920]{1,0:T(8,128)(2,1)}, bf16[272,256]{1,0:T(8,128)(2,1)S(1)}, bf16[272,256]{1,0:T(8,128)(2,1)S(1)}, bf16[272,256]{1,0:T(8,128)(2,1)S(1)}, bf16[272,256]{1,0:T(8,128)(2,1)S(1)}) custom-call(bf16[256,1920]{1,0:T(8,128)(2,1)S(1)} %bitcast.14, f32[32,1536]{1,0:T(8,128)S(1)} %get-tuple-element.33.own_ref, ...), custom_call_target="tpu_custom_call" | custom-call | flops 1761607680 | bytes 1966080 | tf_op jit(solution)/shard_map/conv_backward/pallas_call | solution.py:257
  50.6 0.2 collective-permute-start.5
  50.8 1.8 %collective-permute-start.6 = (bf16[272,256]{1,0:T(8,128)(2,1)S(1)}, bf16[272,256]{1,0:T(8,128)(2,1)S(1)}, u32[]{:S(2)}, u32[]{:S(2)}) collective-permute-start(bf16[272,256]{1,0:T(8,128)(2,1)S(1)} %get-tuple-element.42), channel_id=1, source_target_pairs={{0,2},{1,3},{2,0},{3,1},{4,6},{5,7},{6,4},{7,5},{8,10},{9,11},{10,... | collective-permute-start | bytes 417800 | tf_op jit(solution)/shard_map/ppermute | solution.py:301
  52.6 2.0 %collective-permute-start.7 = (bf16[272,256]{1,0:T(8,128)(2,1)S(1)}, bf16[272,256]{1,0:T(8,128)(2,1)S(1)}, u32[]{:S(2)}, u32[]{:S(2)}) collective-permute-start(bf16[272,256]{1,0:T(8,128)(2,1)S(1)} %get-tuple-element.43), channel_id=1, source_target_pairs={{0,3},{1,2},{2,1},{3,0},{4,7},{5,6},{6,5},{7,4},{8,11},{9,10},{10,... | collective-permute-start | bytes 417800 | tf_op jit(solution)/shard_map/ppermute | solution.py:301
  54.5 3.9 %all-to-all-start.1 = ((bf16[32,8,1920]{2,1,0:T(8,128)(2,1)}), bf16[32,8,1920]{2,1,0:T(8,128)(2,1)S(1)}, u32[]{:S(2)}, u32[]{:S(2)}) async-start(bf16[32,8,1920]{2,1,0:T(8,128)(2,1)} %bitcast.7), calls=%async_computation.1 | async-start | bytes 1966080 | tf_op jit(solution)/shard_map/all_to_all | solution.py:352
  58.5 0.7 unpack.1
  59.2 1.3 %collective-permute-done.8 = bf16[224,256]{1,0:T(8,128)(2,1)S(1)} collective-permute-done((bf16[224,256]{1,0:T(8,128)(2,1)S(1)}, bf16[224,256]{1,0:T(8,128)(2,1)S(1)}, u32[]{:S(2)}, u32[]{:S(2)}) %collective-permute-start.8) | collective-permute-done | bytes 114720 | tf_op jit(solution)/shard_map/ppermute | solution.py:363
  60.5 4.7 %collective-permute-start.9 = (bf16[224,256]{1,0:T(8,128)(2,1)S(1)}, bf16[224,256]{1,0:T(8,128)(2,1)S(1)}, u32[]{:S(2)}, u32[]{:S(2)}) collective-permute-start(bf16[224,256]{1,0:T(8,128)(2,1)S(1)} %add_convert_fusion.filt_ref), channel_id=1, source_target_pairs={{0,64},{32,96},{64,0},{96,32},{1,65},{33,97},{65,1},{97,33},{2,66}... | collective-permute-start | bytes 344072 | tf_op jit(solution)/shard_map/ppermute | solution.py:365
  65.2 5.6 %collective-permute-done.9.other_ref = bf16[224,256]{1,0:T(8,128)(2,1)S(1)} collective-permute-done((bf16[224,256]{1,0:T(8,128)(2,1)S(1)}, bf16[224,256]{1,0:T(8,128)(2,1)S(1)}, u32[]{:S(2)}, u32[]{:S(2)}) %collective-permute-start.9) | collective-permute-done | bytes 114720 | tf_op jit(solution)/shard_map/ppermute | solution.py:365
  70.8 1.8 %all-to-all-done.1.got_ref = bf16[32,8,1920]{2,1,0:T(8,128)(2,1)S(1)} async-done(((bf16[32,8,1920]{2,1,0:T(8,128)(2,1)}), bf16[32,8,1920]{2,1,0:T(8,128)(2,1)S(1)}, u32[]{:S(2)}, u32[]{:S(2)}) %all-to-all-start.1) | async-done | bytes 983072 | tf_op jit(solution)/shard_map/all_to_all | solution.py:352
  72.6 0.8 %collect.1 = (bf16[8,6144]{1,0:T(8,128)(2,1)}, f32[216,256]{1,0:T(8,128)}) custom-call(bf16[32,8,1920]{2,1,0:T(8,128)(2,1)S(1)} %all-to-all-done.1.got_ref, bf16[224,256]{1,0:T(8,128)(2,1)S(1)} %add_convert_fusion.filt_ref, bf16[224,256]{1,0:T(8,128)(2,1)S(1)} %collective-permute-done.9.other_ref), custom_call_target="tpu_custom_call" | custom-call | bytes 983040 | tf_op jit(solution)/shard_map/collect/pallas_call | solution.py:257
  (9 shorter events, 0.0 us)
Async XLA Ops:
  2.8 13.5 %collective-permute-start = (bf16[288,256]{1,0:T(8,128)(2,1)}, bf16[288,256]{1,0:T(8,128)(2,1)S(1)}, u32[]{:S(2)}, u32[]{:S(2)}) collective-permute-start(bf16[288,256]{1,0:T(8,128)(2,1)} %get-tuple-element.28), channel_id=1, source_target_pairs={{0,1},{1,0},{2,3},{3,2},{4,5},{5,4},{6,7},{7,6},{8,9},{9,8},{10,11... | collective-permute-start | bytes 442376 | tf_op jit(solution)/shard_map/ppermute | solution.py:301
  5.0 11.4 %collective-permute-start.1 = (bf16[288,256]{1,0:T(8,128)(2,1)}, bf16[288,256]{1,0:T(8,128)(2,1)S(1)}, u32[]{:S(2)}, u32[]{:S(2)}) collective-permute-start(bf16[288,256]{1,0:T(8,128)(2,1)} %get-tuple-element.29), channel_id=1, source_target_pairs={{0,2},{1,3},{2,0},{3,1},{4,6},{5,7},{6,4},{7,5},{8,10},{9,11},{10,... | collective-permute-start | bytes 442376 | tf_op jit(solution)/shard_map/ppermute | solution.py:301
  7.4 9.2 %collective-permute-start.2 = (bf16[288,256]{1,0:T(8,128)(2,1)}, bf16[288,256]{1,0:T(8,128)(2,1)S(1)}, u32[]{:S(2)}, u32[]{:S(2)}) collective-permute-start(bf16[288,256]{1,0:T(8,128)(2,1)} %get-tuple-element.30), channel_id=1, source_target_pairs={{0,3},{1,2},{2,1},{3,0},{4,7},{5,6},{6,5},{7,4},{8,11},{9,10},{10,... | collective-permute-start | bytes 442376 | tf_op jit(solution)/shard_map/ppermute | solution.py:301
  7.4 9.1 %copy-start = (bf16[288,256]{1,0:T(8,128)(2,1)S(1)}, bf16[288,256]{1,0:T(8,128)(2,1)}, u32[]{:S(2)}) copy-start(bf16[288,256]{1,0:T(8,128)(2,1)} %get-tuple-element.27.refs_0_) | copy-start | bytes 442372
  7.4 22.9 %all-to-all-start = ((bf16[32,8,1920]{2,1,0:T(8,128)(2,1)}), bf16[32,8,1920]{2,1,0:T(8,128)(2,1)S(1)}, u32[]{:S(2)}, u32[]{:S(2)}) async-start(bf16[32,8,1920]{2,1,0:T(8,128)(2,1)} %get-tuple-element.26), calls=%async_computation | async-start | bytes 1966080 | tf_op jit(solution)/shard_map/all_to_all | solution.py:304
  31.7 9.8 %collective-permute-start.3 = (bf16[32,1536]{1,0:T(8,128)(2,1)S(1)}, bf16[32,1536]{1,0:T(8,128)(2,1)S(1)}, u32[]{:S(2)}, u32[]{:S(2)}) collective-permute-start(bf16[32,1536]{1,0:T(8,128)(2,1)S(1)} %get-tuple-element.36), channel_id=1, source_target_pairs={{0,32},{32,64},{64,96},{1,33},{33,65},{65,97},{2,34},{34,66},{66,9... | collective-permute-start | bytes 294920 | tf_op jit(solution)/shard_map/ppermute | solution.py:332
  39.6 7.4 %collective-permute-start.4 = (bf16[32,1536]{1,0:T(8,128)(2,1)S(1)}, bf16[32,1536]{1,0:T(8,128)(2,1)S(1)}, u32[]{:S(2)}, u32[]{:S(2)}) collective-permute-start(bf16[32,1536]{1,0:T(8,128)(2,1)S(1)} %get-tuple-element.37), channel_id=1, source_target_pairs={{32,0},{64,32},{96,64},{33,1},{65,33},{97,65},{34,2},{66,34},{98,6... | collective-permute-start | bytes 294920 | tf_op jit(solution)/shard_map/ppermute | solution.py:333
  50.6 7.9 %collective-permute-start.5 = (bf16[272,256]{1,0:T(8,128)(2,1)S(1)}, bf16[272,256]{1,0:T(8,128)(2,1)S(1)}, u32[]{:S(2)}, u32[]{:S(2)}) collective-permute-start(bf16[272,256]{1,0:T(8,128)(2,1)S(1)} %get-tuple-element.41), channel_id=1, source_target_pairs={{0,1},{1,0},{2,3},{3,2},{4,5},{5,4},{6,7},{7,6},{8,9},{9,8},{10,11... | collective-permute-start | bytes 417800 | tf_op jit(solution)/shard_map/ppermute | solution.py:301
  50.8 7.7 %collective-permute-start.6 = (bf16[272,256]{1,0:T(8,128)(2,1)S(1)}, bf16[272,256]{1,0:T(8,128)(2,1)S(1)}, u32[]{:S(2)}, u32[]{:S(2)}) collective-permute-start(bf16[272,256]{1,0:T(8,128)(2,1)S(1)} %get-tuple-element.42), channel_id=1, source_target_pairs={{0,2},{1,3},{2,0},{3,1},{4,6},{5,7},{6,4},{7,5},{8,10},{9,11},{10,... | collective-permute-start | bytes 417800 | tf_op jit(solution)/shard_map/ppermute | solution.py:301
  52.6 5.9 %collective-permute-start.7 = (bf16[272,256]{1,0:T(8,128)(2,1)S(1)}, bf16[272,256]{1,0:T(8,128)(2,1)S(1)}, u32[]{:S(2)}, u32[]{:S(2)}) collective-permute-start(bf16[272,256]{1,0:T(8,128)(2,1)S(1)} %get-tuple-element.43), channel_id=1, source_target_pairs={{0,3},{1,2},{2,1},{3,0},{4,7},{5,6},{6,5},{7,4},{8,11},{9,10},{10,... | collective-permute-start | bytes 417800 | tf_op jit(solution)/shard_map/ppermute | solution.py:301
  54.5 18.0 %all-to-all-start.1 = ((bf16[32,8,1920]{2,1,0:T(8,128)(2,1)}), bf16[32,8,1920]{2,1,0:T(8,128)(2,1)S(1)}, u32[]{:S(2)}, u32[]{:S(2)}) async-start(bf16[32,8,1920]{2,1,0:T(8,128)(2,1)} %bitcast.7), calls=%async_computation.1 | async-start | bytes 1966080 | tf_op jit(solution)/shard_map/all_to_all | solution.py:352
  59.2 1.3 %collective-permute-start.8 = (bf16[224,256]{1,0:T(8,128)(2,1)S(1)}, bf16[224,256]{1,0:T(8,128)(2,1)S(1)}, u32[]{:S(2)}, u32[]{:S(2)}) collective-permute-start(bf16[224,256]{1,0:T(8,128)(2,1)S(1)} %get-tuple-element.46), channel_id=1, source_target_pairs={{0,32},{32,0},{64,96},{96,64},{1,33},{33,1},{65,97},{97,65},{2,34}... | collective-permute-start | bytes 344072 | tf_op jit(solution)/shard_map/ppermute | solution.py:363
  60.5 10.2 %collective-permute-start.9 = (bf16[224,256]{1,0:T(8,128)(2,1)S(1)}, bf16[224,256]{1,0:T(8,128)(2,1)S(1)}, u32[]{:S(2)}, u32[]{:S(2)}) collective-permute-start(bf16[224,256]{1,0:T(8,128)(2,1)S(1)} %add_convert_fusion.filt_ref), channel_id=1, source_target_pairs={{0,64},{32,96},{64,0},{96,32},{1,65},{33,97},{65,1},{97,33},{2,66}... | collective-permute-start | bytes 344072 | tf_op jit(solution)/shard_map/ppermute | solution.py:365

commit v5 on v4

--- a/solution.py
+++ b/solution.py
@@ -19,7 +19,8 @@
 BLOCK = 8
 WIDE = 256
 TAP_ROWS = 224
-PREPARE = 16 * 10**9
+PACK = 0
+PREPARE = 8 * 10**9
 UNPACK = 16 * 10**9
 F32 = jnp.float32
 BF16 = jnp.bfloat16
@@ -42,19 +43,29 @@
     return (col + kw >= 0) & (col + kw < W)
 
 
-def pack_kernel(planes, x_any, cot_any, w_any, bias_any, chunks, *refs):
-    packs, (x_ref, cot_ref, w_ref, bias_ref, in_sems) = refs[:RING], refs[RING:]
+def hop(slot, core):
+    return (0, 1 + 2 * core, 2, 3 - 2 * core)[slot]
+
+
+def ring_chunk(slot):
+    at = jnp.bitwise_and(lax.axis_index("filt"), RING - 1)
+    core = jnp.bitwise_and(lax.axis_index("space"), 1)
+    return jnp.bitwise_xor(at, hop(slot, core))
+
+
+def swapped(x):
+    return jnp.concatenate([x[slot * BLOCK : (slot + 1) * BLOCK] for slot in (0, 3, 2, 1)], 0)
+
+
+def pack_kernel(planes, x_any, cot_any, bias_any, chunks, *refs):
+    packs, (x_ref, cot_ref, bias_ref, in_sems) = refs[:RING], refs[RING:]
     copies = [
         pltpu.make_async_copy(src, dst, in_sems.at[i])
-        for i, (src, dst) in enumerate(((w_any, w_ref), (x_any, x_ref), (cot_any, cot_ref), (bias_any, bias_ref)))
+        for i, (src, dst) in enumerate(((x_any, x_ref), (cot_any, cot_ref), (bias_any, bias_ref)))
     ]
     for copy in copies:
         copy.start()
     copies[0].wait()
-    w = jnp.concatenate([w_ref[...].astype(F32), jnp.zeros((BLOCK, WIDE), F32)], 0).astype(BF16)
-    for m in range(RING):
-        packs[m][0:TAP_ROWS, :] = w
-    copies[1].wait()
     lane = lax.broadcasted_iota(jnp.int32, (BLOCK, 2 * W), 1)
     for v in range(RING):
         for d in range(planes):
@@ -70,42 +81,48 @@
             for g in range(chunks.shape[0] // RING):
                 chunks[g * RING + v, :, d * OUTER : d * OUTER + INNER] = own
                 chunks[g * RING + v, :, d * OUTER + INNER : (d + 1) * OUTER] = halo
+    copies[1].wait()
     copies[2].wait()
-    copies[3].wait()
     bias = jnp.broadcast_to(bias_ref[...].astype(F32), (16, BLOCK))
     bias = jnp.concatenate([bias, jnp.zeros((16, WIDE - BLOCK), F32)], 1).astype(BF16)
-    for m in range(RING):
-        chunk = jnp.bitwise_xor(jnp.bitwise_and(lax.axis_index("filt"), RING - 1), m)
+    for slot, pack in enumerate(packs):
         for d in range(planes):
-            lanes = pl.ds(pl.multiple_of(chunk * INNER + d * PLANE, INNER), INNER)
-            start = TAP_ROWS + 16 * d
-            packs[m][start : start + 16, :] = fold(cot_ref[:, lanes].astype(F32)).astype(BF16)
-        start = TAP_ROWS + 16 * planes
-        packs[m][start : start + 16, :] = bias
-
-
-def prepare_kernel(planes, *refs):
-    packs, (w_ref, turned_ref, cot_ref, bias_ref) = refs[:RING], refs[RING:]
+            start = ring_chunk(slot) * INNER + d * PLANE
+            rows = cot_ref[:, pl.ds(pl.multiple_of(start, INNER), INNER)]
+            pack[16 * d : 16 * d + 16, :] = fold(rows.astype(F32)).astype(BF16)
+        pack[16 * planes : 16 * planes + 16, :] = bias
+
+
+def upstream(packs, d):
+    rows = slice(16 * d, 16 * d + 16)
+    return jnp.concatenate([unfold(pack[rows, :].astype(F32)) for pack in packs], 0)
+
+
+def offsets(packs, planes):
     diagonal = lax.broadcasted_iota(jnp.int32, (BLOCK, 2 * W), 0) == lax.broadcasted_iota(
         jnp.int32, (BLOCK, 2 * W), 1
     )
-    for m, pack in enumerate(packs):
-        own = slice(m * BLOCK, (m + 1) * BLOCK)
-        w_ref[m * TAP_ROWS : (m + 1) * TAP_ROWS, :] = pack[0:TAP_ROWS, :]
-        for d in range(planes):
-            start = TAP_ROWS + 16 * d
-            lanes = slice(d * INNER, (d + 1) * INNER)
-            cot_ref[own, lanes] = unfold(pack[start : start + 16, :].astype(F32))
-        start = TAP_ROWS + 16 * planes
-        row = pack[start : start + 16, 0 : 2 * W].astype(F32)[:BLOCK]
-        bias = jnp.sum(jnp.where(diagonal, row, 0.0), axis=1, keepdims=True)
-        bias_ref[own, :] = jnp.broadcast_to(bias, (BLOCK, 2 * W))
+    rows = slice(16 * planes, 16 * planes + 16)
+    columns = []
+    for pack in packs:
+        row = pack[rows, 0 : 2 * W].astype(F32)[:BLOCK]
+        columns.append(jnp.sum(jnp.where(diagonal, row, 0.0), axis=1, keepdims=True))
+    return jnp.concatenate(columns, 0)
+
+
+def prepare_kernel(*refs):
+    taps, (w_ref, turned_ref) = refs[:RING], refs[RING:]
+    for m in range(RING):
+        w = jnp.concatenate([taps[m][...].astype(F32), jnp.zeros((BLOCK, WIDE), F32)], 0)
+        w_ref[m * TAP_ROWS : (m + 1) * TAP_ROWS, :] = w.astype(BF16)
     turned_ref[...] = w_ref[...].T
 
 
 def forward_kernel(
-    planes, x_ref, w_ref, cot_ref, own_ref, low_ref, high_ref, up_ref, down_ref, *maps
+    planes, x_ref, w_ref, *refs
 ):
+    packs, (own_ref, low_ref, high_ref, up_ref, down_ref) = refs[:RING], refs[RING : RING + 5]
+    maps = refs[RING + 5 :]
     for m in range(RING):
         w = w_ref[m * TAP_ROWS : (m + 1) * TAP_ROWS, :]
         maps[m][...] = jnp.dot(w, x_ref[...], preferred_element_type=F32)
@@ -142,34 +159,32 @@
         for edge, ref in ((planes - 1, up_ref), (0, down_ref)):
             if out == edge:
                 ref[:, INNER : 2 * INNER] = total.astype(BF16)
-                ref[:, 2 * INNER : 3 * INNER] = cot_ref[
-                    :, out * INNER : (out + 1) * INNER
-                ].astype(BF16)
+                ref[:, 2 * INNER : 3 * INNER] = upstream(packs, out).astype(BF16)
 
 
 def backward_kernel(
-    planes, x_ref, own_ref, low_ref, high_ref, before_ref, after_ref, cot_ref, bias_ref, *refs
+    planes, x_ref, own_ref, low_ref, high_ref, before_ref, after_ref, turned_ref, *refs
 ):
-    turned_ref, part_any, backs = refs[0], refs[1], refs[2 : RING + 2]
-    bank, (shifted, part, sems) = refs[RING + 2 : 2 * RING + 2], refs[2 * RING + 2 :]
-    bias = bias_ref[:, 0:1]
+    packs, part_any, backs = refs[:RING], refs[RING], refs[RING + 1 : 2 * RING + 1]
+    bank, (shifted, part, sems) = refs[2 * RING + 1 : 3 * RING + 1], refs[3 * RING + 1 :]
+    bias = offsets(packs, planes)
     masks = {kw: inside_row(BLOCK, kw) for kw in (-1, 1)}
     for m in range(RING):
         bank[m][TAP_ROWS - BLOCK : TAP_ROWS, :] = jnp.zeros((BLOCK, planes * OUTER), F32)
     for src in range(-1, planes + 1):
         if src < 0:
-            pre = before_ref[:, INNER : 2 * INNER].astype(F32) + low_ref[...]
-            cot = before_ref[:, 2 * INNER : 3 * INNER].astype(F32)
+            pre = swapped(before_ref[:, INNER : 2 * INNER].astype(F32)) + low_ref[...]
+            cot = swapped(before_ref[:, 2 * INNER : 3 * INNER].astype(F32))
         elif src >= planes:
-            pre = after_ref[:, INNER : 2 * INNER].astype(F32) + high_ref[...]
-            cot = after_ref[:, 2 * INNER : 3 * INNER].astype(F32)
+            pre = swapped(after_ref[:, INNER : 2 * INNER].astype(F32)) + high_ref[...]
+            cot = swapped(after_ref[:, 2 * INNER : 3 * INNER].astype(F32))
         else:
             pre = own_ref[:, src * INNER : (src + 1) * INNER]
-            cot = cot_ref[:, src * INNER : (src + 1) * INNER]
+            cot = upstream(packs, src)
             if src == 0:
-                pre = pre + before_ref[:, 0:INNER].astype(F32)
+                pre = pre + swapped(before_ref[:, 0:INNER].astype(F32))
             if src == planes - 1:
-                pre = pre + after_ref[:, 0:INNER].astype(F32)
+                pre = pre + swapped(after_ref[:, 0:INNER].astype(F32))
         pre = pre + bias
         s = jax.nn.sigmoid(pre)
         if 0 <= src < planes:
@@ -217,7 +232,7 @@
     for m, back in enumerate(backs):
         part = back[0:TAP_ROWS, :].astype(F32)
         total = part if total is None else total + part
-        chunk = jnp.bitwise_xor(jnp.bitwise_and(lax.axis_index("filt"), RING - 1), m)
+        chunk = ring_chunk(m)
         for d in range(planes):
             lanes = pl.ds(pl.multiple_of(chunk * INNER + d * PLANE, INNER), INNER)
             start = TAP_ROWS + 16 * d
@@ -276,45 +291,45 @@
     inner = planes * INNER
     group = RING * BLOCK
     w = jnp.transpose(weight, (1, 0, 2)).reshape(len(TAPS) * block, channels)
-    pack = ((TAP_ROWS + 16 * planes + 16, WIDE), BF16)
+
+    def to_slot(value, slot):
+        pairs = [
+            (s * parts + f, s * parts + (f ^ hop(slot, s & 1)))
+            for s in range(slabs)
+            for f in range(parts)
+        ]
+        return lax.ppermute(value, ("space", "filt"), pairs) if slot else value
+
+    first, second = to_slot(w, 1), to_slot(w, 2)
+    pack = ((16 * planes + 16, WIDE), BF16)
     chunks, *packs = call(
         functools.partial(pack_kernel, planes),
-        (features.reshape(block, voxels), cotangent.reshape(block, voxels), w, bias_vec[None]),
+        (features.reshape(block, voxels), cotangent.reshape(block, voxels), bias_vec[None]),
         [((parts, block, outer), BF16)] + [pack] * RING,
         [
             pltpu.VMEM((block, voxels), BF16),
             pltpu.VMEM((block, voxels), BF16),
-            pltpu.VMEM((len(TAPS) * block, channels), BF16),
             pltpu.VMEM((1, block), BF16),
-            pltpu.SemaphoreType.DMA((4,)),
+            pltpu.SemaphoreType.DMA((3,)),
         ],
-        0,
+        PACK,
         2 * parts * block * outer,
         "pack",
-        (0, 1, 2, 3),
+        (0, 1, 2),
         (),
         61,
     )
-
-    def to_ring(values):
-        swap = lambda m: [(i, i ^ m) for i in range(parts)]
-        return [values[0]] + [lax.ppermute(values[m], "filt", swap(m)) for m in range(1, RING)]
-
-    packs = to_ring(packs)
+    packs = [to_slot(value, slot) for slot, value in enumerate(packs)]
+    third = lax.ppermute(first, "space", [(s, s ^ 1) for s in range(slabs)])
     x = lax.all_to_all(chunks, "filt", 0, 0, tiled=True).reshape(channels, outer)
 
     edge = ((group, 3 * INNER), BF16)
     plane = ((group, INNER), F32)
     flops = 2 * RING * TAP_ROWS * channels * outer
-    w, turned, cot, bias = call(
-        functools.partial(prepare_kernel, planes),
-        packs,
-        [
-            ((RING * TAP_ROWS, channels), BF16),
-            ((channels, RING * TAP_ROWS), BF16),
-            ((group, inner), F32),
-            ((group, 2 * W), F32),
-        ],
+    w, turned = call(
+        prepare_kernel,
+        (w, first, second, third),
+        [((RING * TAP_ROWS, channels), BF16), ((channels, RING * TAP_ROWS), BF16)],
         [],
         PREPARE,
         RING * TAP_ROWS * WIDE * 4,
@@ -322,7 +337,7 @@
     )
     own, low, high, up, down = call(
         functools.partial(forward_kernel, planes),
-        (x, w, cot),
+        (x, w, *packs),
         [((group, inner), F32), plane, plane, edge, edge],
         [pltpu.VMEM((TAP_ROWS, outer), F32)] * RING,
         flops,
@@ -334,7 +349,7 @@
     back = ((TAP_ROWS + 16 * planes, WIDE), BF16)
     part, *backs = call(
         functools.partial(backward_kernel, planes),
-        (x, own, low, high, before, after, cot, bias, turned),
+        (x, own, low, high, before, after, turned, *packs),
         [((channels, outer), BF16)] + [back] * RING,
         [pltpu.VMEM((TAP_ROWS, outer), F32)] * RING
         + [
@@ -348,7 +363,7 @@
         (),
         (0,),
     )
-    backs = to_ring(backs)
+    backs = [to_slot(value, slot) for slot, value in enumerate(backs)]
     got = lax.all_to_all(part.reshape(parts, block, outer), "filt", 0, 0, tiled=True)
     filt, activation = call(
         functools.partial(unpack_kernel, planes),

time: 73.8 us -> 73.2 us (level)
  waiting for transfers between devices: 28 us -> 23.5 us
  starting transfers between devices: 35.8 us -> 39.7 us
    all_to_all x1, waiting for transfers between devices: 13.6 us -> 0.01 us  [per_device(): lax.all_to_all(chunks, 'filt', 0, 0, tiled=True).reshape(channels, outer)]
    ppermute x6 -> x9, starting transfers between devices: 8.54 us -> 15.2 us  [the longest x8 12.8 us: to_slot(): return lax.ppermute(value, ('space', 'filt'), pairs) if slot else value]
    ppermute x6 -> x9, waiting for transfers between devices: 0.19 us -> 6.52 us  [the longest x8 6.52 us: to_slot(): return lax.ppermute(value, ('space', 'filt'), pairs) if slot else value]
    ppermute x1, waiting for transfers between devices: 5.57 us -> 8 us  [per_device(): other = lax.ppermute(filt, 'space', by(2))]
    ppermute x1, starting transfers between devices: 4.65 us -> 2.43 us  [per_device(): other = lax.ppermute(filt, 'space', by(2))]
    all_to_all x1, starting transfers between devices: 8.92 us -> 6.81 us  [per_device(): lax.all_to_all(chunks, 'filt', 0, 0, tiled=True).reshape(channels, outer)]
    all_to_all x1, starting transfers between devices: 3.92 us -> 5.09 us  [per_device(): lax.all_to_all(part.reshape(parts, block, outer), 'filt', 0, 0, tiled=True)]
  transfers between devices with their start and end apart: 12 -> 15, of which waited for: 6 -> 6; matrix products, arithmetic and copies ran while one was open for 0% -> 0% of each run, Pallas kernels for 1% -> 4%
where the time goes in v5:
time: 73.2 us; the launch traced here: 72.8 us
  starting transfers between devices  39.7 us (54%)
  waiting for transfers between devices  23.5 us (32%)
  Pallas kernels  8.81 us (12%)
  between operations  0.79 us (1%)
    ppermute x8, starting transfers between devices, to_slot(): return lax.ppermute(value, ('space', 'filt'), pairs) if slot else value  12.8 us
    pallas_call x6, Pallas kernels, call(): pl.pallas_call(kernel, out_shape=shapes, in_specs=[smem if x.dtype == jnp...  8.81 us
    ppermute x1, starting transfers between devices, per_device(): before = lax.ppermute(up, 'space', [(i, i + 1) for i in range(slabs - 1)])  8.15 us
    ppermute x1, waiting for transfers between devices, per_device(): other = lax.ppermute(filt, 'space', by(2))  8 us
    all_to_all x1, starting transfers between devices, per_device(): lax.all_to_all(chunks, 'filt', 0, 0, tiled=True).reshape(channels, outer)  6.81 us
    ppermute x8, waiting for transfers between devices, to_slot(): return lax.ppermute(value, ('space', 'filt'), pairs) if slot else value  6.52 us
    ppermute x1, waiting for transfers between devices, per_device(): after = lax.ppermute(down, 'space', [(i + 1, i) for i in range(slabs - 1)])  5.5 us
    all_to_all x1, starting transfers between devices, per_device(): lax.all_to_all(part.reshape(parts, block, outer), 'filt', 0, 0, tiled=True)  5.09 us
  transfers between devices with their start and end apart: 15, of which 6 were waited for; matrix products, arithmetic and copies ran while one was open for 0% of the time, Pallas kernels for 4%

profile of v5, /device:TPU:1, one launch (start us, length us, event | category | flops | bytes accessed | tf_op | source)
XLA Modules:
  0.0 72.8 jit_solution(10691030242702170664)
XLA Ops:
  0.6 3.4 %collective-permute-start = (bf16[216,256]{1,0:T(8,128)(2,1)}, bf16[216,256]{1,0:T(8,128)(2,1)S(1)}, u32[]{:S(2)}, u32[]{:S(2)}) collective-permute-start(bf16[216,256]{1,0:T(8,128)(2,1)} %bitcast.15), channel_id=1, source_target_pairs={{0,1},{1,0},{2,3},{3,2},{4,5},{5,4},{6,7},{7,6},{8,9},{9,8},{10,11... | collective-permute-start | bytes 331784 | tf_op jit(solution)/shard_map/ppermute | solution.py:301
  4.0 2.0 %pack.1 = (bf16[32,8,1920]{2,1,0:T(8,128)(2,1)}, bf16[64,256]{1,0:T(8,128)(2,1)}, bf16[64,256]{1,0:T(8,128)(2,1)}, bf16[64,256]{1,0:T(8,128)(2,1)}, bf16[64,256]{1,0:T(8,128)(2,1)}) custom-call(bf16[8,6144]{1,0:T(8,128)(2,1)} %bitcast.18, bf16[8,6144]{1,0:T(8,128)(2,1)} %bitcast.19, bf16[1,8]{1,0:T(2,128)(2,1)} %bitcast.20), custom_call_target="tpu_custom_call" | custom-call | bytes 983040 | tf_op jit(solution)/shard_map/pack/pallas_call | solution.py:272
  6.1 6.8 %all-to-all-start = ((bf16[32,8,1920]{2,1,0:T(8,128)(2,1)}), bf16[32,8,1920]{2,1,0:T(8,128)(2,1)S(1)}, u32[]{:S(2)}, u32[]{:S(2)}) async-start(bf16[32,8,1920]{2,1,0:T(8,128)(2,1)} %get-tuple-element.24), calls=%async_computation | async-start | bytes 1966080 | tf_op jit(solution)/shard_map/all_to_all | solution.py:324
  12.9 2.8 %collective-permute-start.1 = (bf16[216,256]{1,0:T(8,128)(2,1)S(1)}, bf16[216,256]{1,0:T(8,128)(2,1)S(1)}, u32[]{:S(2)}, u32[]{:S(2)}) collective-permute-start(bf16[216,256]{1,0:T(8,128)(2,1)S(1)} %bitcast.16), channel_id=1, source_target_pairs={{0,2},{1,3},{2,0},{3,1},{4,6},{5,7},{6,4},{7,5},{8,10},{9,11},{10,... | collective-permute-start | bytes 331784 | tf_op jit(solution)/shard_map/ppermute | solution.py:301
  15.7 2.5 %collective-permute-start.2 = (bf16[216,256]{1,0:T(8,128)(2,1)S(1)}, bf16[216,256]{1,0:T(8,128)(2,1)S(1)}, u32[]{:S(2)}, u32[]{:S(2)}) collective-permute-start(bf16[216,256]{1,0:T(8,128)(2,1)S(1)} %collective-permute-done.refs_1_), channel_id=1, source_target_pairs={{0,32},{32,0},{64,96},{96,64},{1,33},{33,1},{65,97},{97,65},{2,34}... | collective-permute-start | bytes 331784 | tf_op jit(solution)/shard_map/ppermute | solution.py:323
  18.2 0.9 %collective-permute-start.3 = (bf16[64,256]{1,0:T(8,128)(2,1)S(1)}, bf16[64,256]{1,0:T(8,128)(2,1)S(1)}, u32[]{:S(2)}, u32[]{:S(2)}) collective-permute-start(bf16[64,256]{1,0:T(8,128)(2,1)S(1)} %copy-done.4), channel_id=1, source_target_pairs={{0,1},{1,0},{2,3},{3,2},{4,5},{5,4},{6,7},{7,6},{8,9},{9,8},{10,11... | collective-permute-start | bytes 98312 | tf_op jit(solution)/shard_map/ppermute | solution.py:301
  19.1 1.2 %collective-permute-start.4 = (bf16[64,256]{1,0:T(8,128)(2,1)S(1)}, bf16[64,256]{1,0:T(8,128)(2,1)S(1)}, u32[]{:S(2)}, u32[]{:S(2)}) collective-permute-start(bf16[64,256]{1,0:T(8,128)(2,1)S(1)} %copy-done.3), channel_id=1, source_target_pairs={{0,2},{1,3},{2,0},{3,1},{4,6},{5,7},{6,4},{7,5},{8,10},{9,11},{10,... | collective-permute-start | bytes 98312 | tf_op jit(solution)/shard_map/ppermute | solution.py:301
  20.3 1.2 %collective-permute-start.5 = (bf16[64,256]{1,0:T(8,128)(2,1)S(1)}, bf16[64,256]{1,0:T(8,128)(2,1)S(1)}, u32[]{:S(2)}, u32[]{:S(2)}) collective-permute-start(bf16[64,256]{1,0:T(8,128)(2,1)S(1)} %copy-done.2), channel_id=1, source_target_pairs={{0,3},{1,2},{2,1},{3,0},{4,7},{5,6},{6,5},{7,4},{8,11},{9,10},{10,... | collective-permute-start | bytes 98312 | tf_op jit(solution)/shard_map/ppermute | solution.py:301
  21.5 6.0 %collective-permute-done.1.refs_2_ = bf16[216,256]{1,0:T(8,128)(2,1)S(1)} collective-permute-done((bf16[216,256]{1,0:T(8,128)(2,1)S(1)}, bf16[216,256]{1,0:T(8,128)(2,1)S(1)}, u32[]{:S(2)}, u32[]{:S(2)}) %collective-permute-start.1) | collective-permute-done | bytes 110624 | tf_op jit(solution)/shard_map/ppermute | solution.py:301
  28.2 1.4 %conv_forward.1 = (f32[32,1536]{1,0:T(8,128)S(1)}, f32[32,512]{1,0:T(8,128)S(1)}, f32[32,512]{1,0:T(8,128)S(1)}, bf16[32,1536]{1,0:T(8,128)(2,1)S(1)}, bf16[32,1536]{1,0:T(8,128)(2,1)S(1)}) custom-call(bf16[256,1920]{1,0:T(8,128)(2,1)S(1)} %bitcast.13, bf16[896,256]{1,0:T(8,128)(2,1)S(1)} %get-tuple-element.25.w_ref, bf16[64,256]{1,0:T(8,128)(2,1)S(1)} %copy-done.1, ...), custom_call_target="tpu_custom_call" | custom-call | flops 880803840 | bytes 983040 | tf_op jit(solution)/shard_map/conv_forward/pallas_call | solution.py:272
  29.6 8.2 %collective-permute-start.6 = (bf16[32,1536]{1,0:T(8,128)(2,1)S(1)}, bf16[32,1536]{1,0:T(8,128)(2,1)S(1)}, u32[]{:S(2)}, u32[]{:S(2)}) collective-permute-start(bf16[32,1536]{1,0:T(8,128)(2,1)S(1)} %get-tuple-element.33), channel_id=1, source_target_pairs={{0,32},{32,64},{64,96},{1,33},{33,65},{65,97},{2,34},{34,66},{66,9... | collective-permute-start | bytes 294920 | tf_op jit(solution)/shard_map/ppermute | solution.py:347
  37.7 1.9 %collective-permute-start.7 = (bf16[32,1536]{1,0:T(8,128)(2,1)S(1)}, bf16[32,1536]{1,0:T(8,128)(2,1)S(1)}, u32[]{:S(2)}, u32[]{:S(2)}) collective-permute-start(bf16[32,1536]{1,0:T(8,128)(2,1)S(1)} %get-tuple-element.34), channel_id=1, source_target_pairs={{32,0},{64,32},{96,64},{33,1},{65,33},{97,65},{34,2},{66,34},{98,6... | collective-permute-start | bytes 294920 | tf_op jit(solution)/shard_map/ppermute | solution.py:348
  39.7 5.5 %collective-permute-done.7.after_ref = bf16[32,1536]{1,0:T(8,128)(2,1)S(1)} collective-permute-done((bf16[32,1536]{1,0:T(8,128)(2,1)S(1)}, bf16[32,1536]{1,0:T(8,128)(2,1)S(1)}, u32[]{:S(2)}, u32[]{:S(2)}) %collective-permute-start.7) | collective-permute-done | bytes 98336 | tf_op jit(solution)/shard_map/ppermute | solution.py:348
  45.2 3.8 %conv_backward.1 = (bf16[256,1920]{1,0:T(8,128)(2,1)}, bf16[272,256]{1,0:T(8,128)(2,1)S(1)}, bf16[272,256]{1,0:T(8,128)(2,1)S(1)}, bf16[272,256]{1,0:T(8,128)(2,1)S(1)}, bf16[272,256]{1,0:T(8,128)(2,1)S(1)}) custom-call(bf16[256,1920]{1,0:T(8,128)(2,1)S(1)} %bitcast.14, f32[32,1536]{1,0:T(8,128)S(1)} %get-tuple-element.30.own_ref, ...), custom_call_target="tpu_custom_call" | custom-call | flops 1761607680 | bytes 1966080 | tf_op jit(solution)/shard_map/conv_backward/pallas_call | solution.py:272
  48.9 0.9 %collective-permute-start.8 = (bf16[272,256]{1,0:T(8,128)(2,1)S(1)}, bf16[272,256]{1,0:T(8,128)(2,1)S(1)}, u32[]{:S(2)}, u32[]{:S(2)}) collective-permute-start(bf16[272,256]{1,0:T(8,128)(2,1)S(1)} %get-tuple-element.37), channel_id=1, source_target_pairs={{0,1},{1,0},{2,3},{3,2},{4,5},{5,4},{6,7},{7,6},{8,9},{9,8},{10,11... | collective-permute-start | bytes 417800 | tf_op jit(solution)/shard_map/ppermute | solution.py:301
  49.9 1.3 %collective-permute-start.9 = (bf16[272,256]{1,0:T(8,128)(2,1)S(1)}, bf16[272,256]{1,0:T(8,128)(2,1)S(1)}, u32[]{:S(2)}, u32[]{:S(2)}) collective-permute-start(bf16[272,256]{1,0:T(8,128)(2,1)S(1)} %get-tuple-element.38), channel_id=1, source_target_pairs={{0,2},{1,3},{2,0},{3,1},{4,6},{5,7},{6,4},{7,5},{8,10},{9,11},{10,... | collective-permute-start | bytes 417800 | tf_op jit(solution)/shard_map/ppermute | solution.py:301
  51.1 1.1 %collective-permute-start.10 = (bf16[272,256]{1,0:T(8,128)(2,1)S(1)}, bf16[272,256]{1,0:T(8,128)(2,1)S(1)}, u32[]{:S(2)}, u32[]{:S(2)}) collective-permute-start(bf16[272,256]{1,0:T(8,128)(2,1)S(1)} %get-tuple-element.39), channel_id=1, source_target_pairs={{0,3},{1,2},{2,1},{3,0},{4,7},{5,6},{6,5},{7,4},{8,11},{9,10},{10,... | collective-permute-start | bytes 417800 | tf_op jit(solution)/shard_map/ppermute | solution.py:301
  52.3 5.1 %all-to-all-start.1 = ((bf16[32,8,1920]{2,1,0:T(8,128)(2,1)}), bf16[32,8,1920]{2,1,0:T(8,128)(2,1)S(1)}, u32[]{:S(2)}, u32[]{:S(2)}) async-start(bf16[32,8,1920]{2,1,0:T(8,128)(2,1)} %bitcast.8), calls=%async_computation.1 | async-start | bytes 1966080 | tf_op jit(solution)/shard_map/all_to_all | solution.py:367
  57.4 0.7 unpack.1
  58.1 1.3 %collective-permute-done.11 = bf16[224,256]{1,0:T(8,128)(2,1)S(1)} collective-permute-done((bf16[224,256]{1,0:T(8,128)(2,1)S(1)}, bf16[224,256]{1,0:T(8,128)(2,1)S(1)}, u32[]{:S(2)}, u32[]{:S(2)}) %collective-permute-start.11) | collective-permute-done | bytes 114720 | tf_op jit(solution)/shard_map/ppermute | solution.py:378
  59.4 2.4 %collective-permute-start.12 = (bf16[224,256]{1,0:T(8,128)(2,1)S(1)}, bf16[224,256]{1,0:T(8,128)(2,1)S(1)}, u32[]{:S(2)}, u32[]{:S(2)}) collective-permute-start(bf16[224,256]{1,0:T(8,128)(2,1)S(1)} %add_convert_fusion.filt_ref), channel_id=1, source_target_pairs={{0,64},{32,96},{64,0},{96,32},{1,65},{33,97},{65,1},{97,33},{2,66}... | collective-permute-start | bytes 344072 | tf_op jit(solution)/shard_map/ppermute | solution.py:380
  61.9 8.0 %collective-permute-done.12.other_ref = bf16[224,256]{1,0:T(8,128)(2,1)S(1)} collective-permute-done((bf16[224,256]{1,0:T(8,128)(2,1)S(1)}, bf16[224,256]{1,0:T(8,128)(2,1)S(1)}, u32[]{:S(2)}, u32[]{:S(2)}) %collective-permute-start.12) | collective-permute-done | bytes 114720 | tf_op jit(solution)/shard_map/ppermute | solution.py:380
  69.9 2.2 %all-to-all-done.1.got_ref = bf16[32,8,1920]{2,1,0:T(8,128)(2,1)S(1)} async-done(((bf16[32,8,1920]{2,1,0:T(8,128)(2,1)}), bf16[32,8,1920]{2,1,0:T(8,128)(2,1)S(1)}, u32[]{:S(2)}, u32[]{:S(2)}) %all-to-all-start.1) | async-done | bytes 983072 | tf_op jit(solution)/shard_map/all_to_all | solution.py:367
  72.0 0.8 %collect.1 = (bf16[8,6144]{1,0:T(8,128)(2,1)}, f32[216,256]{1,0:T(8,128)}) custom-call(bf16[32,8,1920]{2,1,0:T(8,128)(2,1)S(1)} %all-to-all-done.1.got_ref, bf16[224,256]{1,0:T(8,128)(2,1)S(1)} %add_convert_fusion.filt_ref, bf16[224,256]{1,0:T(8,128)(2,1)S(1)} %collective-permute-done.12.other_ref), custom_call_target="tpu_custom_call" | custom-call | bytes 983040 | tf_op jit(solution)/shard_map/collect/pallas_call | solution.py:272
  (23 shorter events, 0.8 us)
Async XLA Ops:
  0.6 15.1 %collective-permute-start = (bf16[216,256]{1,0:T(8,128)(2,1)}, bf16[216,256]{1,0:T(8,128)(2,1)S(1)}, u32[]{:S(2)}, u32[]{:S(2)}) collective-permute-start(bf16[216,256]{1,0:T(8,128)(2,1)} %bitcast.15), channel_id=1, source_target_pairs={{0,1},{1,0},{2,3},{3,2},{4,5},{5,4},{6,7},{7,6},{8,9},{9,8},{10,11... | collective-permute-start | bytes 331784 | tf_op jit(solution)/shard_map/ppermute | solution.py:301
  6.0 6.9 %copy-start = (bf16[8,27,256]{2,0,1:T(8,128)(2,1)S(1)}, bf16[8,27,256]{2,0,1:T(8,128)(2,1)}, u32[]{:S(2)}) copy-start(bf16[8,27,256]{2,0,1:T(8,128)(2,1)} %param.5) | copy-start | bytes 331780
  6.0 12.1 %copy-start.4 = (bf16[64,256]{1,0:T(8,128)(2,1)S(1)}, bf16[64,256]{1,0:T(8,128)(2,1)}, u32[]{:S(2)}) copy-start(bf16[64,256]{1,0:T(8,128)(2,1)} %get-tuple-element.27) | copy-start | bytes 98308
  6.1 13.0 %copy-start.3 = (bf16[64,256]{1,0:T(8,128)(2,1)S(1)}, bf16[64,256]{1,0:T(8,128)(2,1)}, u32[]{:S(2)}) copy-start(bf16[64,256]{1,0:T(8,128)(2,1)} %get-tuple-element.28) | copy-start | bytes 98308
  6.1 14.2 %copy-start.2 = (bf16[64,256]{1,0:T(8,128)(2,1)S(1)}, bf16[64,256]{1,0:T(8,128)(2,1)}, u32[]{:S(2)}) copy-start(bf16[64,256]{1,0:T(8,128)(2,1)} %get-tuple-element.29) | copy-start | bytes 98308
  6.1 22.1 %all-to-all-start = ((bf16[32,8,1920]{2,1,0:T(8,128)(2,1)}), bf16[32,8,1920]{2,1,0:T(8,128)(2,1)S(1)}, u32[]{:S(2)}, u32[]{:S(2)}) async-start(bf16[32,8,1920]{2,1,0:T(8,128)(2,1)} %get-tuple-element.24), calls=%async_computation | async-start | bytes 1966080 | tf_op jit(solution)/shard_map/all_to_all | solution.py:324
  12.9 14.5 %collective-permute-start.1 = (bf16[216,256]{1,0:T(8,128)(2,1)S(1)}, bf16[216,256]{1,0:T(8,128)(2,1)S(1)}, u32[]{:S(2)}, u32[]{:S(2)}) collective-permute-start(bf16[216,256]{1,0:T(8,128)(2,1)S(1)} %bitcast.16), channel_id=1, source_target_pairs={{0,2},{1,3},{2,0},{3,1},{4,6},{5,7},{6,4},{7,5},{8,10},{9,11},{10,... | collective-permute-start | bytes 331784 | tf_op jit(solution)/shard_map/ppermute | solution.py:301
  15.7 11.7 %collective-permute-start.2 = (bf16[216,256]{1,0:T(8,128)(2,1)S(1)}, bf16[216,256]{1,0:T(8,128)(2,1)S(1)}, u32[]{:S(2)}, u32[]{:S(2)}) collective-permute-start(bf16[216,256]{1,0:T(8,128)(2,1)S(1)} %collective-permute-done.refs_1_), channel_id=1, source_target_pairs={{0,32},{32,0},{64,96},{96,64},{1,33},{33,1},{65,97},{97,65},{2,34}... | collective-permute-start | bytes 331784 | tf_op jit(solution)/shard_map/ppermute | solution.py:323
  18.2 9.5 %collective-permute-start.3 = (bf16[64,256]{1,0:T(8,128)(2,1)S(1)}, bf16[64,256]{1,0:T(8,128)(2,1)S(1)}, u32[]{:S(2)}, u32[]{:S(2)}) collective-permute-start(bf16[64,256]{1,0:T(8,128)(2,1)S(1)} %copy-done.4), channel_id=1, source_target_pairs={{0,1},{1,0},{2,3},{3,2},{4,5},{5,4},{6,7},{7,6},{8,9},{9,8},{10,11... | collective-permute-start | bytes 98312 | tf_op jit(solution)/shard_map/ppermute | solution.py:301
  19.1 9.1 %collective-permute-start.4 = (bf16[64,256]{1,0:T(8,128)(2,1)S(1)}, bf16[64,256]{1,0:T(8,128)(2,1)S(1)}, u32[]{:S(2)}, u32[]{:S(2)}) collective-permute-start(bf16[64,256]{1,0:T(8,128)(2,1)S(1)} %copy-done.3), channel_id=1, source_target_pairs={{0,2},{1,3},{2,0},{3,1},{4,6},{5,7},{6,4},{7,5},{8,10},{9,11},{10,... | collective-permute-start | bytes 98312 | tf_op jit(solution)/shard_map/ppermute | solution.py:301
  20.3 7.9 %copy-start.1 = (bf16[64,256]{1,0:T(8,128)(2,1)S(1)}, bf16[64,256]{1,0:T(8,128)(2,1)}, u32[]{:S(2)}) copy-start(bf16[64,256]{1,0:T(8,128)(2,1)} %get-tuple-element.26.refs_0_) | copy-start | bytes 98308
  20.3 7.9 %collective-permute-start.5 = (bf16[64,256]{1,0:T(8,128)(2,1)S(1)}, bf16[64,256]{1,0:T(8,128)(2,1)S(1)}, u32[]{:S(2)}, u32[]{:S(2)}) collective-permute-start(bf16[64,256]{1,0:T(8,128)(2,1)S(1)} %copy-done.2), channel_id=1, source_target_pairs={{0,3},{1,2},{2,1},{3,0},{4,7},{5,6},{6,5},{7,4},{8,11},{9,10},{10,... | collective-permute-start | bytes 98312 | tf_op jit(solution)/shard_map/ppermute | solution.py:301
  29.6 10.1 %collective-permute-start.6 = (bf16[32,1536]{1,0:T(8,128)(2,1)S(1)}, bf16[32,1536]{1,0:T(8,128)(2,1)S(1)}, u32[]{:S(2)}, u32[]{:S(2)}) collective-permute-start(bf16[32,1536]{1,0:T(8,128)(2,1)S(1)} %get-tuple-element.33), channel_id=1, source_target_pairs={{0,32},{32,64},{64,96},{1,33},{33,65},{65,97},{2,34},{34,66},{66,9... | collective-permute-start | bytes 294920 | tf_op jit(solution)/shard_map/ppermute | solution.py:347
  37.7 7.4 %collective-permute-start.7 = (bf16[32,1536]{1,0:T(8,128)(2,1)S(1)}, bf16[32,1536]{1,0:T(8,128)(2,1)S(1)}, u32[]{:S(2)}, u32[]{:S(2)}) collective-permute-start(bf16[32,1536]{1,0:T(8,128)(2,1)S(1)} %get-tuple-element.34), channel_id=1, source_target_pairs={{32,0},{64,32},{96,64},{33,1},{65,33},{97,65},{34,2},{66,34},{98,6... | collective-permute-start | bytes 294920 | tf_op jit(solution)/shard_map/ppermute | solution.py:348
  48.9 8.4 %collective-permute-start.8 = (bf16[272,256]{1,0:T(8,128)(2,1)S(1)}, bf16[272,256]{1,0:T(8,128)(2,1)S(1)}, u32[]{:S(2)}, u32[]{:S(2)}) collective-permute-start(bf16[272,256]{1,0:T(8,128)(2,1)S(1)} %get-tuple-element.37), channel_id=1, source_target_pairs={{0,1},{1,0},{2,3},{3,2},{4,5},{5,4},{6,7},{7,6},{8,9},{9,8},{10,11... | collective-permute-start | bytes 417800 | tf_op jit(solution)/shard_map/ppermute | solution.py:301
  49.9 7.5 %collective-permute-start.9 = (bf16[272,256]{1,0:T(8,128)(2,1)S(1)}, bf16[272,256]{1,0:T(8,128)(2,1)S(1)}, u32[]{:S(2)}, u32[]{:S(2)}) collective-permute-start(bf16[272,256]{1,0:T(8,128)(2,1)S(1)} %get-tuple-element.38), channel_id=1, source_target_pairs={{0,2},{1,3},{2,0},{3,1},{4,6},{5,7},{6,4},{7,5},{8,10},{9,11},{10,... | collective-permute-start | bytes 417800 | tf_op jit(solution)/shard_map/ppermute | solution.py:301
  51.1 6.3 %collective-permute-start.10 = (bf16[272,256]{1,0:T(8,128)(2,1)S(1)}, bf16[272,256]{1,0:T(8,128)(2,1)S(1)}, u32[]{:S(2)}, u32[]{:S(2)}) collective-permute-start(bf16[272,256]{1,0:T(8,128)(2,1)S(1)} %get-tuple-element.39), channel_id=1, source_target_pairs={{0,3},{1,2},{2,1},{3,0},{4,7},{5,6},{6,5},{7,4},{8,11},{9,10},{10,... | collective-permute-start | bytes 417800 | tf_op jit(solution)/shard_map/ppermute | solution.py:301
  52.3 19.7 %all-to-all-start.1 = ((bf16[32,8,1920]{2,1,0:T(8,128)(2,1)}), bf16[32,8,1920]{2,1,0:T(8,128)(2,1)S(1)}, u32[]{:S(2)}, u32[]{:S(2)}) async-start(bf16[32,8,1920]{2,1,0:T(8,128)(2,1)} %bitcast.8), calls=%async_computation.1 | async-start | bytes 1966080 | tf_op jit(solution)/shard_map/all_to_all | solution.py:367
  58.1 1.3 %collective-permute-start.11 = (bf16[224,256]{1,0:T(8,128)(2,1)S(1)}, bf16[224,256]{1,0:T(8,128)(2,1)S(1)}, u32[]{:S(2)}, u32[]{:S(2)}) collective-permute-start(bf16[224,256]{1,0:T(8,128)(2,1)S(1)} %get-tuple-element.42), channel_id=1, source_target_pairs={{0,32},{32,0},{64,96},{96,64},{1,33},{33,1},{65,97},{97,65},{2,34}... | collective-permute-start | bytes 344072 | tf_op jit(solution)/shard_map/ppermute | solution.py:378
  59.4 10.4 %collective-permute-start.12 = (bf16[224,256]{1,0:T(8,128)(2,1)S(1)}, bf16[224,256]{1,0:T(8,128)(2,1)S(1)}, u32[]{:S(2)}, u32[]{:S(2)}) collective-permute-start(bf16[224,256]{1,0:T(8,128)(2,1)S(1)} %add_convert_fusion.filt_ref), channel_id=1, source_target_pairs={{0,64},{32,96},{64,0},{96,32},{1,65},{33,97},{65,1},{97,33},{2,66}... | collective-permute-start | bytes 344072 | tf_op jit(solution)/shard_map/ppermute | solution.py:380

commit v6 on v5

--- a/solution.py
+++ b/solution.py
@@ -93,6 +93,10 @@
         pack[16 * planes : 16 * planes + 16, :] = bias
 
 
+def odd_slab():
+    return jnp.bitwise_and(lax.axis_index("space"), 1) == 1
+
+
 def upstream(packs, d):
     rows = slice(16 * d, 16 * d + 16)
     return jnp.concatenate([unfold(pack[rows, :].astype(F32)) for pack in packs], 0)
@@ -121,8 +125,9 @@
 def forward_kernel(
     planes, x_ref, w_ref, *refs
 ):
-    packs, (own_ref, low_ref, high_ref, up_ref, down_ref) = refs[:RING], refs[RING : RING + 5]
-    maps = refs[RING + 5 :]
+    packs, (own_ref, low_ref, high_ref, far_ref, near_ref) = refs[:RING], refs[RING : RING + 5]
+    maps, edges = refs[RING + 5 : 2 * RING + 5], refs[2 * RING + 5 :]
+    down_ref, up_ref = edges
     for m in range(RING):
         w = w_ref[m * TAP_ROWS : (m + 1) * TAP_ROWS, :]
         maps[m][...] = jnp.dot(w, x_ref[...], preferred_element_type=F32)
@@ -150,41 +155,46 @@
         total = jnp.concatenate(pieces, 0)
         if out < 0:
             low_ref[...] = total
-            down_ref[:, 0:INNER] = total.astype(BF16)
+            down_ref[:, 0:INNER] = total
         elif out >= planes:
             high_ref[...] = total
-            up_ref[:, 0:INNER] = total.astype(BF16)
+            up_ref[:, 0:INNER] = total
         else:
             own_ref[:, out * INNER : (out + 1) * INNER] = total
         for edge, ref in ((planes - 1, up_ref), (0, down_ref)):
             if out == edge:
-                ref[:, INNER : 2 * INNER] = total.astype(BF16)
-                ref[:, 2 * INNER : 3 * INNER] = upstream(packs, out).astype(BF16)
+                ref[:, INNER : 2 * INNER] = total
+                ref[:, 2 * INNER : 3 * INNER] = upstream(packs, out)
+    down, up = down_ref[...], up_ref[...]
+    near_ref[...] = jnp.where(odd_slab(), down, up).astype(BF16)
+    far_ref[...] = jnp.where(odd_slab(), up, down).astype(BF16)
 
 
 def backward_kernel(
-    planes, x_ref, own_ref, low_ref, high_ref, before_ref, after_ref, turned_ref, *refs
+    planes, x_ref, own_ref, low_ref, high_ref, far_ref, near_ref, turned_ref, *refs
 ):
     packs, part_any, backs = refs[:RING], refs[RING], refs[RING + 1 : 2 * RING + 1]
     bank, (shifted, part, sems) = refs[2 * RING + 1 : 3 * RING + 1], refs[3 * RING + 1 :]
     bias = offsets(packs, planes)
+    near, far = swapped(near_ref[...].astype(F32)), swapped(far_ref[...].astype(F32))
+    before, after = jnp.where(odd_slab(), near, far), jnp.where(odd_slab(), far, near)
     masks = {kw: inside_row(BLOCK, kw) for kw in (-1, 1)}
     for m in range(RING):
         bank[m][TAP_ROWS - BLOCK : TAP_ROWS, :] = jnp.zeros((BLOCK, planes * OUTER), F32)
     for src in range(-1, planes + 1):
         if src < 0:
-            pre = swapped(before_ref[:, INNER : 2 * INNER].astype(F32)) + low_ref[...]
-            cot = swapped(before_ref[:, 2 * INNER : 3 * INNER].astype(F32))
+            pre = before[:, INNER : 2 * INNER] + low_ref[...]
+            cot = before[:, 2 * INNER : 3 * INNER]
         elif src >= planes:
-            pre = swapped(after_ref[:, INNER : 2 * INNER].astype(F32)) + high_ref[...]
-            cot = swapped(after_ref[:, 2 * INNER : 3 * INNER].astype(F32))
+            pre = after[:, INNER : 2 * INNER] + high_ref[...]
+            cot = after[:, 2 * INNER : 3 * INNER]
         else:
             pre = own_ref[:, src * INNER : (src + 1) * INNER]
             cot = upstream(packs, src)
             if src == 0:
-                pre = pre + swapped(before_ref[:, 0:INNER].astype(F32))
+                pre = pre + before[:, 0:INNER]
             if src == planes - 1:
-                pre = pre + swapped(after_ref[:, 0:INNER].astype(F32))
+                pre = pre + after[:, 0:INNER]
         pre = pre + bias
         s = jax.nn.sigmoid(pre)
         if 0 <= src < planes:
@@ -335,21 +345,22 @@
         RING * TAP_ROWS * WIDE * 4,
         "prepare",
     )
-    own, low, high, up, down = call(
+    own, low, high, far, near = call(
         functools.partial(forward_kernel, planes),
         (x, w, *packs),
         [((group, inner), F32), plane, plane, edge, edge],
-        [pltpu.VMEM((TAP_ROWS, outer), F32)] * RING,
+        [pltpu.VMEM((TAP_ROWS, outer), F32)] * RING + [pltpu.VMEM((group, 3 * INNER), F32)] * 2,
         flops,
         2 * channels * outer,
         "conv_forward",
     )
-    before = lax.ppermute(up, "space", [(i, i + 1) for i in range(slabs - 1)])
-    after = lax.ppermute(down, "space", [(i + 1, i) for i in range(slabs - 1)])
+    inner_slabs = [(s, s + 1 - 2 * (1 - s % 2)) for s in range(1, slabs - 1)]
+    far = lax.ppermute(far, "space", inner_slabs)
+    near = lax.ppermute(near, "space", [(s, s ^ 1) for s in range(slabs)])
     back = ((TAP_ROWS + 16 * planes, WIDE), BF16)
     part, *backs = call(
         functools.partial(backward_kernel, planes),
-        (x, own, low, high, before, after, turned, *packs),
+        (x, own, low, high, far, near, turned, *packs),
         [((channels, outer), BF16)] + [back] * RING,
         [pltpu.VMEM((TAP_ROWS, outer), F32)] * RING
         + [

time: 73.2 us -> 69.3 us (0.947)
  waiting for transfers between devices: 23.5 us -> 18.2 us
  starting transfers between devices: 39.7 us -> 40.8 us
    ppermute x2, waiting for transfers between devices: 5.5 us -> 2.2 us  [the longest x1 2.19 us: per_device(): far = lax.ppermute(far, 'space', inner_slabs)]
    all_to_all x1, waiting for transfers between devices: 2.15 us -> 0.01 us  [per_device(): lax.all_to_all(part.reshape(parts, block, outer), 'filt', 0, 0, tiled=True)]
    ppermute x2, starting transfers between devices: 10.1 us -> 8.23 us  [the longest x1 8.15 us: per_device(): far = lax.ppermute(far, 'space', inner_slabs)]
    ppermute x1, starting transfers between devices: 2.43 us -> 4.22 us  [per_device(): other = lax.ppermute(filt, 'space', by(2))]
    ppermute x1, starting transfers between devices: 0.01 us -> 1.17 us  [per_device(): other = lax.ppermute(filt, 'space', by(1))]
    ppermute x8, waiting for transfers between devices: 6.52 us -> 7.27 us  [to_slot(): return lax.ppermute(value, ('space', 'filt'), pairs) if slot else value]
where the time goes in v6:
time: 69.3 us; the launch traced here: 68.6 us
  starting transfers between devices  40.8 us (59%)
  waiting for transfers between devices  18.2 us (26%)
  Pallas kernels  8.81 us (13%)
  between operations  0.76 us (1%)
    ppermute x8, starting transfers between devices, to_slot(): return lax.ppermute(value, ('space', 'filt'), pairs) if slot else value  12.8 us
    pallas_call x6, Pallas kernels, call(): pl.pallas_call(kernel, out_shape=shapes, in_specs=[smem if x.dtype == jnp...  8.81 us
    ppermute x1, starting transfers between devices, per_device(): far = lax.ppermute(far, 'space', inner_slabs)  8.15 us
    ppermute x1, waiting for transfers between devices, per_device(): other = lax.ppermute(filt, 'space', by(2))  7.72 us
    ppermute x8, waiting for transfers between devices, to_slot(): return lax.ppermute(value, ('space', 'filt'), pairs) if slot else value  7.27 us
    all_to_all x1, starting transfers between devices, per_device(): lax.all_to_all(chunks, 'filt', 0, 0, tiled=True).reshape(channels, outer)  6.81 us
    all_to_all x1, starting transfers between devices, per_device(): lax.all_to_all(part.reshape(parts, block, outer), 'filt', 0, 0, tiled=True)  5.09 us
    ppermute x1, starting transfers between devices, per_device(): other = lax.ppermute(filt, 'space', by(2))  4.22 us
  transfers between devices with their start and end apart: 15, of which 6 were waited for; matrix products, arithmetic and copies ran while one was open for 0% of the time, Pallas kernels for 4%

profile of v6, /device:TPU:1, one launch (start us, length us, event | category | flops | bytes accessed | tf_op | source)
XLA Modules:
  0.0 68.6 jit_solution(12289561447260725972)
XLA Ops:
  0.6 3.4 %collective-permute-start = (bf16[216,256]{1,0:T(8,128)(2,1)}, bf16[216,256]{1,0:T(8,128)(2,1)S(1)}, u32[]{:S(2)}, u32[]{:S(2)}) collective-permute-start(bf16[216,256]{1,0:T(8,128)(2,1)} %bitcast.15), channel_id=1, source_target_pairs={{0,1},{1,0},{2,3},{3,2},{4,5},{5,4},{6,7},{7,6},{8,9},{9,8},{10,11... | collective-permute-start | bytes 331784 | tf_op jit(solution)/shard_map/ppermute | solution.py:311
  4.0 2.0 %pack.1 = (bf16[32,8,1920]{2,1,0:T(8,128)(2,1)}, bf16[64,256]{1,0:T(8,128)(2,1)}, bf16[64,256]{1,0:T(8,128)(2,1)}, bf16[64,256]{1,0:T(8,128)(2,1)}, bf16[64,256]{1,0:T(8,128)(2,1)}) custom-call(bf16[8,6144]{1,0:T(8,128)(2,1)} %bitcast.18, bf16[8,6144]{1,0:T(8,128)(2,1)} %bitcast.19, bf16[1,8]{1,0:T(2,128)(2,1)} %bitcast.20), custom_call_target="tpu_custom_call" | custom-call | bytes 983040 | tf_op jit(solution)/shard_map/pack/pallas_call | solution.py:282
  6.1 6.8 %all-to-all-start = ((bf16[32,8,1920]{2,1,0:T(8,128)(2,1)}), bf16[32,8,1920]{2,1,0:T(8,128)(2,1)S(1)}, u32[]{:S(2)}, u32[]{:S(2)}) async-start(bf16[32,8,1920]{2,1,0:T(8,128)(2,1)} %get-tuple-element.24), calls=%async_computation | async-start | bytes 1966080 | tf_op jit(solution)/shard_map/all_to_all | solution.py:334
  12.9 2.8 %collective-permute-start.1 = (bf16[216,256]{1,0:T(8,128)(2,1)S(1)}, bf16[216,256]{1,0:T(8,128)(2,1)S(1)}, u32[]{:S(2)}, u32[]{:S(2)}) collective-permute-start(bf16[216,256]{1,0:T(8,128)(2,1)S(1)} %bitcast.16), channel_id=1, source_target_pairs={{0,2},{1,3},{2,0},{3,1},{4,6},{5,7},{6,4},{7,5},{8,10},{9,11},{10,... | collective-permute-start | bytes 331784 | tf_op jit(solution)/shard_map/ppermute | solution.py:311
  15.7 2.5 %collective-permute-start.2 = (bf16[216,256]{1,0:T(8,128)(2,1)S(1)}, bf16[216,256]{1,0:T(8,128)(2,1)S(1)}, u32[]{:S(2)}, u32[]{:S(2)}) collective-permute-start(bf16[216,256]{1,0:T(8,128)(2,1)S(1)} %collective-permute-done.refs_1_), channel_id=1, source_target_pairs={{0,32},{32,0},{64,96},{96,64},{1,33},{33,1},{65,97},{97,65},{2,34}... | collective-permute-start | bytes 331784 | tf_op jit(solution)/shard_map/ppermute | solution.py:333
  18.2 0.9 %collective-permute-start.3 = (bf16[64,256]{1,0:T(8,128)(2,1)S(1)}, bf16[64,256]{1,0:T(8,128)(2,1)S(1)}, u32[]{:S(2)}, u32[]{:S(2)}) collective-permute-start(bf16[64,256]{1,0:T(8,128)(2,1)S(1)} %copy-done.4), channel_id=1, source_target_pairs={{0,1},{1,0},{2,3},{3,2},{4,5},{5,4},{6,7},{7,6},{8,9},{9,8},{10,11... | collective-permute-start | bytes 98312 | tf_op jit(solution)/shard_map/ppermute | solution.py:311
  19.1 1.2 %collective-permute-start.4 = (bf16[64,256]{1,0:T(8,128)(2,1)S(1)}, bf16[64,256]{1,0:T(8,128)(2,1)S(1)}, u32[]{:S(2)}, u32[]{:S(2)}) collective-permute-start(bf16[64,256]{1,0:T(8,128)(2,1)S(1)} %copy-done.3), channel_id=1, source_target_pairs={{0,2},{1,3},{2,0},{3,1},{4,6},{5,7},{6,4},{7,5},{8,10},{9,11},{10,... | collective-permute-start | bytes 98312 | tf_op jit(solution)/shard_map/ppermute | solution.py:311
  20.3 1.2 %collective-permute-start.5 = (bf16[64,256]{1,0:T(8,128)(2,1)S(1)}, bf16[64,256]{1,0:T(8,128)(2,1)S(1)}, u32[]{:S(2)}, u32[]{:S(2)}) collective-permute-start(bf16[64,256]{1,0:T(8,128)(2,1)S(1)} %copy-done.2), channel_id=1, source_target_pairs={{0,3},{1,2},{2,1},{3,0},{4,7},{5,6},{6,5},{7,4},{8,11},{9,10},{10,... | collective-permute-start | bytes 98312 | tf_op jit(solution)/shard_map/ppermute | solution.py:311
  21.5 6.0 %collective-permute-done.1.refs_2_ = bf16[216,256]{1,0:T(8,128)(2,1)S(1)} collective-permute-done((bf16[216,256]{1,0:T(8,128)(2,1)S(1)}, bf16[216,256]{1,0:T(8,128)(2,1)S(1)}, u32[]{:S(2)}, u32[]{:S(2)}) %collective-permute-start.1) | collective-permute-done | bytes 110624 | tf_op jit(solution)/shard_map/ppermute | solution.py:311
  28.2 1.4 %conv_forward.1 = (f32[32,1536]{1,0:T(8,128)S(1)}, f32[32,512]{1,0:T(8,128)S(1)}, f32[32,512]{1,0:T(8,128)S(1)}, bf16[32,1536]{1,0:T(8,128)(2,1)S(1)}, bf16[32,1536]{1,0:T(8,128)(2,1)S(1)}) custom-call(bf16[256,1920]{1,0:T(8,128)(2,1)S(1)} %bitcast.13, bf16[896,256]{1,0:T(8,128)(2,1)S(1)} %get-tuple-element.25.w_ref, bf16[64,256]{1,0:T(8,128)(2,1)S(1)} %copy-done.1, ...), custom_call_target="tpu_custom_call" | custom-call | flops 880803840 | bytes 983040 | tf_op jit(solution)/shard_map/conv_forward/pallas_call | solution.py:282
  29.6 8.1 %collective-permute-start.6 = (bf16[32,1536]{1,0:T(8,128)(2,1)S(1)}, bf16[32,1536]{1,0:T(8,128)(2,1)S(1)}, u32[]{:S(2)}, u32[]{:S(2)}) collective-permute-start(bf16[32,1536]{1,0:T(8,128)(2,1)S(1)} %get-tuple-element.33), channel_id=1, source_target_pairs={{32,64},{64,32},{33,65},{65,33},{34,66},{66,34},{35,67},{67,35},{3... | collective-permute-start | bytes 294920 | tf_op jit(solution)/shard_map/ppermute | solution.py:358
  37.8 2.2 %collective-permute-done.6.far_ref = bf16[32,1536]{1,0:T(8,128)(2,1)S(1)} collective-permute-done((bf16[32,1536]{1,0:T(8,128)(2,1)S(1)}, bf16[32,1536]{1,0:T(8,128)(2,1)S(1)}, u32[]{:S(2)}, u32[]{:S(2)}) %collective-permute-start.6) | collective-permute-done | bytes 98336 | tf_op jit(solution)/shard_map/ppermute | solution.py:358
  40.0 3.8 %conv_backward.1 = (bf16[256,1920]{1,0:T(8,128)(2,1)}, bf16[272,256]{1,0:T(8,128)(2,1)S(1)}, bf16[272,256]{1,0:T(8,128)(2,1)S(1)}, bf16[272,256]{1,0:T(8,128)(2,1)S(1)}, bf16[272,256]{1,0:T(8,128)(2,1)S(1)}) custom-call(bf16[256,1920]{1,0:T(8,128)(2,1)S(1)} %bitcast.14, f32[32,1536]{1,0:T(8,128)S(1)} %get-tuple-element.30.own_ref, ...), custom_call_target="tpu_custom_call" | custom-call | flops 1761607680 | bytes 1966080 | tf_op jit(solution)/shard_map/conv_backward/pallas_call | solution.py:282
  43.8 0.9 %collective-permute-start.8 = (bf16[272,256]{1,0:T(8,128)(2,1)S(1)}, bf16[272,256]{1,0:T(8,128)(2,1)S(1)}, u32[]{:S(2)}, u32[]{:S(2)}) collective-permute-start(bf16[272,256]{1,0:T(8,128)(2,1)S(1)} %get-tuple-element.37), channel_id=1, source_target_pairs={{0,1},{1,0},{2,3},{3,2},{4,5},{5,4},{6,7},{7,6},{8,9},{9,8},{10,11... | collective-permute-start | bytes 417800 | tf_op jit(solution)/shard_map/ppermute | solution.py:311
  44.7 1.3 %collective-permute-start.9 = (bf16[272,256]{1,0:T(8,128)(2,1)S(1)}, bf16[272,256]{1,0:T(8,128)(2,1)S(1)}, u32[]{:S(2)}, u32[]{:S(2)}) collective-permute-start(bf16[272,256]{1,0:T(8,128)(2,1)S(1)} %get-tuple-element.38), channel_id=1, source_target_pairs={{0,2},{1,3},{2,0},{3,1},{4,6},{5,7},{6,4},{7,5},{8,10},{9,11},{10,... | collective-permute-start | bytes 417800 | tf_op jit(solution)/shard_map/ppermute | solution.py:311
  46.0 1.1 %collective-permute-start.10 = (bf16[272,256]{1,0:T(8,128)(2,1)S(1)}, bf16[272,256]{1,0:T(8,128)(2,1)S(1)}, u32[]{:S(2)}, u32[]{:S(2)}) collective-permute-start(bf16[272,256]{1,0:T(8,128)(2,1)S(1)} %get-tuple-element.39), channel_id=1, source_target_pairs={{0,3},{1,2},{2,1},{3,0},{4,7},{5,6},{6,5},{7,4},{8,11},{9,10},{10,... | collective-permute-start | bytes 417800 | tf_op jit(solution)/shard_map/ppermute | solution.py:311
  47.1 5.1 %all-to-all-start.1 = ((bf16[32,8,1920]{2,1,0:T(8,128)(2,1)}), bf16[32,8,1920]{2,1,0:T(8,128)(2,1)S(1)}, u32[]{:S(2)}, u32[]{:S(2)}) async-start(bf16[32,8,1920]{2,1,0:T(8,128)(2,1)} %bitcast.8), calls=%async_computation.1 | async-start | bytes 1966080 | tf_op jit(solution)/shard_map/all_to_all | solution.py:378
  52.2 0.8 %collective-permute-done.8.refs_1_ = bf16[272,256]{1,0:T(8,128)(2,1)S(1)} collective-permute-done((bf16[272,256]{1,0:T(8,128)(2,1)S(1)}, bf16[272,256]{1,0:T(8,128)(2,1)S(1)}, u32[]{:S(2)}, u32[]{:S(2)}) %collective-permute-start.8) | collective-permute-done | bytes 139296 | tf_op jit(solution)/shard_map/ppermute | solution.py:311
  53.0 0.7 unpack.1
  53.6 1.2 %collective-permute-start.11 = (bf16[224,256]{1,0:T(8,128)(2,1)S(1)}, bf16[224,256]{1,0:T(8,128)(2,1)S(1)}, u32[]{:S(2)}, u32[]{:S(2)}) collective-permute-start(bf16[224,256]{1,0:T(8,128)(2,1)S(1)} %get-tuple-element.42), channel_id=1, source_target_pairs={{0,32},{32,0},{64,96},{96,64},{1,33},{33,1},{65,97},{97,65},{2,34}... | collective-permute-start | bytes 344072 | tf_op jit(solution)/shard_map/ppermute | solution.py:389
  54.8 1.0 %collective-permute-done.11 = bf16[224,256]{1,0:T(8,128)(2,1)S(1)} collective-permute-done((bf16[224,256]{1,0:T(8,128)(2,1)S(1)}, bf16[224,256]{1,0:T(8,128)(2,1)S(1)}, u32[]{:S(2)}, u32[]{:S(2)}) %collective-permute-start.11) | collective-permute-done | bytes 114720 | tf_op jit(solution)/shard_map/ppermute | solution.py:389
  55.8 4.2 %collective-permute-start.12 = (bf16[224,256]{1,0:T(8,128)(2,1)S(1)}, bf16[224,256]{1,0:T(8,128)(2,1)S(1)}, u32[]{:S(2)}, u32[]{:S(2)}) collective-permute-start(bf16[224,256]{1,0:T(8,128)(2,1)S(1)} %add_convert_fusion.filt_ref), channel_id=1, source_target_pairs={{0,64},{32,96},{64,0},{96,32},{1,65},{33,97},{65,1},{97,33},{2,66}... | collective-permute-start | bytes 344072 | tf_op jit(solution)/shard_map/ppermute | solution.py:391
  60.0 7.7 %collective-permute-done.12.other_ref = bf16[224,256]{1,0:T(8,128)(2,1)S(1)} collective-permute-done((bf16[224,256]{1,0:T(8,128)(2,1)S(1)}, bf16[224,256]{1,0:T(8,128)(2,1)S(1)}, u32[]{:S(2)}, u32[]{:S(2)}) %collective-permute-start.12) | collective-permute-done | bytes 114720 | tf_op jit(solution)/shard_map/ppermute | solution.py:391
  67.8 0.8 %collect.1 = (bf16[8,6144]{1,0:T(8,128)(2,1)}, f32[216,256]{1,0:T(8,128)}) custom-call(bf16[32,8,1920]{2,1,0:T(8,128)(2,1)S(1)} %all-to-all-done.1.got_ref, bf16[224,256]{1,0:T(8,128)(2,1)S(1)} %add_convert_fusion.filt_ref, bf16[224,256]{1,0:T(8,128)(2,1)S(1)} %collective-permute-done.12.other_ref), custom_call_target="tpu_custom_call" | custom-call | bytes 983040 | tf_op jit(solution)/shard_map/collect/pallas_call | solution.py:282
  (23 shorter events, 0.8 us)
Async XLA Ops:
  0.6 15.1 %collective-permute-start = (bf16[216,256]{1,0:T(8,128)(2,1)}, bf16[216,256]{1,0:T(8,128)(2,1)S(1)}, u32[]{:S(2)}, u32[]{:S(2)}) collective-permute-start(bf16[216,256]{1,0:T(8,128)(2,1)} %bitcast.15), channel_id=1, source_target_pairs={{0,1},{1,0},{2,3},{3,2},{4,5},{5,4},{6,7},{7,6},{8,9},{9,8},{10,11... | collective-permute-start | bytes 331784 | tf_op jit(solution)/shard_map/ppermute | solution.py:311
  6.0 6.9 %copy-start = (bf16[8,27,256]{2,0,1:T(8,128)(2,1)S(1)}, bf16[8,27,256]{2,0,1:T(8,128)(2,1)}, u32[]{:S(2)}) copy-start(bf16[8,27,256]{2,0,1:T(8,128)(2,1)} %param.5) | copy-start | bytes 331780
  6.0 12.1 %copy-start.4 = (bf16[64,256]{1,0:T(8,128)(2,1)S(1)}, bf16[64,256]{1,0:T(8,128)(2,1)}, u32[]{:S(2)}) copy-start(bf16[64,256]{1,0:T(8,128)(2,1)} %get-tuple-element.27) | copy-start | bytes 98308
  6.1 13.0 %copy-start.3 = (bf16[64,256]{1,0:T(8,128)(2,1)S(1)}, bf16[64,256]{1,0:T(8,128)(2,1)}, u32[]{:S(2)}) copy-start(bf16[64,256]{1,0:T(8,128)(2,1)} %get-tuple-element.28) | copy-start | bytes 98308
  6.1 14.2 %copy-start.2 = (bf16[64,256]{1,0:T(8,128)(2,1)S(1)}, bf16[64,256]{1,0:T(8,128)(2,1)}, u32[]{:S(2)}) copy-start(bf16[64,256]{1,0:T(8,128)(2,1)} %get-tuple-element.29) | copy-start | bytes 98308
  6.1 22.1 %all-to-all-start = ((bf16[32,8,1920]{2,1,0:T(8,128)(2,1)}), bf16[32,8,1920]{2,1,0:T(8,128)(2,1)S(1)}, u32[]{:S(2)}, u32[]{:S(2)}) async-start(bf16[32,8,1920]{2,1,0:T(8,128)(2,1)} %get-tuple-element.24), calls=%async_computation | async-start | bytes 1966080 | tf_op jit(solution)/shard_map/all_to_all | solution.py:334
  12.9 14.5 %collective-permute-start.1 = (bf16[216,256]{1,0:T(8,128)(2,1)S(1)}, bf16[216,256]{1,0:T(8,128)(2,1)S(1)}, u32[]{:S(2)}, u32[]{:S(2)}) collective-permute-start(bf16[216,256]{1,0:T(8,128)(2,1)S(1)} %bitcast.16), channel_id=1, source_target_pairs={{0,2},{1,3},{2,0},{3,1},{4,6},{5,7},{6,4},{7,5},{8,10},{9,11},{10,... | collective-permute-start | bytes 331784 | tf_op jit(solution)/shard_map/ppermute | solution.py:311
  15.7 11.7 %collective-permute-start.2 = (bf16[216,256]{1,0:T(8,128)(2,1)S(1)}, bf16[216,256]{1,0:T(8,128)(2,1)S(1)}, u32[]{:S(2)}, u32[]{:S(2)}) collective-permute-start(bf16[216,256]{1,0:T(8,128)(2,1)S(1)} %collective-permute-done.refs_1_), channel_id=1, source_target_pairs={{0,32},{32,0},{64,96},{96,64},{1,33},{33,1},{65,97},{97,65},{2,34}... | collective-permute-start | bytes 331784 | tf_op jit(solution)/shard_map/ppermute | solution.py:333
  18.2 9.5 %collective-permute-start.3 = (bf16[64,256]{1,0:T(8,128)(2,1)S(1)}, bf16[64,256]{1,0:T(8,128)(2,1)S(1)}, u32[]{:S(2)}, u32[]{:S(2)}) collective-permute-start(bf16[64,256]{1,0:T(8,128)(2,1)S(1)} %copy-done.4), channel_id=1, source_target_pairs={{0,1},{1,0},{2,3},{3,2},{4,5},{5,4},{6,7},{7,6},{8,9},{9,8},{10,11... | collective-permute-start | bytes 98312 | tf_op jit(solution)/shard_map/ppermute | solution.py:311
  19.1 9.1 %collective-permute-start.4 = (bf16[64,256]{1,0:T(8,128)(2,1)S(1)}, bf16[64,256]{1,0:T(8,128)(2,1)S(1)}, u32[]{:S(2)}, u32[]{:S(2)}) collective-permute-start(bf16[64,256]{1,0:T(8,128)(2,1)S(1)} %copy-done.3), channel_id=1, source_target_pairs={{0,2},{1,3},{2,0},{3,1},{4,6},{5,7},{6,4},{7,5},{8,10},{9,11},{10,... | collective-permute-start | bytes 98312 | tf_op jit(solution)/shard_map/ppermute | solution.py:311
  20.3 7.9 %copy-start.1 = (bf16[64,256]{1,0:T(8,128)(2,1)S(1)}, bf16[64,256]{1,0:T(8,128)(2,1)}, u32[]{:S(2)}) copy-start(bf16[64,256]{1,0:T(8,128)(2,1)} %get-tuple-element.26.refs_0_) | copy-start | bytes 98308
  20.3 7.9 %collective-permute-start.5 = (bf16[64,256]{1,0:T(8,128)(2,1)S(1)}, bf16[64,256]{1,0:T(8,128)(2,1)S(1)}, u32[]{:S(2)}, u32[]{:S(2)}) collective-permute-start(bf16[64,256]{1,0:T(8,128)(2,1)S(1)} %copy-done.2), channel_id=1, source_target_pairs={{0,3},{1,2},{2,1},{3,0},{4,7},{5,6},{6,5},{7,4},{8,11},{9,10},{10,... | collective-permute-start | bytes 98312 | tf_op jit(solution)/shard_map/ppermute | solution.py:311
  29.6 10.4 %collective-permute-start.6 = (bf16[32,1536]{1,0:T(8,128)(2,1)S(1)}, bf16[32,1536]{1,0:T(8,128)(2,1)S(1)}, u32[]{:S(2)}, u32[]{:S(2)}) collective-permute-start(bf16[32,1536]{1,0:T(8,128)(2,1)S(1)} %get-tuple-element.33), channel_id=1, source_target_pairs={{32,64},{64,32},{33,65},{65,33},{34,66},{66,34},{35,67},{67,35},{3... | collective-permute-start | bytes 294920 | tf_op jit(solution)/shard_map/ppermute | solution.py:358
  37.7 2.3 %collective-permute-start.7 = (bf16[32,1536]{1,0:T(8,128)(2,1)S(1)}, bf16[32,1536]{1,0:T(8,128)(2,1)S(1)}, u32[]{:S(2)}, u32[]{:S(2)}) collective-permute-start(bf16[32,1536]{1,0:T(8,128)(2,1)S(1)} %get-tuple-element.34), channel_id=1, source_target_pairs={{0,32},{32,0},{64,96},{96,64},{1,33},{33,1},{65,97},{97,65},{2,34}... | collective-permute-start | bytes 294920 | tf_op jit(solution)/shard_map/ppermute | solution.py:359
  43.8 9.2 %collective-permute-start.8 = (bf16[272,256]{1,0:T(8,128)(2,1)S(1)}, bf16[272,256]{1,0:T(8,128)(2,1)S(1)}, u32[]{:S(2)}, u32[]{:S(2)}) collective-permute-start(bf16[272,256]{1,0:T(8,128)(2,1)S(1)} %get-tuple-element.37), channel_id=1, source_target_pairs={{0,1},{1,0},{2,3},{3,2},{4,5},{5,4},{6,7},{7,6},{8,9},{9,8},{10,11... | collective-permute-start | bytes 417800 | tf_op jit(solution)/shard_map/ppermute | solution.py:311
  44.7 8.3 %collective-permute-start.9 = (bf16[272,256]{1,0:T(8,128)(2,1)S(1)}, bf16[272,256]{1,0:T(8,128)(2,1)S(1)}, u32[]{:S(2)}, u32[]{:S(2)}) collective-permute-start(bf16[272,256]{1,0:T(8,128)(2,1)S(1)} %get-tuple-element.38), channel_id=1, source_target_pairs={{0,2},{1,3},{2,0},{3,1},{4,6},{5,7},{6,4},{7,5},{8,10},{9,11},{10,... | collective-permute-start | bytes 417800 | tf_op jit(solution)/shard_map/ppermute | solution.py:311
  46.0 7.0 %collective-permute-start.10 = (bf16[272,256]{1,0:T(8,128)(2,1)S(1)}, bf16[272,256]{1,0:T(8,128)(2,1)S(1)}, u32[]{:S(2)}, u32[]{:S(2)}) collective-permute-start(bf16[272,256]{1,0:T(8,128)(2,1)S(1)} %get-tuple-element.39), channel_id=1, source_target_pairs={{0,3},{1,2},{2,1},{3,0},{4,7},{5,6},{6,5},{7,4},{8,11},{9,10},{10,... | collective-permute-start | bytes 417800 | tf_op jit(solution)/shard_map/ppermute | solution.py:311
  47.1 20.6 %all-to-all-start.1 = ((bf16[32,8,1920]{2,1,0:T(8,128)(2,1)}), bf16[32,8,1920]{2,1,0:T(8,128)(2,1)S(1)}, u32[]{:S(2)}, u32[]{:S(2)}) async-start(bf16[32,8,1920]{2,1,0:T(8,128)(2,1)} %bitcast.8), calls=%async_computation.1 | async-start | bytes 1966080 | tf_op jit(solution)/shard_map/all_to_all | solution.py:378
  53.6 2.1 %collective-permute-start.11 = (bf16[224,256]{1,0:T(8,128)(2,1)S(1)}, bf16[224,256]{1,0:T(8,128)(2,1)S(1)}, u32[]{:S(2)}, u32[]{:S(2)}) collective-permute-start(bf16[224,256]{1,0:T(8,128)(2,1)S(1)} %get-tuple-element.42), channel_id=1, source_target_pairs={{0,32},{32,0},{64,96},{96,64},{1,33},{33,1},{65,97},{97,65},{2,34}... | collective-permute-start | bytes 344072 | tf_op jit(solution)/shard_map/ppermute | solution.py:389
  55.8 11.9 %collective-permute-start.12 = (bf16[224,256]{1,0:T(8,128)(2,1)S(1)}, bf16[224,256]{1,0:T(8,128)(2,1)S(1)}, u32[]{:S(2)}, u32[]{:S(2)}) collective-permute-start(bf16[224,256]{1,0:T(8,128)(2,1)S(1)} %add_convert_fusion.filt_ref), channel_id=1, source_target_pairs={{0,64},{32,96},{64,0},{96,32},{1,65},{33,97},{65,1},{97,33},{2,66}... | collective-permute-start | bytes 344072 | tf_op jit(solution)/shard_map/ppermute | solution.py:391

commit v7 on v6

--- a/solution.py
+++ b/solution.py
@@ -17,6 +17,7 @@
 INNER = ROWS * W
 OUTER = INNER + 2 * W
 BLOCK = 8
+GROUP = RING * BLOCK
 WIDE = 256
 TAP_ROWS = 224
 PACK = 0
@@ -116,43 +117,38 @@
 
 def prepare_kernel(*refs):
     taps, (w_ref, turned_ref) = refs[:RING], refs[RING:]
-    for m in range(RING):
-        w = jnp.concatenate([taps[m][...].astype(F32), jnp.zeros((BLOCK, WIDE), F32)], 0)
-        w_ref[m * TAP_ROWS : (m + 1) * TAP_ROWS, :] = w.astype(BF16)
+    w = [ref[...].astype(F32) for ref in taps]
+    for t in range(len(TAPS)):
+        rows = [x[t * BLOCK : (t + 1) * BLOCK] for x in w]
+        w_ref[t * GROUP : (t + 1) * GROUP, :] = jnp.concatenate(rows, 0).astype(BF16)
+    end = len(TAPS) * GROUP
+    w_ref[end:, :] = jnp.zeros((w_ref.shape[0] - end, WIDE), BF16)
     turned_ref[...] = w_ref[...].T
 
 
-def forward_kernel(
-    planes, x_ref, w_ref, *refs
-):
+def forward_kernel(planes, x_ref, w_ref, *refs):
     packs, (own_ref, low_ref, high_ref, far_ref, near_ref) = refs[:RING], refs[RING : RING + 5]
-    maps, edges = refs[RING + 5 : 2 * RING + 5], refs[2 * RING + 5 :]
-    down_ref, up_ref = edges
-    for m in range(RING):
-        w = w_ref[m * TAP_ROWS : (m + 1) * TAP_ROWS, :]
-        maps[m][...] = jnp.dot(w, x_ref[...], preferred_element_type=F32)
-    masks = {kw: inside_row(BLOCK, kw) for kw in (-1, 1)}
+    maps, down_ref, up_ref = refs[RING + 5 :]
+    maps[...] = jnp.dot(w_ref[...], x_ref[...], preferred_element_type=F32)
+    masks = {kw: inside_row(GROUP, kw) for kw in (-1, 1)}
     for out in range(-1, planes + 1):
-        pieces = []
-        for m in range(RING):
-            total = None
-            for kh in (-1, 0, 1):
-                line = None
-                for kw in (-1, 0, 1):
-                    term = None
-                    for kd in (-1, 0, 1):
-                        if 0 <= out + kd < planes:
-                            at = TAPS.index((kd, kh, kw)) * BLOCK
-                            d = out + kd
-                            part = maps[m][at : at + BLOCK, d * OUTER : (d + 1) * OUTER]
-                            term = part if term is None else term + part
-                    if kw:
-                        term = jnp.where(masks[kw], moved(term, -kw), 0.0)
-                    line = term if line is None else line + term
-                line = moved(line, -kh * W)
-                total = line if total is None else total + line
-            pieces.append(total[:, :INNER])
-        total = jnp.concatenate(pieces, 0)
+        total = None
+        for kh in (-1, 0, 1):
+            line = None
+            for kw in (-1, 0, 1):
+                term = None
+                for kd in (-1, 0, 1):
+                    d = out + kd
+                    if 0 <= d < planes:
+                        at = TAPS.index((kd, kh, kw)) * GROUP
+                        part = maps[at : at + GROUP, d * OUTER : (d + 1) * OUTER]
+                        term = part if term is None else term + part
+                if kw:
+                    term = jnp.where(masks[kw], moved(term, -kw), 0.0)
+                line = term if line is None else line + term
+            line = moved(line, -kh * W)
+            total = line if total is None else total + line
+        total = total[:, :INNER]
         if out < 0:
             low_ref[...] = total
             down_ref[:, 0:INNER] = total
@@ -174,13 +170,13 @@
     planes, x_ref, own_ref, low_ref, high_ref, far_ref, near_ref, turned_ref, *refs
 ):
     packs, part_any, backs = refs[:RING], refs[RING], refs[RING + 1 : 2 * RING + 1]
-    bank, (shifted, part, sems) = refs[2 * RING + 1 : 3 * RING + 1], refs[3 * RING + 1 :]
+    shifted, part, sems = refs[2 * RING + 1 :]
     bias = offsets(packs, planes)
     near, far = swapped(near_ref[...].astype(F32)), swapped(far_ref[...].astype(F32))
     before, after = jnp.where(odd_slab(), near, far), jnp.where(odd_slab(), far, near)
-    masks = {kw: inside_row(BLOCK, kw) for kw in (-1, 1)}
-    for m in range(RING):
-        bank[m][TAP_ROWS - BLOCK : TAP_ROWS, :] = jnp.zeros((BLOCK, planes * OUTER), F32)
+    masks = {kw: inside_row(GROUP, kw) for kw in (-1, 1)}
+    end = len(TAPS) * GROUP
+    shifted[end:, :] = jnp.zeros((shifted.shape[0] - end, planes * OUTER), BF16)
     for src in range(-1, planes + 1):
         if src < 0:
             pre = before[:, INNER : 2 * INNER] + low_ref[...]
@@ -205,26 +201,18 @@
                 backs[m][at : at + 16, :] = fold(rows).astype(BF16)
         grad = (cot * (s * (1.0 + pre * (1.0 - s)))).astype(BF16).astype(F32)
         grad = jnp.concatenate([grad, jnp.zeros((grad.shape[0], 2 * W), F32)], 1)
-        for m in range(RING):
-            own = grad[m * BLOCK : (m + 1) * BLOCK]
-            for kh in (-1, 0, 1):
-                line = moved(own, kh * W)
-                for kw in (-1, 0, 1):
-                    term = line
-                    if kw:
-                        term = jnp.where(masks[-kw], moved(line, kw), 0.0)
-                    for kd in (-1, 0, 1):
-                        d = src + kd
-                        if 0 <= d < planes:
-                            at = TAPS.index((kd, kh, kw)) * BLOCK
-                            bank[m][at : at + BLOCK, d * OUTER : (d + 1) * OUTER] = term
-    for m in range(RING):
-        rows = slice(m * TAP_ROWS, (m + 1) * TAP_ROWS)
-        shifted[rows, :] = bank[m][...].astype(BF16)
-        filt = lax.dot_general(
-            shifted[rows, :], x_ref[...], (((1,), (1,)), ((), ())), preferred_element_type=F32
-        )
-        backs[m][0:TAP_ROWS, :] = filt.astype(BF16)
+        for kh in (-1, 0, 1):
+            line = moved(grad, kh * W)
+            for kw in (-1, 0, 1):
+                term = line
+                if kw:
+                    term = jnp.where(masks[-kw], moved(line, kw), 0.0)
+                term = term.astype(BF16)
+                for kd in (-1, 0, 1):
+                    d = src + kd
+                    if 0 <= d < planes:
+                        at = TAPS.index((kd, kh, kw)) * GROUP
+                        shifted[at : at + GROUP, d * OUTER : (d + 1) * OUTER] = term
     copies = []
     for d in range(planes):
         lanes = slice(d * OUTER, (d + 1) * OUTER)
@@ -232,6 +220,13 @@
         part[:, lanes] = total.astype(BF16)
         copies.append(pltpu.make_async_copy(part.at[:, lanes], part_any.at[:, lanes], sems.at[d]))
         copies[-1].start()
+    filt = lax.dot_general(
+        shifted[...], x_ref[...], (((1,), (1,)), ((), ())), preferred_element_type=F32
+    )
+    for m in range(RING):
+        rows = [t * GROUP + m * BLOCK for t in range(len(TAPS))]
+        pieces = [filt[at : at + BLOCK] for at in rows] + [jnp.zeros((BLOCK, WIDE), F32)]
+        backs[m][0:TAP_ROWS, :] = jnp.concatenate(pieces, 0).astype(BF16)
     for copy in copies:
         copy.wait()
 
@@ -349,7 +344,7 @@
         functools.partial(forward_kernel, planes),
         (x, w, *packs),
         [((group, inner), F32), plane, plane, edge, edge],
-        [pltpu.VMEM((TAP_ROWS, outer), F32)] * RING + [pltpu.VMEM((group, 3 * INNER), F32)] * 2,
+        [pltpu.VMEM((RING * TAP_ROWS, outer), F32)] + [pltpu.VMEM((group, 3 * INNER), F32)] * 2,
         flops,
         2 * channels * outer,
         "conv_forward",
@@ -362,8 +357,7 @@
         functools.partial(backward_kernel, planes),
         (x, own, low, high, far, near, turned, *packs),
         [((channels, outer), BF16)] + [back] * RING,
-        [pltpu.VMEM((TAP_ROWS, outer), F32)] * RING
-        + [
+        [
             pltpu.VMEM((RING * TAP_ROWS, outer), BF16),
             pltpu.VMEM((channels, outer), BF16),
             pltpu.SemaphoreType.DMA((planes,)),

time: 69.3 us -> 68.5 us (0.988)
  Pallas kernels: 8.81 us -> 8.06 us
    pallas_call x6, Pallas kernels: 8.81 us -> 8.06 us  [call(): pl.pallas_call(kernel, out_shape=shapes, in_specs=[smem if x.dtype == jnp...]
where the time goes in v7:
time: 68.5 us; the launch traced here: 67.8 us
  starting transfers between devices  40.8 us (60%)
  waiting for transfers between devices  18.2 us (27%)
  Pallas kernels  8.06 us (12%)
  between operations  0.76 us (1%)
    ppermute x8, starting transfers between devices, to_slot(): return lax.ppermute(value, ('space', 'filt'), pairs) if slot else value  12.8 us
    ppermute x1, starting transfers between devices, per_device(): far = lax.ppermute(far, 'space', inner_slabs)  8.14 us
    pallas_call x6, Pallas kernels, call(): pl.pallas_call(kernel, out_shape=shapes, in_specs=[smem if x.dtype == jnp...  8.06 us
    ppermute x1, waiting for transfers between devices, per_device(): other = lax.ppermute(filt, 'space', by(2))  7.72 us
    ppermute x8, waiting for transfers between devices, to_slot(): return lax.ppermute(value, ('space', 'filt'), pairs) if slot else value  7.27 us
    all_to_all x1, starting transfers between devices, per_device(): lax.all_to_all(chunks, 'filt', 0, 0, tiled=True).reshape(channels, outer)  6.81 us
    all_to_all x1, starting transfers between devices, per_device(): lax.all_to_all(part.reshape(parts, block, outer), 'filt', 0, 0, tiled=True)  5.09 us
    ppermute x1, starting transfers between devices, per_device(): other = lax.ppermute(filt, 'space', by(2))  4.21 us
  transfers between devices with their start and end apart: 15, of which 6 were waited for; matrix products, arithmetic and copies ran while one was open for 0% of the time, Pallas kernels for 4%

profile of v7, /device:TPU:1, one launch (start us, length us, event | category | flops | bytes accessed | tf_op | source)
XLA Modules:
  0.0 67.8 jit_solution(17220004109558483951)
XLA Ops:
  0.6 3.4 %collective-permute-start = (bf16[216,256]{1,0:T(8,128)(2,1)}, bf16[216,256]{1,0:T(8,128)(2,1)S(1)}, u32[]{:S(2)}, u32[]{:S(2)}) collective-permute-start(bf16[216,256]{1,0:T(8,128)(2,1)} %bitcast.15), channel_id=1, source_target_pairs={{0,1},{1,0},{2,3},{3,2},{4,5},{5,4},{6,7},{7,6},{8,9},{9,8},{10,11... | collective-permute-start | bytes 331784 | tf_op jit(solution)/shard_map/ppermute | solution.py:306
  4.0 2.0 %pack.1 = (bf16[32,8,1920]{2,1,0:T(8,128)(2,1)}, bf16[64,256]{1,0:T(8,128)(2,1)}, bf16[64,256]{1,0:T(8,128)(2,1)}, bf16[64,256]{1,0:T(8,128)(2,1)}, bf16[64,256]{1,0:T(8,128)(2,1)}) custom-call(bf16[8,6144]{1,0:T(8,128)(2,1)} %bitcast.18, bf16[8,6144]{1,0:T(8,128)(2,1)} %bitcast.19, bf16[1,8]{1,0:T(2,128)(2,1)} %bitcast.20), custom_call_target="tpu_custom_call" | custom-call | bytes 983040 | tf_op jit(solution)/shard_map/pack/pallas_call | solution.py:277
  6.1 6.8 %all-to-all-start = ((bf16[32,8,1920]{2,1,0:T(8,128)(2,1)}), bf16[32,8,1920]{2,1,0:T(8,128)(2,1)S(1)}, u32[]{:S(2)}, u32[]{:S(2)}) async-start(bf16[32,8,1920]{2,1,0:T(8,128)(2,1)} %get-tuple-element.24), calls=%async_computation | async-start | bytes 1966080 | tf_op jit(solution)/shard_map/all_to_all | solution.py:329
  12.9 2.8 %collective-permute-start.1 = (bf16[216,256]{1,0:T(8,128)(2,1)S(1)}, bf16[216,256]{1,0:T(8,128)(2,1)S(1)}, u32[]{:S(2)}, u32[]{:S(2)}) collective-permute-start(bf16[216,256]{1,0:T(8,128)(2,1)S(1)} %bitcast.16), channel_id=1, source_target_pairs={{0,2},{1,3},{2,0},{3,1},{4,6},{5,7},{6,4},{7,5},{8,10},{9,11},{10,... | collective-permute-start | bytes 331784 | tf_op jit(solution)/shard_map/ppermute | solution.py:306
  15.7 2.5 %collective-permute-start.2 = (bf16[216,256]{1,0:T(8,128)(2,1)S(1)}, bf16[216,256]{1,0:T(8,128)(2,1)S(1)}, u32[]{:S(2)}, u32[]{:S(2)}) collective-permute-start(bf16[216,256]{1,0:T(8,128)(2,1)S(1)} %collective-permute-done.refs_1_), channel_id=1, source_target_pairs={{0,32},{32,0},{64,96},{96,64},{1,33},{33,1},{65,97},{97,65},{2,34}... | collective-permute-start | bytes 331784 | tf_op jit(solution)/shard_map/ppermute | solution.py:328
  18.2 0.9 %collective-permute-start.3 = (bf16[64,256]{1,0:T(8,128)(2,1)S(1)}, bf16[64,256]{1,0:T(8,128)(2,1)S(1)}, u32[]{:S(2)}, u32[]{:S(2)}) collective-permute-start(bf16[64,256]{1,0:T(8,128)(2,1)S(1)} %copy-done.4), channel_id=1, source_target_pairs={{0,1},{1,0},{2,3},{3,2},{4,5},{5,4},{6,7},{7,6},{8,9},{9,8},{10,11... | collective-permute-start | bytes 98312 | tf_op jit(solution)/shard_map/ppermute | solution.py:306
  19.1 1.2 %collective-permute-start.4 = (bf16[64,256]{1,0:T(8,128)(2,1)S(1)}, bf16[64,256]{1,0:T(8,128)(2,1)S(1)}, u32[]{:S(2)}, u32[]{:S(2)}) collective-permute-start(bf16[64,256]{1,0:T(8,128)(2,1)S(1)} %copy-done.3), channel_id=1, source_target_pairs={{0,2},{1,3},{2,0},{3,1},{4,6},{5,7},{6,4},{7,5},{8,10},{9,11},{10,... | collective-permute-start | bytes 98312 | tf_op jit(solution)/shard_map/ppermute | solution.py:306
  20.3 1.2 %collective-permute-start.5 = (bf16[64,256]{1,0:T(8,128)(2,1)S(1)}, bf16[64,256]{1,0:T(8,128)(2,1)S(1)}, u32[]{:S(2)}, u32[]{:S(2)}) collective-permute-start(bf16[64,256]{1,0:T(8,128)(2,1)S(1)} %copy-done.2), channel_id=1, source_target_pairs={{0,3},{1,2},{2,1},{3,0},{4,7},{5,6},{6,5},{7,4},{8,11},{9,10},{10,... | collective-permute-start | bytes 98312 | tf_op jit(solution)/shard_map/ppermute | solution.py:306
  21.5 6.0 %collective-permute-done.1.refs_2_ = bf16[216,256]{1,0:T(8,128)(2,1)S(1)} collective-permute-done((bf16[216,256]{1,0:T(8,128)(2,1)S(1)}, bf16[216,256]{1,0:T(8,128)(2,1)S(1)}, u32[]{:S(2)}, u32[]{:S(2)}) %collective-permute-start.1) | collective-permute-done | bytes 110624 | tf_op jit(solution)/shard_map/ppermute | solution.py:306
  28.2 1.4 %conv_forward.1 = (f32[32,1536]{1,0:T(8,128)S(1)}, f32[32,512]{1,0:T(8,128)S(1)}, f32[32,512]{1,0:T(8,128)S(1)}, bf16[32,1536]{1,0:T(8,128)(2,1)S(1)}, bf16[32,1536]{1,0:T(8,128)(2,1)S(1)}) custom-call(bf16[256,1920]{1,0:T(8,128)(2,1)S(1)} %bitcast.13, bf16[896,256]{1,0:T(8,128)(2,1)S(1)} %get-tuple-element.25.w_ref, bf16[64,256]{1,0:T(8,128)(2,1)S(1)} %copy-done.1, ...), custom_call_target="tpu_custom_call" | custom-call | flops 880803840 | bytes 983040 | tf_op jit(solution)/shard_map/conv_forward/pallas_call | solution.py:277
  29.6 8.1 %collective-permute-start.6 = (bf16[32,1536]{1,0:T(8,128)(2,1)S(1)}, bf16[32,1536]{1,0:T(8,128)(2,1)S(1)}, u32[]{:S(2)}, u32[]{:S(2)}) collective-permute-start(bf16[32,1536]{1,0:T(8,128)(2,1)S(1)} %get-tuple-element.33), channel_id=1, source_target_pairs={{32,64},{64,32},{33,65},{65,33},{34,66},{66,34},{35,67},{67,35},{3... | collective-permute-start | bytes 294920 | tf_op jit(solution)/shard_map/ppermute | solution.py:353
  37.9 2.2 %collective-permute-done.6.far_ref = bf16[32,1536]{1,0:T(8,128)(2,1)S(1)} collective-permute-done((bf16[32,1536]{1,0:T(8,128)(2,1)S(1)}, bf16[32,1536]{1,0:T(8,128)(2,1)S(1)}, u32[]{:S(2)}, u32[]{:S(2)}) %collective-permute-start.6) | collective-permute-done | bytes 98336 | tf_op jit(solution)/shard_map/ppermute | solution.py:353
  40.1 3.0 %conv_backward.1 = (bf16[256,1920]{1,0:T(8,128)(2,1)}, bf16[272,256]{1,0:T(8,128)(2,1)S(1)}, bf16[272,256]{1,0:T(8,128)(2,1)S(1)}, bf16[272,256]{1,0:T(8,128)(2,1)S(1)}, bf16[272,256]{1,0:T(8,128)(2,1)S(1)}) custom-call(bf16[256,1920]{1,0:T(8,128)(2,1)S(1)} %bitcast.14, f32[32,1536]{1,0:T(8,128)S(1)} %get-tuple-element.30.own_ref, ...), custom_call_target="tpu_custom_call" | custom-call | flops 1761607680 | bytes 1966080 | tf_op jit(solution)/shard_map/conv_backward/pallas_call | solution.py:277
  43.0 0.9 %collective-permute-start.8 = (bf16[272,256]{1,0:T(8,128)(2,1)S(1)}, bf16[272,256]{1,0:T(8,128)(2,1)S(1)}, u32[]{:S(2)}, u32[]{:S(2)}) collective-permute-start(bf16[272,256]{1,0:T(8,128)(2,1)S(1)} %get-tuple-element.37), channel_id=1, source_target_pairs={{0,1},{1,0},{2,3},{3,2},{4,5},{5,4},{6,7},{7,6},{8,9},{9,8},{10,11... | collective-permute-start | bytes 417800 | tf_op jit(solution)/shard_map/ppermute | solution.py:306
  44.0 1.3 %collective-permute-start.9 = (bf16[272,256]{1,0:T(8,128)(2,1)S(1)}, bf16[272,256]{1,0:T(8,128)(2,1)S(1)}, u32[]{:S(2)}, u32[]{:S(2)}) collective-permute-start(bf16[272,256]{1,0:T(8,128)(2,1)S(1)} %get-tuple-element.38), channel_id=1, source_target_pairs={{0,2},{1,3},{2,0},{3,1},{4,6},{5,7},{6,4},{7,5},{8,10},{9,11},{10,... | collective-permute-start | bytes 417800 | tf_op jit(solution)/shard_map/ppermute | solution.py:306
  45.2 1.1 %collective-permute-start.10 = (bf16[272,256]{1,0:T(8,128)(2,1)S(1)}, bf16[272,256]{1,0:T(8,128)(2,1)S(1)}, u32[]{:S(2)}, u32[]{:S(2)}) collective-permute-start(bf16[272,256]{1,0:T(8,128)(2,1)S(1)} %get-tuple-element.39), channel_id=1, source_target_pairs={{0,3},{1,2},{2,1},{3,0},{4,7},{5,6},{6,5},{7,4},{8,11},{9,10},{10,... | collective-permute-start | bytes 417800 | tf_op jit(solution)/shard_map/ppermute | solution.py:306
  46.4 5.1 %all-to-all-start.1 = ((bf16[32,8,1920]{2,1,0:T(8,128)(2,1)}), bf16[32,8,1920]{2,1,0:T(8,128)(2,1)S(1)}, u32[]{:S(2)}, u32[]{:S(2)}) async-start(bf16[32,8,1920]{2,1,0:T(8,128)(2,1)} %bitcast.8), calls=%async_computation.1 | async-start | bytes 1966080 | tf_op jit(solution)/shard_map/all_to_all | solution.py:372
  51.5 0.8 %collective-permute-done.8.refs_1_ = bf16[272,256]{1,0:T(8,128)(2,1)S(1)} collective-permute-done((bf16[272,256]{1,0:T(8,128)(2,1)S(1)}, bf16[272,256]{1,0:T(8,128)(2,1)S(1)}, u32[]{:S(2)}, u32[]{:S(2)}) %collective-permute-start.8) | collective-permute-done | bytes 139296 | tf_op jit(solution)/shard_map/ppermute | solution.py:306
  52.2 0.7 unpack.1
  52.9 1.2 %collective-permute-start.11 = (bf16[224,256]{1,0:T(8,128)(2,1)S(1)}, bf16[224,256]{1,0:T(8,128)(2,1)S(1)}, u32[]{:S(2)}, u32[]{:S(2)}) collective-permute-start(bf16[224,256]{1,0:T(8,128)(2,1)S(1)} %get-tuple-element.42), channel_id=1, source_target_pairs={{0,32},{32,0},{64,96},{96,64},{1,33},{33,1},{65,97},{97,65},{2,34}... | collective-permute-start | bytes 344072 | tf_op jit(solution)/shard_map/ppermute | solution.py:383
  54.1 1.0 %collective-permute-done.11 = bf16[224,256]{1,0:T(8,128)(2,1)S(1)} collective-permute-done((bf16[224,256]{1,0:T(8,128)(2,1)S(1)}, bf16[224,256]{1,0:T(8,128)(2,1)S(1)}, u32[]{:S(2)}, u32[]{:S(2)}) %collective-permute-start.11) | collective-permute-done | bytes 114720 | tf_op jit(solution)/shard_map/ppermute | solution.py:383
  55.1 4.2 %collective-permute-start.12 = (bf16[224,256]{1,0:T(8,128)(2,1)S(1)}, bf16[224,256]{1,0:T(8,128)(2,1)S(1)}, u32[]{:S(2)}, u32[]{:S(2)}) collective-permute-start(bf16[224,256]{1,0:T(8,128)(2,1)S(1)} %add_convert_fusion.filt_ref), channel_id=1, source_target_pairs={{0,64},{32,96},{64,0},{96,32},{1,65},{33,97},{65,1},{97,33},{2,66}... | collective-permute-start | bytes 344072 | tf_op jit(solution)/shard_map/ppermute | solution.py:385
  59.3 7.7 %collective-permute-done.12.other_ref = bf16[224,256]{1,0:T(8,128)(2,1)S(1)} collective-permute-done((bf16[224,256]{1,0:T(8,128)(2,1)S(1)}, bf16[224,256]{1,0:T(8,128)(2,1)S(1)}, u32[]{:S(2)}, u32[]{:S(2)}) %collective-permute-start.12) | collective-permute-done | bytes 114720 | tf_op jit(solution)/shard_map/ppermute | solution.py:385
  67.0 0.8 %collect.1 = (bf16[8,6144]{1,0:T(8,128)(2,1)}, f32[216,256]{1,0:T(8,128)}) custom-call(bf16[32,8,1920]{2,1,0:T(8,128)(2,1)S(1)} %all-to-all-done.1.got_ref, bf16[224,256]{1,0:T(8,128)(2,1)S(1)} %add_convert_fusion.filt_ref, bf16[224,256]{1,0:T(8,128)(2,1)S(1)} %collective-permute-done.12.other_ref), custom_call_target="tpu_custom_call" | custom-call | bytes 983040 | tf_op jit(solution)/shard_map/collect/pallas_call | solution.py:277
  (23 shorter events, 0.8 us)
Async XLA Ops:
  0.6 15.1 %collective-permute-start = (bf16[216,256]{1,0:T(8,128)(2,1)}, bf16[216,256]{1,0:T(8,128)(2,1)S(1)}, u32[]{:S(2)}, u32[]{:S(2)}) collective-permute-start(bf16[216,256]{1,0:T(8,128)(2,1)} %bitcast.15), channel_id=1, source_target_pairs={{0,1},{1,0},{2,3},{3,2},{4,5},{5,4},{6,7},{7,6},{8,9},{9,8},{10,11... | collective-permute-start | bytes 331784 | tf_op jit(solution)/shard_map/ppermute | solution.py:306
  6.0 6.9 %copy-start = (bf16[8,27,256]{2,0,1:T(8,128)(2,1)S(1)}, bf16[8,27,256]{2,0,1:T(8,128)(2,1)}, u32[]{:S(2)}) copy-start(bf16[8,27,256]{2,0,1:T(8,128)(2,1)} %param.5) | copy-start | bytes 331780
  6.0 12.1 %copy-start.4 = (bf16[64,256]{1,0:T(8,128)(2,1)S(1)}, bf16[64,256]{1,0:T(8,128)(2,1)}, u32[]{:S(2)}) copy-start(bf16[64,256]{1,0:T(8,128)(2,1)} %get-tuple-element.27) | copy-start | bytes 98308
  6.1 13.0 %copy-start.3 = (bf16[64,256]{1,0:T(8,128)(2,1)S(1)}, bf16[64,256]{1,0:T(8,128)(2,1)}, u32[]{:S(2)}) copy-start(bf16[64,256]{1,0:T(8,128)(2,1)} %get-tuple-element.28) | copy-start | bytes 98308
  6.1 14.2 %copy-start.2 = (bf16[64,256]{1,0:T(8,128)(2,1)S(1)}, bf16[64,256]{1,0:T(8,128)(2,1)}, u32[]{:S(2)}) copy-start(bf16[64,256]{1,0:T(8,128)(2,1)} %get-tuple-element.29) | copy-start | bytes 98308
  6.1 22.1 %all-to-all-start = ((bf16[32,8,1920]{2,1,0:T(8,128)(2,1)}), bf16[32,8,1920]{2,1,0:T(8,128)(2,1)S(1)}, u32[]{:S(2)}, u32[]{:S(2)}) async-start(bf16[32,8,1920]{2,1,0:T(8,128)(2,1)} %get-tuple-element.24), calls=%async_computation | async-start | bytes 1966080 | tf_op jit(solution)/shard_map/all_to_all | solution.py:329
  12.9 14.5 %collective-permute-start.1 = (bf16[216,256]{1,0:T(8,128)(2,1)S(1)}, bf16[216,256]{1,0:T(8,128)(2,1)S(1)}, u32[]{:S(2)}, u32[]{:S(2)}) collective-permute-start(bf16[216,256]{1,0:T(8,128)(2,1)S(1)} %bitcast.16), channel_id=1, source_target_pairs={{0,2},{1,3},{2,0},{3,1},{4,6},{5,7},{6,4},{7,5},{8,10},{9,11},{10,... | collective-permute-start | bytes 331784 | tf_op jit(solution)/shard_map/ppermute | solution.py:306
  15.7 11.7 %collective-permute-start.2 = (bf16[216,256]{1,0:T(8,128)(2,1)S(1)}, bf16[216,256]{1,0:T(8,128)(2,1)S(1)}, u32[]{:S(2)}, u32[]{:S(2)}) collective-permute-start(bf16[216,256]{1,0:T(8,128)(2,1)S(1)} %collective-permute-done.refs_1_), channel_id=1, source_target_pairs={{0,32},{32,0},{64,96},{96,64},{1,33},{33,1},{65,97},{97,65},{2,34}... | collective-permute-start | bytes 331784 | tf_op jit(solution)/shard_map/ppermute | solution.py:328
  18.2 9.5 %collective-permute-start.3 = (bf16[64,256]{1,0:T(8,128)(2,1)S(1)}, bf16[64,256]{1,0:T(8,128)(2,1)S(1)}, u32[]{:S(2)}, u32[]{:S(2)}) collective-permute-start(bf16[64,256]{1,0:T(8,128)(2,1)S(1)} %copy-done.4), channel_id=1, source_target_pairs={{0,1},{1,0},{2,3},{3,2},{4,5},{5,4},{6,7},{7,6},{8,9},{9,8},{10,11... | collective-permute-start | bytes 98312 | tf_op jit(solution)/shard_map/ppermute | solution.py:306
  19.1 9.1 %collective-permute-start.4 = (bf16[64,256]{1,0:T(8,128)(2,1)S(1)}, bf16[64,256]{1,0:T(8,128)(2,1)S(1)}, u32[]{:S(2)}, u32[]{:S(2)}) collective-permute-start(bf16[64,256]{1,0:T(8,128)(2,1)S(1)} %copy-done.3), channel_id=1, source_target_pairs={{0,2},{1,3},{2,0},{3,1},{4,6},{5,7},{6,4},{7,5},{8,10},{9,11},{10,... | collective-permute-start | bytes 98312 | tf_op jit(solution)/shard_map/ppermute | solution.py:306
  20.3 7.9 %copy-start.1 = (bf16[64,256]{1,0:T(8,128)(2,1)S(1)}, bf16[64,256]{1,0:T(8,128)(2,1)}, u32[]{:S(2)}) copy-start(bf16[64,256]{1,0:T(8,128)(2,1)} %get-tuple-element.26.refs_0_) | copy-start | bytes 98308
  20.3 7.9 %collective-permute-start.5 = (bf16[64,256]{1,0:T(8,128)(2,1)S(1)}, bf16[64,256]{1,0:T(8,128)(2,1)S(1)}, u32[]{:S(2)}, u32[]{:S(2)}) collective-permute-start(bf16[64,256]{1,0:T(8,128)(2,1)S(1)} %copy-done.2), channel_id=1, source_target_pairs={{0,3},{1,2},{2,1},{3,0},{4,7},{5,6},{6,5},{7,4},{8,11},{9,10},{10,... | collective-permute-start | bytes 98312 | tf_op jit(solution)/shard_map/ppermute | solution.py:306
  29.6 10.4 %collective-permute-start.6 = (bf16[32,1536]{1,0:T(8,128)(2,1)S(1)}, bf16[32,1536]{1,0:T(8,128)(2,1)S(1)}, u32[]{:S(2)}, u32[]{:S(2)}) collective-permute-start(bf16[32,1536]{1,0:T(8,128)(2,1)S(1)} %get-tuple-element.33), channel_id=1, source_target_pairs={{32,64},{64,32},{33,65},{65,33},{34,66},{66,34},{35,67},{67,35},{3... | collective-permute-start | bytes 294920 | tf_op jit(solution)/shard_map/ppermute | solution.py:353
  37.8 2.3 %collective-permute-start.7 = (bf16[32,1536]{1,0:T(8,128)(2,1)S(1)}, bf16[32,1536]{1,0:T(8,128)(2,1)S(1)}, u32[]{:S(2)}, u32[]{:S(2)}) collective-permute-start(bf16[32,1536]{1,0:T(8,128)(2,1)S(1)} %get-tuple-element.34), channel_id=1, source_target_pairs={{0,32},{32,0},{64,96},{96,64},{1,33},{33,1},{65,97},{97,65},{2,34}... | collective-permute-start | bytes 294920 | tf_op jit(solution)/shard_map/ppermute | solution.py:354
  43.0 9.2 %collective-permute-start.8 = (bf16[272,256]{1,0:T(8,128)(2,1)S(1)}, bf16[272,256]{1,0:T(8,128)(2,1)S(1)}, u32[]{:S(2)}, u32[]{:S(2)}) collective-permute-start(bf16[272,256]{1,0:T(8,128)(2,1)S(1)} %get-tuple-element.37), channel_id=1, source_target_pairs={{0,1},{1,0},{2,3},{3,2},{4,5},{5,4},{6,7},{7,6},{8,9},{9,8},{10,11... | collective-permute-start | bytes 417800 | tf_op jit(solution)/shard_map/ppermute | solution.py:306
  44.0 8.3 %collective-permute-start.9 = (bf16[272,256]{1,0:T(8,128)(2,1)S(1)}, bf16[272,256]{1,0:T(8,128)(2,1)S(1)}, u32[]{:S(2)}, u32[]{:S(2)}) collective-permute-start(bf16[272,256]{1,0:T(8,128)(2,1)S(1)} %get-tuple-element.38), channel_id=1, source_target_pairs={{0,2},{1,3},{2,0},{3,1},{4,6},{5,7},{6,4},{7,5},{8,10},{9,11},{10,... | collective-permute-start | bytes 417800 | tf_op jit(solution)/shard_map/ppermute | solution.py:306
  45.2 7.0 %collective-permute-start.10 = (bf16[272,256]{1,0:T(8,128)(2,1)S(1)}, bf16[272,256]{1,0:T(8,128)(2,1)S(1)}, u32[]{:S(2)}, u32[]{:S(2)}) collective-permute-start(bf16[272,256]{1,0:T(8,128)(2,1)S(1)} %get-tuple-element.39), channel_id=1, source_target_pairs={{0,3},{1,2},{2,1},{3,0},{4,7},{5,6},{6,5},{7,4},{8,11},{9,10},{10,... | collective-permute-start | bytes 417800 | tf_op jit(solution)/shard_map/ppermute | solution.py:306
  46.4 20.6 %all-to-all-start.1 = ((bf16[32,8,1920]{2,1,0:T(8,128)(2,1)}), bf16[32,8,1920]{2,1,0:T(8,128)(2,1)S(1)}, u32[]{:S(2)}, u32[]{:S(2)}) async-start(bf16[32,8,1920]{2,1,0:T(8,128)(2,1)} %bitcast.8), calls=%async_computation.1 | async-start | bytes 1966080 | tf_op jit(solution)/shard_map/all_to_all | solution.py:372
  52.9 2.1 %collective-permute-start.11 = (bf16[224,256]{1,0:T(8,128)(2,1)S(1)}, bf16[224,256]{1,0:T(8,128)(2,1)S(1)}, u32[]{:S(2)}, u32[]{:S(2)}) collective-permute-start(bf16[224,256]{1,0:T(8,128)(2,1)S(1)} %get-tuple-element.42), channel_id=1, source_target_pairs={{0,32},{32,0},{64,96},{96,64},{1,33},{33,1},{65,97},{97,65},{2,34}... | collective-permute-start | bytes 344072 | tf_op jit(solution)/shard_map/ppermute | solution.py:383
  55.1 11.9 %collective-permute-start.12 = (bf16[224,256]{1,0:T(8,128)(2,1)S(1)}, bf16[224,256]{1,0:T(8,128)(2,1)S(1)}, u32[]{:S(2)}, u32[]{:S(2)}) collective-permute-start(bf16[224,256]{1,0:T(8,128)(2,1)S(1)} %add_convert_fusion.filt_ref), channel_id=1, source_target_pairs={{0,64},{32,96},{64,0},{96,32},{1,65},{33,97},{65,1},{97,33},{2,66}... | collective-permute-start | bytes 344072 | tf_op jit(solution)/shard_map/ppermute | solution.py:385

commit v8 on v7

--- a/solution.py
+++ b/solution.py
@@ -58,8 +58,9 @@
     return jnp.concatenate([x[slot * BLOCK : (slot + 1) * BLOCK] for slot in (0, 3, 2, 1)], 0)
 
 
-def pack_kernel(planes, x_any, cot_any, bias_any, chunks, *refs):
-    packs, (x_ref, cot_ref, bias_ref, in_sems) = refs[:RING], refs[RING:]
+def pack_kernel(planes, x_any, cot_any, bias_any, chunks_any, *refs):
+    packs, (x_ref, cot_ref, bias_ref, chunks, in_sems, out_sems) = refs[:RING], refs[RING:]
+    sent = []
     copies = [
         pltpu.make_async_copy(src, dst, in_sems.at[i])
         for i, (src, dst) in enumerate(((x_any, x_ref), (cot_any, cot_ref), (bias_any, bias_ref)))
@@ -79,9 +80,11 @@
                 above = x_ref[:, base - 2 * W : base].astype(F32)
                 halo = jnp.where(lane < W, halo, above)
             own, halo = x_ref[:, base : base + INNER], halo.astype(BF16)
-            for g in range(chunks.shape[0] // RING):
-                chunks[g * RING + v, :, d * OUTER : d * OUTER + INNER] = own
-                chunks[g * RING + v, :, d * OUTER + INNER : (d + 1) * OUTER] = halo
+            for g in range(chunks.shape[1]):
+                chunks[v, g, :, d * OUTER : d * OUTER + INNER] = own
+                chunks[v, g, :, d * OUTER + INNER : (d + 1) * OUTER] = halo
+        sent.append(pltpu.make_async_copy(chunks.at[v], chunks_any.at[:, v], out_sems.at[v]))
+        sent[-1].start()
     copies[1].wait()
     copies[2].wait()
     bias = jnp.broadcast_to(bias_ref[...].astype(F32), (16, BLOCK))
@@ -92,6 +95,8 @@
             rows = cot_ref[:, pl.ds(pl.multiple_of(start, INNER), INNER)]
             pack[16 * d : 16 * d + 16, :] = fold(rows.astype(F32)).astype(BF16)
         pack[16 * planes : 16 * planes + 16, :] = bias
+    for copy in sent:
+        copy.wait()
 
 
 def odd_slab():
@@ -310,20 +315,23 @@
     chunks, *packs = call(
         functools.partial(pack_kernel, planes),
         (features.reshape(block, voxels), cotangent.reshape(block, voxels), bias_vec[None]),
-        [((parts, block, outer), BF16)] + [pack] * RING,
+        [((parts // RING, RING, block, outer), BF16)] + [pack] * RING,
         [
             pltpu.VMEM((block, voxels), BF16),
             pltpu.VMEM((block, voxels), BF16),
             pltpu.VMEM((1, block), BF16),
+            pltpu.VMEM((RING, parts // RING, block, outer), BF16),
             pltpu.SemaphoreType.DMA((3,)),
+            pltpu.SemaphoreType.DMA((RING,)),
         ],
         PACK,
         2 * parts * block * outer,
         "pack",
         (0, 1, 2),
-        (),
+        (0,),
         61,
     )
+    chunks = chunks.reshape(parts, block, outer)
     packs = [to_slot(value, slot) for slot, value in enumerate(packs)]
     third = lax.ppermute(first, "space", [(s, s ^ 1) for s in range(slabs)])
     x = lax.all_to_all(chunks, "filt", 0, 0, tiled=True).reshape(channels, outer)

time: 68.5 us -> 69.1 us (level)
  transfers between devices with their start and end apart: 15 -> 15, of which waited for: 6 -> 6; matrix products, arithmetic and copies ran while one was open for 0% -> 0% of each run, Pallas kernels for 4% -> 5%
where the time goes in v8:
time: 69.1 us; the launch traced here: 68.4 us
  starting transfers between devices  40.8 us (59%)
  waiting for transfers between devices  18.2 us (26%)
  Pallas kernels  8.66 us (13%)
  between operations  0.76 us (1%)
    ppermute x8, starting transfers between devices, to_slot(): return lax.ppermute(value, ('space', 'filt'), pairs) if slot else value  12.8 us
    pallas_call x6, Pallas kernels, call(): pl.pallas_call(kernel, out_shape=shapes, in_specs=[smem if x.dtype == jnp...  8.66 us
    ppermute x1, starting transfers between devices, per_device(): far = lax.ppermute(far, 'space', inner_slabs)  8.15 us
    ppermute x1, waiting for transfers between devices, per_device(): other = lax.ppermute(filt, 'space', by(2))  7.72 us
    ppermute x8, waiting for transfers between devices, to_slot(): return lax.ppermute(value, ('space', 'filt'), pairs) if slot else value  7.27 us
    all_to_all x1, starting transfers between devices, per_device(): lax.all_to_all(chunks, 'filt', 0, 0, tiled=True).reshape(channels, outer)  6.81 us
    all_to_all x1, starting transfers between devices, per_device(): lax.all_to_all(part.reshape(parts, block, outer), 'filt', 0, 0, tiled=True)  5.09 us
    ppermute x1, starting transfers between devices, per_device(): other = lax.ppermute(filt, 'space', by(2))  4.21 us
  transfers between devices with their start and end apart: 15, of which 6 were waited for; matrix products, arithmetic and copies ran while one was open for 0% of the time, Pallas kernels for 5%

profile of v8, /device:TPU:1, one launch (start us, length us, event | category | flops | bytes accessed | tf_op | source)
XLA Modules:
  0.0 68.4 jit_solution(11165269292149313243)
XLA Ops:
  0.6 3.4 %collective-permute-start = (bf16[216,256]{1,0:T(8,128)(2,1)}, bf16[216,256]{1,0:T(8,128)(2,1)S(1)}, u32[]{:S(2)}, u32[]{:S(2)}) collective-permute-start(bf16[216,256]{1,0:T(8,128)(2,1)} %bitcast.16), channel_id=1, source_target_pairs={{0,1},{1,0},{2,3},{3,2},{4,5},{5,4},{6,7},{7,6},{8,9},{9,8},{10,11... | collective-permute-start | bytes 331784 | tf_op jit(solution)/shard_map/ppermute | solution.py:311
  4.0 2.6 %pack.1 = (bf16[8,4,8,1920]{3,2,1,0:T(8,128)(2,1)}, bf16[64,256]{1,0:T(8,128)(2,1)}, bf16[64,256]{1,0:T(8,128)(2,1)}, bf16[64,256]{1,0:T(8,128)(2,1)}, bf16[64,256]{1,0:T(8,128)(2,1)}) custom-call(bf16[8,6144]{1,0:T(8,128)(2,1)} %bitcast.20, bf16[8,6144]{1,0:T(8,128)(2,1)} %bitcast.21, bf16[1,8]{1,0:T(2,128)(2,1)} %bitcast.22), custom_call_target="tpu_custom_call" | custom-call | bytes 983040 | tf_op jit(solution)/shard_map/pack/pallas_call | solution.py:282
  6.7 6.8 %all-to-all-start = ((bf16[32,8,1920]{2,1,0:T(8,128)(2,1)}), bf16[32,8,1920]{2,1,0:T(8,128)(2,1)S(1)}, u32[]{:S(2)}, u32[]{:S(2)}) async-start(bf16[32,8,1920]{2,1,0:T(8,128)(2,1)} %bitcast.19), calls=%async_computation | async-start | bytes 1966080 | tf_op jit(solution)/shard_map/all_to_all | solution.py:337
  13.5 2.8 %collective-permute-start.1 = (bf16[216,256]{1,0:T(8,128)(2,1)S(1)}, bf16[216,256]{1,0:T(8,128)(2,1)S(1)}, u32[]{:S(2)}, u32[]{:S(2)}) collective-permute-start(bf16[216,256]{1,0:T(8,128)(2,1)S(1)} %bitcast.17), channel_id=1, source_target_pairs={{0,2},{1,3},{2,0},{3,1},{4,6},{5,7},{6,4},{7,5},{8,10},{9,11},{10,... | collective-permute-start | bytes 331784 | tf_op jit(solution)/shard_map/ppermute | solution.py:311
  16.3 2.5 %collective-permute-start.2 = (bf16[216,256]{1,0:T(8,128)(2,1)S(1)}, bf16[216,256]{1,0:T(8,128)(2,1)S(1)}, u32[]{:S(2)}, u32[]{:S(2)}) collective-permute-start(bf16[216,256]{1,0:T(8,128)(2,1)S(1)} %collective-permute-done.refs_1_), channel_id=1, source_target_pairs={{0,32},{32,0},{64,96},{96,64},{1,33},{33,1},{65,97},{97,65},{2,34}... | collective-permute-start | bytes 331784 | tf_op jit(solution)/shard_map/ppermute | solution.py:336
  18.8 0.9 %collective-permute-start.3 = (bf16[64,256]{1,0:T(8,128)(2,1)S(1)}, bf16[64,256]{1,0:T(8,128)(2,1)S(1)}, u32[]{:S(2)}, u32[]{:S(2)}) collective-permute-start(bf16[64,256]{1,0:T(8,128)(2,1)S(1)} %copy-done.4), channel_id=1, source_target_pairs={{0,1},{1,0},{2,3},{3,2},{4,5},{5,4},{6,7},{7,6},{8,9},{9,8},{10,11... | collective-permute-start | bytes 98312 | tf_op jit(solution)/shard_map/ppermute | solution.py:311
  19.7 1.2 %collective-permute-start.4 = (bf16[64,256]{1,0:T(8,128)(2,1)S(1)}, bf16[64,256]{1,0:T(8,128)(2,1)S(1)}, u32[]{:S(2)}, u32[]{:S(2)}) collective-permute-start(bf16[64,256]{1,0:T(8,128)(2,1)S(1)} %copy-done.3), channel_id=1, source_target_pairs={{0,2},{1,3},{2,0},{3,1},{4,6},{5,7},{6,4},{7,5},{8,10},{9,11},{10,... | collective-permute-start | bytes 98312 | tf_op jit(solution)/shard_map/ppermute | solution.py:311
  20.9 1.2 %collective-permute-start.5 = (bf16[64,256]{1,0:T(8,128)(2,1)S(1)}, bf16[64,256]{1,0:T(8,128)(2,1)S(1)}, u32[]{:S(2)}, u32[]{:S(2)}) collective-permute-start(bf16[64,256]{1,0:T(8,128)(2,1)S(1)} %copy-done.2), channel_id=1, source_target_pairs={{0,3},{1,2},{2,1},{3,0},{4,7},{5,6},{6,5},{7,4},{8,11},{9,10},{10,... | collective-permute-start | bytes 98312 | tf_op jit(solution)/shard_map/ppermute | solution.py:311
  22.0 6.0 %collective-permute-done.1.refs_2_ = bf16[216,256]{1,0:T(8,128)(2,1)S(1)} collective-permute-done((bf16[216,256]{1,0:T(8,128)(2,1)S(1)}, bf16[216,256]{1,0:T(8,128)(2,1)S(1)}, u32[]{:S(2)}, u32[]{:S(2)}) %collective-permute-start.1) | collective-permute-done | bytes 110624 | tf_op jit(solution)/shard_map/ppermute | solution.py:311
  28.8 1.4 %conv_forward.1 = (f32[32,1536]{1,0:T(8,128)S(1)}, f32[32,512]{1,0:T(8,128)S(1)}, f32[32,512]{1,0:T(8,128)S(1)}, bf16[32,1536]{1,0:T(8,128)(2,1)S(1)}, bf16[32,1536]{1,0:T(8,128)(2,1)S(1)}) custom-call(bf16[256,1920]{1,0:T(8,128)(2,1)S(1)} %bitcast.14, bf16[896,256]{1,0:T(8,128)(2,1)S(1)} %get-tuple-element.25.w_ref, bf16[64,256]{1,0:T(8,128)(2,1)S(1)} %copy-done.1, ...), custom_call_target="tpu_custom_call" | custom-call | flops 880803840 | bytes 983040 | tf_op jit(solution)/shard_map/conv_forward/pallas_call | solution.py:282
  30.2 8.2 %collective-permute-start.6 = (bf16[32,1536]{1,0:T(8,128)(2,1)S(1)}, bf16[32,1536]{1,0:T(8,128)(2,1)S(1)}, u32[]{:S(2)}, u32[]{:S(2)}) collective-permute-start(bf16[32,1536]{1,0:T(8,128)(2,1)S(1)} %get-tuple-element.33), channel_id=1, source_target_pairs={{32,64},{64,32},{33,65},{65,33},{34,66},{66,34},{35,67},{67,35},{3... | collective-permute-start | bytes 294920 | tf_op jit(solution)/shard_map/ppermute | solution.py:361
  38.5 2.2 %collective-permute-done.6.far_ref = bf16[32,1536]{1,0:T(8,128)(2,1)S(1)} collective-permute-done((bf16[32,1536]{1,0:T(8,128)(2,1)S(1)}, bf16[32,1536]{1,0:T(8,128)(2,1)S(1)}, u32[]{:S(2)}, u32[]{:S(2)}) %collective-permute-start.6) | collective-permute-done | bytes 98336 | tf_op jit(solution)/shard_map/ppermute | solution.py:361
  40.7 3.0 %conv_backward.1 = (bf16[256,1920]{1,0:T(8,128)(2,1)}, bf16[272,256]{1,0:T(8,128)(2,1)S(1)}, bf16[272,256]{1,0:T(8,128)(2,1)S(1)}, bf16[272,256]{1,0:T(8,128)(2,1)S(1)}, bf16[272,256]{1,0:T(8,128)(2,1)S(1)}) custom-call(bf16[256,1920]{1,0:T(8,128)(2,1)S(1)} %bitcast.15, f32[32,1536]{1,0:T(8,128)S(1)} %get-tuple-element.30.own_ref, ...), custom_call_target="tpu_custom_call" | custom-call | flops 1761607680 | bytes 1966080 | tf_op jit(solution)/shard_map/conv_backward/pallas_call | solution.py:282
  43.6 0.9 %collective-permute-start.8 = (bf16[272,256]{1,0:T(8,128)(2,1)S(1)}, bf16[272,256]{1,0:T(8,128)(2,1)S(1)}, u32[]{:S(2)}, u32[]{:S(2)}) collective-permute-start(bf16[272,256]{1,0:T(8,128)(2,1)S(1)} %get-tuple-element.37), channel_id=1, source_target_pairs={{0,1},{1,0},{2,3},{3,2},{4,5},{5,4},{6,7},{7,6},{8,9},{9,8},{10,11... | collective-permute-start | bytes 417800 | tf_op jit(solution)/shard_map/ppermute | solution.py:311
  44.6 1.3 %collective-permute-start.9 = (bf16[272,256]{1,0:T(8,128)(2,1)S(1)}, bf16[272,256]{1,0:T(8,128)(2,1)S(1)}, u32[]{:S(2)}, u32[]{:S(2)}) collective-permute-start(bf16[272,256]{1,0:T(8,128)(2,1)S(1)} %get-tuple-element.38), channel_id=1, source_target_pairs={{0,2},{1,3},{2,0},{3,1},{4,6},{5,7},{6,4},{7,5},{8,10},{9,11},{10,... | collective-permute-start | bytes 417800 | tf_op jit(solution)/shard_map/ppermute | solution.py:311
  45.8 1.1 %collective-permute-start.10 = (bf16[272,256]{1,0:T(8,128)(2,1)S(1)}, bf16[272,256]{1,0:T(8,128)(2,1)S(1)}, u32[]{:S(2)}, u32[]{:S(2)}) collective-permute-start(bf16[272,256]{1,0:T(8,128)(2,1)S(1)} %get-tuple-element.39), channel_id=1, source_target_pairs={{0,3},{1,2},{2,1},{3,0},{4,7},{5,6},{6,5},{7,4},{8,11},{9,10},{10,... | collective-permute-start | bytes 417800 | tf_op jit(solution)/shard_map/ppermute | solution.py:311
  47.0 5.1 %all-to-all-start.1 = ((bf16[32,8,1920]{2,1,0:T(8,128)(2,1)}), bf16[32,8,1920]{2,1,0:T(8,128)(2,1)S(1)}, u32[]{:S(2)}, u32[]{:S(2)}) async-start(bf16[32,8,1920]{2,1,0:T(8,128)(2,1)} %bitcast.9), calls=%async_computation.1 | async-start | bytes 1966080 | tf_op jit(solution)/shard_map/all_to_all | solution.py:380
  52.1 0.8 %collective-permute-done.8.refs_1_ = bf16[272,256]{1,0:T(8,128)(2,1)S(1)} collective-permute-done((bf16[272,256]{1,0:T(8,128)(2,1)S(1)}, bf16[272,256]{1,0:T(8,128)(2,1)S(1)}, u32[]{:S(2)}, u32[]{:S(2)}) %collective-permute-start.8) | collective-permute-done | bytes 139296 | tf_op jit(solution)/shard_map/ppermute | solution.py:311
  52.8 0.7 unpack.1
  53.5 1.2 %collective-permute-start.11 = (bf16[224,256]{1,0:T(8,128)(2,1)S(1)}, bf16[224,256]{1,0:T(8,128)(2,1)S(1)}, u32[]{:S(2)}, u32[]{:S(2)}) collective-permute-start(bf16[224,256]{1,0:T(8,128)(2,1)S(1)} %get-tuple-element.42), channel_id=1, source_target_pairs={{0,32},{32,0},{64,96},{96,64},{1,33},{33,1},{65,97},{97,65},{2,34}... | collective-permute-start | bytes 344072 | tf_op jit(solution)/shard_map/ppermute | solution.py:391
  54.7 1.0 %collective-permute-done.11 = bf16[224,256]{1,0:T(8,128)(2,1)S(1)} collective-permute-done((bf16[224,256]{1,0:T(8,128)(2,1)S(1)}, bf16[224,256]{1,0:T(8,128)(2,1)S(1)}, u32[]{:S(2)}, u32[]{:S(2)}) %collective-permute-start.11) | collective-permute-done | bytes 114720 | tf_op jit(solution)/shard_map/ppermute | solution.py:391
  55.7 4.2 %collective-permute-start.12 = (bf16[224,256]{1,0:T(8,128)(2,1)S(1)}, bf16[224,256]{1,0:T(8,128)(2,1)S(1)}, u32[]{:S(2)}, u32[]{:S(2)}) collective-permute-start(bf16[224,256]{1,0:T(8,128)(2,1)S(1)} %add_convert_fusion.filt_ref), channel_id=1, source_target_pairs={{0,64},{32,96},{64,0},{96,32},{1,65},{33,97},{65,1},{97,33},{2,66}... | collective-permute-start | bytes 344072 | tf_op jit(solution)/shard_map/ppermute | solution.py:393
  59.9 7.7 %collective-permute-done.12.other_ref = bf16[224,256]{1,0:T(8,128)(2,1)S(1)} collective-permute-done((bf16[224,256]{1,0:T(8,128)(2,1)S(1)}, bf16[224,256]{1,0:T(8,128)(2,1)S(1)}, u32[]{:S(2)}, u32[]{:S(2)}) %collective-permute-start.12) | collective-permute-done | bytes 114720 | tf_op jit(solution)/shard_map/ppermute | solution.py:393
  67.6 0.8 %collect.1 = (bf16[8,6144]{1,0:T(8,128)(2,1)}, f32[216,256]{1,0:T(8,128)}) custom-call(bf16[32,8,1920]{2,1,0:T(8,128)(2,1)S(1)} %all-to-all-done.1.got_ref, bf16[224,256]{1,0:T(8,128)(2,1)S(1)} %add_convert_fusion.filt_ref, bf16[224,256]{1,0:T(8,128)(2,1)S(1)} %collective-permute-done.12.other_ref), custom_call_target="tpu_custom_call" | custom-call | bytes 983040 | tf_op jit(solution)/shard_map/collect/pallas_call | solution.py:282
  (23 shorter events, 0.8 us)
Async XLA Ops:
  0.6 15.7 %collective-permute-start = (bf16[216,256]{1,0:T(8,128)(2,1)}, bf16[216,256]{1,0:T(8,128)(2,1)S(1)}, u32[]{:S(2)}, u32[]{:S(2)}) collective-permute-start(bf16[216,256]{1,0:T(8,128)(2,1)} %bitcast.16), channel_id=1, source_target_pairs={{0,1},{1,0},{2,3},{3,2},{4,5},{5,4},{6,7},{7,6},{8,9},{9,8},{10,11... | collective-permute-start | bytes 331784 | tf_op jit(solution)/shard_map/ppermute | solution.py:311
  6.6 6.9 %copy-start = (bf16[8,27,256]{2,0,1:T(8,128)(2,1)S(1)}, bf16[8,27,256]{2,0,1:T(8,128)(2,1)}, u32[]{:S(2)}) copy-start(bf16[8,27,256]{2,0,1:T(8,128)(2,1)} %param.5) | copy-start | bytes 331780
  6.6 12.1 %copy-start.4 = (bf16[64,256]{1,0:T(8,128)(2,1)S(1)}, bf16[64,256]{1,0:T(8,128)(2,1)}, u32[]{:S(2)}) copy-start(bf16[64,256]{1,0:T(8,128)(2,1)} %get-tuple-element.27) | copy-start | bytes 98308
  6.6 13.0 %copy-start.3 = (bf16[64,256]{1,0:T(8,128)(2,1)S(1)}, bf16[64,256]{1,0:T(8,128)(2,1)}, u32[]{:S(2)}) copy-start(bf16[64,256]{1,0:T(8,128)(2,1)} %get-tuple-element.28) | copy-start | bytes 98308
  6.7 14.2 %copy-start.2 = (bf16[64,256]{1,0:T(8,128)(2,1)S(1)}, bf16[64,256]{1,0:T(8,128)(2,1)}, u32[]{:S(2)}) copy-start(bf16[64,256]{1,0:T(8,128)(2,1)} %get-tuple-element.29) | copy-start | bytes 98308
  6.7 22.1 %all-to-all-start = ((bf16[32,8,1920]{2,1,0:T(8,128)(2,1)}), bf16[32,8,1920]{2,1,0:T(8,128)(2,1)S(1)}, u32[]{:S(2)}, u32[]{:S(2)}) async-start(bf16[32,8,1920]{2,1,0:T(8,128)(2,1)} %bitcast.19), calls=%async_computation | async-start | bytes 1966080 | tf_op jit(solution)/shard_map/all_to_all | solution.py:337
  13.5 14.5 %collective-permute-start.1 = (bf16[216,256]{1,0:T(8,128)(2,1)S(1)}, bf16[216,256]{1,0:T(8,128)(2,1)S(1)}, u32[]{:S(2)}, u32[]{:S(2)}) collective-permute-start(bf16[216,256]{1,0:T(8,128)(2,1)S(1)} %bitcast.17), channel_id=1, source_target_pairs={{0,2},{1,3},{2,0},{3,1},{4,6},{5,7},{6,4},{7,5},{8,10},{9,11},{10,... | collective-permute-start | bytes 331784 | tf_op jit(solution)/shard_map/ppermute | solution.py:311
  16.3 11.7 %collective-permute-start.2 = (bf16[216,256]{1,0:T(8,128)(2,1)S(1)}, bf16[216,256]{1,0:T(8,128)(2,1)S(1)}, u32[]{:S(2)}, u32[]{:S(2)}) collective-permute-start(bf16[216,256]{1,0:T(8,128)(2,1)S(1)} %collective-permute-done.refs_1_), channel_id=1, source_target_pairs={{0,32},{32,0},{64,96},{96,64},{1,33},{33,1},{65,97},{97,65},{2,34}... | collective-permute-start | bytes 331784 | tf_op jit(solution)/shard_map/ppermute | solution.py:336
  18.8 9.5 %collective-permute-start.3 = (bf16[64,256]{1,0:T(8,128)(2,1)S(1)}, bf16[64,256]{1,0:T(8,128)(2,1)S(1)}, u32[]{:S(2)}, u32[]{:S(2)}) collective-permute-start(bf16[64,256]{1,0:T(8,128)(2,1)S(1)} %copy-done.4), channel_id=1, source_target_pairs={{0,1},{1,0},{2,3},{3,2},{4,5},{5,4},{6,7},{7,6},{8,9},{9,8},{10,11... | collective-permute-start | bytes 98312 | tf_op jit(solution)/shard_map/ppermute | solution.py:311
  19.7 9.1 %collective-permute-start.4 = (bf16[64,256]{1,0:T(8,128)(2,1)S(1)}, bf16[64,256]{1,0:T(8,128)(2,1)S(1)}, u32[]{:S(2)}, u32[]{:S(2)}) collective-permute-start(bf16[64,256]{1,0:T(8,128)(2,1)S(1)} %copy-done.3), channel_id=1, source_target_pairs={{0,2},{1,3},{2,0},{3,1},{4,6},{5,7},{6,4},{7,5},{8,10},{9,11},{10,... | collective-permute-start | bytes 98312 | tf_op jit(solution)/shard_map/ppermute | solution.py:311
  20.9 7.9 %copy-start.1 = (bf16[64,256]{1,0:T(8,128)(2,1)S(1)}, bf16[64,256]{1,0:T(8,128)(2,1)}, u32[]{:S(2)}) copy-start(bf16[64,256]{1,0:T(8,128)(2,1)} %get-tuple-element.26.refs_0_) | copy-start | bytes 98308
  20.9 7.9 %collective-permute-start.5 = (bf16[64,256]{1,0:T(8,128)(2,1)S(1)}, bf16[64,256]{1,0:T(8,128)(2,1)S(1)}, u32[]{:S(2)}, u32[]{:S(2)}) collective-permute-start(bf16[64,256]{1,0:T(8,128)(2,1)S(1)} %copy-done.2), channel_id=1, source_target_pairs={{0,3},{1,2},{2,1},{3,0},{4,7},{5,6},{6,5},{7,4},{8,11},{9,10},{10,... | collective-permute-start | bytes 98312 | tf_op jit(solution)/shard_map/ppermute | solution.py:311
  30.2 10.4 %collective-permute-start.6 = (bf16[32,1536]{1,0:T(8,128)(2,1)S(1)}, bf16[32,1536]{1,0:T(8,128)(2,1)S(1)}, u32[]{:S(2)}, u32[]{:S(2)}) collective-permute-start(bf16[32,1536]{1,0:T(8,128)(2,1)S(1)} %get-tuple-element.33), channel_id=1, source_target_pairs={{32,64},{64,32},{33,65},{65,33},{34,66},{66,34},{35,67},{67,35},{3... | collective-permute-start | bytes 294920 | tf_op jit(solution)/shard_map/ppermute | solution.py:361
  38.4 2.3 %collective-permute-start.7 = (bf16[32,1536]{1,0:T(8,128)(2,1)S(1)}, bf16[32,1536]{1,0:T(8,128)(2,1)S(1)}, u32[]{:S(2)}, u32[]{:S(2)}) collective-permute-start(bf16[32,1536]{1,0:T(8,128)(2,1)S(1)} %get-tuple-element.34), channel_id=1, source_target_pairs={{0,32},{32,0},{64,96},{96,64},{1,33},{33,1},{65,97},{97,65},{2,34}... | collective-permute-start | bytes 294920 | tf_op jit(solution)/shard_map/ppermute | solution.py:362
  43.6 9.2 %collective-permute-start.8 = (bf16[272,256]{1,0:T(8,128)(2,1)S(1)}, bf16[272,256]{1,0:T(8,128)(2,1)S(1)}, u32[]{:S(2)}, u32[]{:S(2)}) collective-permute-start(bf16[272,256]{1,0:T(8,128)(2,1)S(1)} %get-tuple-element.37), channel_id=1, source_target_pairs={{0,1},{1,0},{2,3},{3,2},{4,5},{5,4},{6,7},{7,6},{8,9},{9,8},{10,11... | collective-permute-start | bytes 417800 | tf_op jit(solution)/shard_map/ppermute | solution.py:311
  44.6 8.3 %collective-permute-start.9 = (bf16[272,256]{1,0:T(8,128)(2,1)S(1)}, bf16[272,256]{1,0:T(8,128)(2,1)S(1)}, u32[]{:S(2)}, u32[]{:S(2)}) collective-permute-start(bf16[272,256]{1,0:T(8,128)(2,1)S(1)} %get-tuple-element.38), channel_id=1, source_target_pairs={{0,2},{1,3},{2,0},{3,1},{4,6},{5,7},{6,4},{7,5},{8,10},{9,11},{10,... | collective-permute-start | bytes 417800 | tf_op jit(solution)/shard_map/ppermute | solution.py:311
  45.8 7.0 %collective-permute-start.10 = (bf16[272,256]{1,0:T(8,128)(2,1)S(1)}, bf16[272,256]{1,0:T(8,128)(2,1)S(1)}, u32[]{:S(2)}, u32[]{:S(2)}) collective-permute-start(bf16[272,256]{1,0:T(8,128)(2,1)S(1)} %get-tuple-element.39), channel_id=1, source_target_pairs={{0,3},{1,2},{2,1},{3,0},{4,7},{5,6},{6,5},{7,4},{8,11},{9,10},{10,... | collective-permute-start | bytes 417800 | tf_op jit(solution)/shard_map/ppermute | solution.py:311
  47.0 20.6 %all-to-all-start.1 = ((bf16[32,8,1920]{2,1,0:T(8,128)(2,1)}), bf16[32,8,1920]{2,1,0:T(8,128)(2,1)S(1)}, u32[]{:S(2)}, u32[]{:S(2)}) async-start(bf16[32,8,1920]{2,1,0:T(8,128)(2,1)} %bitcast.9), calls=%async_computation.1 | async-start | bytes 1966080 | tf_op jit(solution)/shard_map/all_to_all | solution.py:380
  53.5 2.1 %collective-permute-start.11 = (bf16[224,256]{1,0:T(8,128)(2,1)S(1)}, bf16[224,256]{1,0:T(8,128)(2,1)S(1)}, u32[]{:S(2)}, u32[]{:S(2)}) collective-permute-start(bf16[224,256]{1,0:T(8,128)(2,1)S(1)} %get-tuple-element.42), channel_id=1, source_target_pairs={{0,32},{32,0},{64,96},{96,64},{1,33},{33,1},{65,97},{97,65},{2,34}... | collective-permute-start | bytes 344072 | tf_op jit(solution)/shard_map/ppermute | solution.py:391
  55.7 11.9 %collective-permute-start.12 = (bf16[224,256]{1,0:T(8,128)(2,1)S(1)}, bf16[224,256]{1,0:T(8,128)(2,1)S(1)}, u32[]{:S(2)}, u32[]{:S(2)}) collective-permute-start(bf16[224,256]{1,0:T(8,128)(2,1)S(1)} %add_convert_fusion.filt_ref), channel_id=1, source_target_pairs={{0,64},{32,96},{64,0},{96,32},{1,65},{33,97},{65,1},{97,33},{2,66}... | collective-permute-start | bytes 344072 | tf_op jit(solution)/shard_map/ppermute | solution.py:393
